TPU v7x, 256 devices: a whole 4x4x8 slice. The times are simulated.
256 devices in a mesh: tm: 8 (over y, core), lon: 16 (over x_hi, z), head: 2 (over x_lo).
Axes of the slice: x: 4 (x_hi: 2, x_lo: 2; x = x_hi * 2 + x_lo), y: 4, z: 8, core: 2. Of those that a mesh axis runs over, the one named last changes fastest.
Arguments:
- query_field: bfloat16 [96, 8, 128, 1536], P('tm', None, 'lon', 'head'), may hold values from -8 to 8
- key_field: bfloat16 [96, 8, 128, 1536], P('tm', None, 'lon', 'head'), may hold values from -8 to 8
- value_field: bfloat16 [96, 8, 128, 1536], P('tm', None, 'lon', 'head'), may hold values from -6 to 6
- tile_offsets: int32 [16, 16], P('tm', 'lon'), may hold values from -1 to 1
- timesteps: int32 [16], P('tm'), may hold values from 0 to 999
- gate_weight: float32 [256, 1536], P(None, 'head'), may hold values from -0.375 to 0.375
Outputs:
- gated_field: bfloat16 [96, 8, 128, 1536], P('tm', None, 'lon', 'head')
Inputs may be any that keep to these rules, and one draw needn't show every extreme that they name: `tile_offsets`: the query tile (t, L) with shift s attends longitude tiles L + s - 1 to L + s + 1 around the loop.
All inputs are finite; a program needn't handle non-finite values.
Results may differ from a plain program's by a relative error of at most 0.0037.
Values may be sent and summed in bfloat16 or wider, within the bound.
No kernel may reach another device: no remote copies, remote signals or barrier semaphores. Data moves between devices by JAX's collectives and lax.ppermute only.
A program may use at most 128 MiB of HBM per device.

v0:
```python
import math

import jax
import jax.numpy as jnp
from jax import lax
from jax.sharding import PartitionSpec as P

HD = 128
FREQ = 256
TILE_T = 6
TILE_H = 8
TILE_W = 8


def from_behind(block, axis, distance):
    devices = range(lax.axis_size(axis))
    route = [((i - distance) % len(devices), i) for i in devices]
    return lax.ppermute(block, axis, route)


def extended_2(x, sides, width):
    for axis, dim in sides:
        size, length = (lax.axis_size(axis), x.shape[dim])
        up = [(i, (i + 1) % size) for i in range(size - 1)]
        down = [(j, i) for i, j in up]
        last = lax.slice_in_dim(x, length - width, length, axis=dim)
        leading = lax.slice_in_dim(x, 0, width, axis=dim)
        before = lax.ppermute(last, axis, up)
        after = lax.ppermute(leading, axis, down)
        x = jnp.concatenate([before, x, after], axis=dim)
    return x


def start_at(*entries):
    return tuple((jnp.asarray(entry).astype(jnp.int32) for entry in entries))


def lon_extend(column_block):
    pieces = {}
    for shift_by in (2, 1, -1, -2):
        pieces[shift_by] = from_behind(column_block, "lon", shift_by)
    return jnp.concatenate([pieces[2], pieces[1], column_block, pieces[-1], pieces[-2]], axis=4)


def local(query_field, key_field, value_field, tile_offsets, timesteps, gate_weight):
    tiles_here = query_field.shape[0] // TILE_T
    features = query_field.shape[3]
    heads_here = features // HD
    tile_size = TILE_T * TILE_H * TILE_W
    tile_first = lax.axis_index("tm") * tiles_here
    time_count = tiles_here * lax.axis_size("tm")
    tiled_shape = (tiles_here, TILE_T, TILE_H, TILE_W, features)
    stacked = jnp.stack([key_field.reshape(tiled_shape), value_field.reshape(tiled_shape)], axis=1)
    rimmed = extended_2(stacked, (("tm", 0),), 1)
    extended = lon_extend(rimmed)
    half_freq = FREQ // 2
    frequencies = jnp.exp(-math.log(10000.0) * jnp.arange(half_freq, dtype=jnp.float32) / half_freq)
    angles = timesteps.astype(jnp.float32)[:, None] * frequencies[None, :]
    embedding = jnp.concatenate([jnp.cos(angles), jnp.sin(angles)], axis=1)
    gate_rows = jnp.dot(
        embedding, gate_weight, precision=lax.Precision.HIGHEST, preferred_element_type=jnp.float32
    )
    query_tiles = query_field.reshape(tiled_shape)
    inv_root = 1.0 / math.sqrt(HD)
    window_rows = 3 * TILE_T * TILE_H * 3 * TILE_W

    def one_pair(pair_index):
        tile_index = pair_index // heads_here
        head_index = pair_index % heads_here
        lon_shift = tile_offsets[tile_index, 0]
        window = lax.dynamic_slice(
            extended,
            start_at(tile_index, 0, 0, 0, (lon_shift + 1) * TILE_W, head_index * HD),
            (3, 2, TILE_T, TILE_H, 3 * TILE_W, HD),
        )
        key_rows = window[:, 0].reshape(window_rows, HD)
        value_rows = window[:, 1].reshape(window_rows, HD)
        query_rows = lax.dynamic_slice(
            query_tiles,
            start_at(tile_index, 0, 0, 0, head_index * HD),
            (1, TILE_T, TILE_H, TILE_W, HD),
        ).reshape(tile_size, HD)
        scores = (
            lax.dot_general(
                query_rows, key_rows, (((1,), (1,)), ((), ())), preferred_element_type=jnp.float32
            )
            * inv_root
        )
        window_times = tile_first + tile_index - 1 + jnp.arange(3, dtype=jnp.int32)
        usable = (window_times >= 0) & (window_times < time_count)
        scores = jnp.where(
            usable[None, :, None], scores.reshape(tile_size, 3, window_rows // 3), -1e30
        )
        scores = scores.reshape(tile_size, window_rows)
        row_max = jnp.max(scores, axis=1, keepdims=True)
        raised = jnp.exp(scores - row_max)
        totals = jnp.sum(raised, axis=1, keepdims=True)
        weights = raised.astype(jnp.bfloat16)
        weighted = jnp.dot(weights, value_rows, preferred_element_type=jnp.float32)
        gate_part = lax.dynamic_slice(gate_rows, start_at(tile_index, head_index * HD), (1, HD))
        return (weighted / totals * gate_part).astype(jnp.bfloat16)

    results = lax.map(one_pair, jnp.arange(tiles_here * heads_here, dtype=jnp.int32))
    results = results.reshape(tiles_here, heads_here, TILE_T, TILE_H, TILE_W, HD)
    results = jnp.transpose(results, (0, 2, 3, 4, 1, 5))
    return results.reshape(tiles_here * TILE_T, TILE_H, TILE_W, features)


def solution(mesh):
    return jax.shard_map(
        local,
        mesh=mesh,
        in_specs=(
            P("tm", None, "lon", "head"),
            P("tm", None, "lon", "head"),
            P("tm", None, "lon", "head"),
            P("tm", "lon"),
            P("tm"),
            P(None, "head"),
        ),
        out_specs=P("tm", None, "lon", "head"),
        check_vma=False,
    )
```

profile of v0, /device:TPU:17, one launch (start us, length us, event | category | flops | bytes accessed | tf_op | source)
XLA Modules:
  0.0 480.2 jit_solution(11797386088702306986)
XLA Ops:
  0.0 2.0 fusion.22
  2.0 3.5 collective-permute-start
  5.5 1.9 collective-permute-start.1
  7.4 11.2 %collective-permute-done = bf16[1,2,6,8,8,768]{5,4,3,2,1,0:T(8,128)(2,1)S(1)} collective-permute-done((bf16[1,2,6,8,8,768]{5,4,3,2,1,0:T(8,128)(2,1)S(1)}, bf16[1,2,6,8,8,768]{5,4,3,2,1,0:T(8,128)(2,1)S(1)}, u32[]{:S(2)}, u32[]{:S(2)}) %collective-permute-start) | collective-permute-done | bytes 1179680 | tf_op jit(solution)/shard_map/ppermute | solution.py:28
  18.6 4.4 collective-permute-done.1
  23.0 2.6 pad_maximum_fusion.1
  25.6 3.0 collective-permute-start.2
  28.6 1.6 collective-permute-start.3
  30.2 3.5 collective-permute-start.4
  33.7 2.3 collective-permute-start.5
  36.8 141.4 %collective-permute-done.2 = bf16[4,2,6,8,8,768]{5,4,3,2,1,0:T(8,128)(2,1)} collective-permute-done((bf16[4,2,6,8,8,768]{5,4,3,2,1,0:T(8,128)(2,1)}, bf16[4,2,6,8,8,768]{5,4,3,2,1,0:T(8,128)(2,1)}, u32[]{:S(2)}, u32[]{:S(2)}) %collective-permute-start.2) | collective-permute-done | bytes 4718624 | tf_op jit(solution)/shard_map/ppermute | solution.py:18
  178.2 2.6 constant_dynamic-update-slice_fusion.3
  180.9 156.5 %collective-permute-done.3 = bf16[4,2,6,8,8,768]{5,4,3,2,1,0:T(8,128)(2,1)} collective-permute-done((bf16[4,2,6,8,8,768]{5,4,3,2,1,0:T(8,128)(2,1)}, bf16[4,2,6,8,8,768]{5,4,3,2,1,0:T(8,128)(2,1)}, u32[]{:S(2)}, u32[]{:S(2)}) %collective-permute-start.3) | collective-permute-done | bytes 4718624 | tf_op jit(solution)/shard_map/ppermute | solution.py:18
  337.4 2.9 constant_dynamic-update-slice_fusion.2
  340.3 1.9 fusion.21
  342.2 2.7 constant_dynamic-update-slice_fusion.1
  344.9 2.9 constant_dynamic-update-slice_fusion
  347.8 7.8 %copy-done.4 = bf16[4,2,6,8,40,768]{5,4,3,2,1,0:T(8,128)(2,1)} copy-done((bf16[4,2,6,8,40,768]{5,4,3,2,1,0:T(8,128)(2,1)}, bf16[4,2,6,8,40,768]{5,4,3,2,1,0:T(8,128)(2,1)S(1)}, u32[]{:S(2)}) %copy-start.4) | copy-done | bytes 23592984
  355.6 122.0 %while.13 = (s32[]{:T(128)}, bf16[12,384,128]{2,1,0:T(8,128)(2,1)}, s32[12]{0:T(128)S(1)}, s32[]{:T(128)}, bf16[2,6,8,8,768]{4,3,2,1,0:T(8,128)(2,1)}, /*index=5...) while((s32[]{:T(128)}, bf16[12,384,128]{2,1,0:T(8,128)(2,1)}, ...), condition=%wide.region_3.4_spmd, body=%wide.region_0.3_spmd.sunk | while | flops 688913664 | bytes 21650988 | solution.py:103
  359.5 1.8 constant_dynamic-slice_fusion.6
  369.6 1.8 constant_dynamic-slice_fusion.6
  379.8 1.8 constant_dynamic-slice_fusion.6
  389.9 1.8 constant_dynamic-slice_fusion.6
  400.1 1.8 constant_dynamic-slice_fusion.6
  410.3 1.8 constant_dynamic-slice_fusion.6
  420.4 1.8 constant_dynamic-slice_fusion.6
  430.6 1.8 constant_dynamic-slice_fusion.6
  440.8 1.8 constant_dynamic-slice_fusion.6
  450.9 1.8 constant_dynamic-slice_fusion.6
  461.1 1.8 constant_dynamic-slice_fusion.6
  471.3 1.8 constant_dynamic-slice_fusion.6
  477.6 2.6 copy.7
  (148 shorter events, 69.2 us)
Async XLA Ops:
  0.0 36.4 %copy-start = (f32[256,768]{1,0:T(8,128)S(1)}, f32[256,768]{1,0:T(8,128)}, u32[]{:S(2)}) copy-start(f32[256,768]{1,0:T(8,128)} %param.13) | copy-start | bytes 2359300
  0.0 23.0 %copy-start.2 = (bf16[12,8,8,768]{3,2,1,0:T(8,128)(2,1)S(1)}, bf16[12,8,8,768]{3,2,1,0:T(8,128)(2,1)}, u32[]{:S(2)}) copy-start(bf16[12,8,8,768]{3,2,1,0:T(8,128)(2,1)} %param.9) | copy-start | bytes 3538948
  0.0 23.0 %copy-start.3 = (bf16[12,8,8,768]{3,2,1,0:T(8,128)(2,1)S(1)}, bf16[12,8,8,768]{3,2,1,0:T(8,128)(2,1)}, u32[]{:S(2)}) copy-start(bf16[12,8,8,768]{3,2,1,0:T(8,128)(2,1)} %param.10) | copy-start | bytes 3538948
  2.0 16.6 %collective-permute-start = (bf16[1,2,6,8,8,768]{5,4,3,2,1,0:T(8,128)(2,1)S(1)}, bf16[1,2,6,8,8,768]{5,4,3,2,1,0:T(8,128)(2,1)S(1)}, u32[]{:S(2)}, u32[]{:S(2)}) collective-permute-start(bf16[1,2,6,8,8,768]{5,4,3,2,1,0:T(8,128)(2,1)S(1)} %get-tuple-element.158), channel_id=1, source_target_pairs={{0,32},{32,64},{64,96},{96,128},{128,160},{160,192},{192,224},{1,3... | collective-permute-start | bytes 3538952 | tf_op jit(solution)/shard_map/ppermute | solution.py:28
  5.4 30.6 %copy-start.8 = (s32[2]{0:T(128)S(1)}, s32[2]{0:T(128)}, u32[]{:S(2)}) copy-start(s32[2]{0:T(128)} %param.12) | copy-start | bytes 28
  5.5 17.5 %collective-permute-start.1 = (bf16[1,2,6,8,8,768]{5,4,3,2,1,0:T(8,128)(2,1)S(1)}, bf16[1,2,6,8,8,768]{5,4,3,2,1,0:T(8,128)(2,1)S(1)}, u32[]{:S(2)}, u32[]{:S(2)}) collective-permute-start(bf16[1,2,6,8,8,768]{5,4,3,2,1,0:T(8,128)(2,1)S(1)} %get-tuple-element.159), channel_id=1, source_target_pairs={{32,0},{64,32},{96,64},{128,96},{160,128},{192,160},{224,192},{33,... | collective-permute-start | bytes 3538952 | tf_op jit(solution)/shard_map/ppermute | solution.py:29
  18.6 4.4 copy-start.5
  23.0 2.6 copy-start.7
  25.6 152.6 %collective-permute-start.2 = (bf16[4,2,6,8,8,768]{5,4,3,2,1,0:T(8,128)(2,1)}, bf16[4,2,6,8,8,768]{5,4,3,2,1,0:T(8,128)(2,1)}, u32[]{:S(2)}, u32[]{:S(2)}) collective-permute-start(bf16[4,2,6,8,8,768]{5,4,3,2,1,0:T(8,128)(2,1)} %pad_maximum_fusion.1), channel_id=1, source_target_pairs={{28,0},{30,2},{0,4},{2,6},{4,8},{6,10},{8,12},{10,14},{12,16},{14,... | collective-permute-start | bytes 14155784 | tf_op jit(solution)/shard_map/ppermute | solution.py:18
  28.6 308.8 %collective-permute-start.3 = (bf16[4,2,6,8,8,768]{5,4,3,2,1,0:T(8,128)(2,1)}, bf16[4,2,6,8,8,768]{5,4,3,2,1,0:T(8,128)(2,1)}, u32[]{:S(2)}, u32[]{:S(2)}) collective-permute-start(bf16[4,2,6,8,8,768]{5,4,3,2,1,0:T(8,128)(2,1)} %pad_maximum_fusion.1), channel_id=1, source_target_pairs={{30,0},{0,2},{2,4},{4,6},{6,8},{8,10},{10,12},{12,14},{14,16},{16,... | collective-permute-start | bytes 14155784 | tf_op jit(solution)/shard_map/ppermute | solution.py:18
  30.2 312.0 %collective-permute-start.4 = (bf16[4,2,6,8,8,768]{5,4,3,2,1,0:T(8,128)(2,1)}, bf16[4,2,6,8,8,768]{5,4,3,2,1,0:T(8,128)(2,1)}, u32[]{:S(2)}, u32[]{:S(2)}) collective-permute-start(bf16[4,2,6,8,8,768]{5,4,3,2,1,0:T(8,128)(2,1)} %pad_maximum_fusion.1), channel_id=1, source_target_pairs={{2,0},{4,2},{6,4},{8,6},{10,8},{12,10},{14,12},{16,14},{18,16},{20... | collective-permute-start | bytes 14155784 | tf_op jit(solution)/shard_map/ppermute | solution.py:18
  33.7 311.2 %collective-permute-start.5 = (bf16[4,2,6,8,8,768]{5,4,3,2,1,0:T(8,128)(2,1)}, bf16[4,2,6,8,8,768]{5,4,3,2,1,0:T(8,128)(2,1)}, u32[]{:S(2)}, u32[]{:S(2)}) collective-permute-start(bf16[4,2,6,8,8,768]{5,4,3,2,1,0:T(8,128)(2,1)} %pad_maximum_fusion.1), channel_id=1, source_target_pairs={{4,0},{6,2},{8,4},{10,6},{12,8},{14,10},{16,12},{18,14},{20,16},{2... | collective-permute-start | bytes 14155784 | tf_op jit(solution)/shard_map/ppermute | solution.py:18
  180.8 159.4 %copy-start.6 = (bf16[1,2,6,8,8,768]{5,4,3,2,1,0:T(8,128)(2,1)S(1)}, bf16[1,2,6,8,8,768]{5,4,3,2,1,0:T(8,128)(2,1)}, u32[]{:S(2)}) copy-start(bf16[1,2,6,8,8,768]{5,4,3,2,1,0:T(8,128)(2,1)} %copy-done.5) | copy-start | bytes 3538948
  344.9 10.7 %copy-start.9 = (s32[2,1]{0,1:T(1,128)S(1)}, s32[2,1]{0,1:T(1,128)}, u32[]{:S(2)}) copy-start(s32[2,1]{0,1:T(1,128)} %param.11) | copy-start | bytes 28
  347.8 7.8 %copy-start.4 = (bf16[4,2,6,8,40,768]{5,4,3,2,1,0:T(8,128)(2,1)}, bf16[4,2,6,8,40,768]{5,4,3,2,1,0:T(8,128)(2,1)S(1)}, u32[]{:S(2)}) copy-start(bf16[4,2,6,8,40,768]{5,4,3,2,1,0:T(8,128)(2,1)S(1)} %constant_dynamic-update-slice_fusion) | copy-start | bytes 70778880
  477.6 2.6 copy-start.1
where the time goes:
time: 482 us; the launch traced here: 480 us
  waiting for transfers between devices  313 us (65%)
  local copies, waits for them, and re-layouts  63.2 us (13%)
  loops' own time  31.9 us (7%)
  matrix products  31.4 us (7%)
  other arithmetic  24.2 us (5%)
  starting transfers between devices  15.8 us (3%)
    ppermute x4, waiting for transfers between devices, from_behind(): return lax.ppermute(block, axis, route)  298 us
    another operation x1, loops' own time, local(): lax.map(one_pair, jnp.arange(tiles_here * heads_here, dtype=jnp.int32))  31.9 us
    slice x12, local copies, waits for them, and re-layouts, one_pair(): key_rows = window[:, 0].reshape(window_rows, HD)  21.7 us
    dot_general x12, matrix products, one_pair(): weighted = jnp.dot(weights, value_rows, preferred_element_type=jnp.float32)  18.5 us
    unnamed x23, local copies, waits for them, and re-layouts  16 us
    dot_general x12, matrix products, one_pair(): lax.dot_general(query_rows, key_rows, (((1,), (1,)), ((), ())), preferred...  12.4 us
    ppermute x1, waiting for transfers between devices, extended_2(): before = lax.ppermute(last, axis, up)  11.2 us
    dynamic_slice x12, local copies, waits for them, and re-layouts, one_pair(): lax.dynamic_slice(query_tiles, start_at(tile_index, 0, 0, 0, head_index *...  10.9 us
  transfers between devices with their start and end apart: 6, of which 4 were waited for; matrix products, arithmetic and copies ran while one was open for 2% of the time, Pallas kernels for 0%

commit v1 on v0

v1 whole, which is shorter than its diff:
```python
import functools
import itertools
import math

import jax
import jax.numpy as jnp
from jax import lax
from jax.experimental import pallas as pl
from jax.experimental.pallas import tpu as pltpu
from jax.sharding import PartitionSpec as P

HD = 128
FREQ = 256
ROWS = 384
TT = 6
SCALE = math.log2(math.e) / math.sqrt(HD)
GROUPS = ((0, 3), (3, 2), (5, 1))
ANY = pl.BlockSpec(memory_space=pltpu.HBM)
SMALL = pl.CostEstimate(flops=0, bytes_accessed=1024, transcendentals=0)
VMEM = pl.BlockSpec(memory_space=pltpu.VMEM)
SMEM = pl.BlockSpec(memory_space=pltpu.SMEM)


def run_copies(copies):
    for copy in copies:
        copy.start()
    for copy in copies:
        copy.wait()


def split_kernel(groups, k_ref, v_ref, *refs):
    outs, sem = refs[:-1], refs[-1]
    copies = []
    for out, (first, count) in zip(outs, groups):
        for t in range(2):
            for i in range(count):
                for which, ref in enumerate((k_ref, v_ref)):
                    lanes = pl.ds((first + i) * HD, HD)
                    copies.append(pltpu.make_async_copy(ref.at[pl.ds(t * TT, TT), :, :, lanes], out.at[i, t, which], sem.at[len(copies)]))
    run_copies(copies)


def split(k, v, groups):
    outs = pl.pallas_call(
        functools.partial(split_kernel, groups),
        out_shape=[jax.ShapeDtypeStruct((n, 2, 2, TT, 8, 8, HD), k.dtype) for _, n in groups],
        in_specs=[ANY, ANY],
        out_specs=[VMEM] * len(groups),
        scratch_shapes=[pltpu.SemaphoreType.DMA((4 * sum(n for _, n in groups),))],
        cost_estimate=SMALL,
        compiler_params=pltpu.CompilerParams(vmem_limit_bytes=60 * 2**20),
        name=f"split_{groups[0][0]}",
    )(k, v)
    return [x.reshape(x.shape[:3] + (ROWS, HD)) for x in outs]


def pack_kernel(rows, place_ref, *refs):
    ins, (off, on, sem) = refs[:-3], refs[-3:]
    core = place_ref[0]
    copies = []
    for ref, (row, start, count) in zip(ins, rows):
        for out, tile in ((off, core), (on, 1 - core)):
            copies.append(pltpu.make_async_copy(ref.at[:, tile], out.at[row, pl.ds(start, count)], sem.at[len(copies)]))
    run_copies(copies)


def pack(name, place, *sides):
    rows = []
    for row, xs in enumerate(sides):
        start = 0
        for x in xs:
            rows.append((row, start, x.shape[0]))
            start += x.shape[0]
    shape = jax.ShapeDtypeStruct((len(sides), start) + xs[0].shape[2:], xs[0].dtype)
    return pl.pallas_call(
        functools.partial(pack_kernel, rows),
        out_shape=[shape, shape],
        in_specs=[SMEM] + [ANY] * len(rows),
        out_specs=[VMEM, VMEM],
        scratch_shapes=[pltpu.SemaphoreType.DMA((2 * len(rows),))],
        cost_estimate=SMALL,
        compiler_params=pltpu.CompilerParams(vmem_limit_bytes=60 * 2**20),
        name=name,
    )(place, *[x for xs in sides for x in xs])


def attn_kernel(plan, first, count, s_ref, place_ref, q_ref, *refs):
    names, starts, finishes, sides, pick = plan
    ops = dict(zip(names, refs))
    out_ref, kv, qv, sc0, sc1, top0, top1, si, so, ov, ksem, qsem, isem, osem = refs[len(refs) - 14:]
    core, cut = place_ref[0], place_ref[1]

    def fill(i, slot):
        h = first + i
        for t in range(2):
            side = pick(s_ref[t, 0])
            for c, (segments, far, near) in enumerate(sides):
                for name, low, high in segments:
                    inside = (side == c) & (h >= low) & (h < high)

                    @pl.when(inside)
                    def _():
                        own = ops[name].at[h - low]
                        halo = kv.at[slot, t, 2 * t]
                        pltpu.make_async_copy(own, kv.at[slot, t, pl.ds(1 - t, 2)], ksem.at[slot, t]).start()
                        far_name, far_lead, far_low = far
                        near_name, near_lead, near_low = near
                        far_at = place_ref[2] if far_lead is None else far_lead

                        @pl.when((core == t) & (cut == 0))
                        def _():
                            pltpu.make_async_copy(ops[far_name].at[far_at, h - far_low], halo, ksem.at[slot, t]).start()

                        @pl.when((core == t) & (cut != 0))
                        def _():
                            pltpu.make_async_copy(own.at[t], halo, ksem.at[slot, t]).start()

                        @pl.when(core != t)
                        def _():
                            pltpu.make_async_copy(ops[near_name].at[near_lead, h - near_low], halo, ksem.at[slot, t]).start()
        q_copy(i, slot).start()
        if not starts:
            state_in(i, slot).start()

    def filled(i, slot):
        for t in range(2):
            pltpu.make_async_copy(kv.at[slot, t], kv.at[slot, t], ksem.at[slot, t]).wait()
        q_copy(i, slot).wait()
        if not starts:
            state_in(i, slot).wait()

    def lanes(i):
        return pl.ds(pl.multiple_of((first + i) * HD, HD), HD)

    def q_copy(i, slot):
        return pltpu.make_async_copy(q_ref.at[:, :, :, lanes(i)], qv.at[slot], qsem.at[slot])

    def state_in(i, slot):
        return pltpu.make_async_copy(ops["state"].at[first + i], si.at[slot], isem.at[slot])

    def result(i):
        slot = lax.rem(i, 2)
        if finishes:
            return pltpu.make_async_copy(ov.at[slot], out_ref.at[:, :, :, lanes(i)], osem.at[slot])
        return pltpu.make_async_copy(so.at[slot], out_ref.at[first + i], osem.at[slot])

    def scores(slot, t, sc, top):
        q = qv[slot, pl.ds(t * TT, TT)].reshape(ROWS, HD)
        m = None
        for j in range(3):
            s = lax.dot_general(q, kv[slot, t, j, 0], (((1,), (1,)), ((), ())), preferred_element_type=jnp.float32)
            sc[j] = s
            mj = jnp.maximum(jnp.maximum(s[:, :128], s[:, 128:256]), s[:, 256:])
            m = mj if m is None else jnp.maximum(m, mj)
            yield
        m = jnp.broadcast_to(jnp.max(m, axis=1, keepdims=True), (ROWS, HD))
        if not starts:
            m = jnp.maximum(m, si[slot, t, :, 2 * HD:])
        top[...] = m
        yield

    def weigh(i, slot, t, sc, top):
        to = lax.rem(i, 2)
        m1 = top[...]
        m = jnp.concatenate([m1] * 3, axis=1)
        acc = None
        if not starts:
            fade = jnp.exp2((si[slot, t, :, 2 * HD:] - m1) * SCALE)
            acc = si[slot, t, :, :2 * HD] * jnp.concatenate([fade, fade], axis=1)
        for j in range(3):
            p = jnp.exp2((sc[j] - m) * SCALE).astype(jnp.bfloat16)
            v2 = jnp.concatenate([kv[slot, t, j, 1], jnp.ones((ROWS, HD), jnp.bfloat16)], axis=1)
            if j == 2 * t:
                v2 = jnp.where((cut != 0) & (core == t), jnp.zeros_like(v2), v2)
            part = jnp.dot(p, v2, preferred_element_type=jnp.float32)
            acc = part if acc is None else acc + part
            yield
        if finishes:
            o = acc[:, :HD] / acc[:, HD:] * ops["gate"][t, first + i]
            ov[to, pl.ds(t * TT, TT)] = o.astype(jnp.bfloat16).reshape(TT, 8, 8, HD)
        else:
            so[to, t, :, :2 * HD] = acc
            so[to, t, :, 2 * HD:] = m1
        yield

    def both(*steps):
        for _ in itertools.zip_longest(*steps):
            pass

    def head(i, last):
        slot, ahead = lax.rem(i, 3), lax.rem(i + 1, 3)
        if not last:
            @pl.when(i + 2 < count)
            def _():
                fill(i + 2, lax.rem(i + 2, 3))

        @pl.when(i >= 2)
        def _():
            result(i - 2).wait()
        both(weigh(i, slot, 0, sc0, top0), scores(slot, 1, sc1, top1))
        if last:
            both(weigh(i, slot, 1, sc1, top1))
        else:
            filled(i + 1, ahead)
            both(weigh(i, slot, 1, sc1, top1), scores(ahead, 0, sc0, top0))
        result(i).start()

    fill(0, 0)
    if count > 1:
        fill(1, 1)
    filled(0, 0)
    both(scores(0, 0, sc0, top0))

    def step(i, _):
        head(i, False)
        return 0
    lax.fori_loop(0, count - 1, step, 0)
    head(jnp.int32(count - 1), True)
    for i in range(max(0, count - 2), count):
        result(i).wait()


PICKS = (lambda s: 0 * s, lambda s: jnp.where(s > 0, 1, 0), lambda s: jnp.where(s == 0, 2, jnp.where(s > 0, 1, 0)))


def attend(name, phase, first, count, *, s, place, q, arrays, sides, state=None, gate=None, prev=None):
    arrays = dict(arrays)
    if state is not None:
        arrays["state"] = state
    if gate is not None:
        arrays["gate"] = gate
    if prev is not None:
        arrays["prev"] = prev
    names = tuple(arrays)
    heads = q.shape[3] // HD
    plan = (names, phase == 0, phase == 2, sides, PICKS[phase])
    final = phase == 2
    shape = jax.ShapeDtypeStruct(q.shape, q.dtype) if final else jax.ShapeDtypeStruct((heads, 2, ROWS, 3 * HD), jnp.float32)
    aliases = {3 + names.index("prev"): 0} if prev is not None else {}
    return pl.pallas_call(
        functools.partial(attn_kernel, plan, first, count),
        out_shape=shape,
        in_specs=[SMEM, SMEM, ANY] + [VMEM if n == "gate" else ANY for n in names],
        out_specs=ANY,
        input_output_aliases=aliases,
        scratch_shapes=[
            pltpu.VMEM((3, 2, 3, 2, ROWS, HD), jnp.bfloat16),
            pltpu.VMEM((3, 12, 8, 8, HD), jnp.bfloat16),
            pltpu.VMEM((3, ROWS, ROWS), jnp.float32), pltpu.VMEM((3, ROWS, ROWS), jnp.float32),
            pltpu.VMEM((ROWS, HD), jnp.float32), pltpu.VMEM((ROWS, HD), jnp.float32),
            pltpu.VMEM((3, 2, ROWS, 3 * HD), jnp.float32),
            pltpu.VMEM((2, 2, ROWS, 3 * HD), jnp.float32),
            pltpu.VMEM((2, 12, 8, 8, HD), jnp.bfloat16),
            pltpu.SemaphoreType.DMA((3, 2)), pltpu.SemaphoreType.DMA((3,)),
            pltpu.SemaphoreType.DMA((3,)), pltpu.SemaphoreType.DMA((2,))],
        compiler_params=pltpu.CompilerParams(vmem_limit_bytes=60 * 2**20),
        cost_estimate=SMALL,
        name=name,
    )(s, place, q, *arrays.values())


def from_behind(block, distance):
    size = lax.axis_size("lon")
    return lax.ppermute(block, "lon", [((i - distance) % size, i) for i in range(size)])


def after(x, *others):
    return lax.optimization_barrier((x, *others))[0]


def pairs(off):
    size = lax.axis_size("tm")
    return [[i + off, (i + off + 1) % size] for i in range(0, size, 2)]


def far_gather(x):
    return lax.all_gather(x, "tm", axis_index_groups=pairs(1))


def far_swap(x):
    route = [r for a, b in pairs(1)[:-1] for r in ((a, b), (b, a))]
    return lax.ppermute(x, "tm", route)


def near_gather(x):
    return lax.all_gather(x, "tm", axis_index_groups=pairs(0))


def near_swap(x):
    route = [r for a, b in pairs(0) for r in ((a, b), (b, a))]
    return lax.ppermute(x, "tm", route)


def local(query_field, key_field, value_field, tile_offsets, timesteps, gate_weight):
    features = query_field.shape[3]
    heads = features // HD
    tiles = query_field.shape[0] // TT
    tm, size = lax.axis_index("tm"), lax.axis_size("tm")
    core = tm % 2
    other = jnp.where(tm == 0, 0, core)
    cut = ((tm == 0) | (tm == size - 1)).astype(jnp.int32)
    place = jnp.stack([core, cut, other]).astype(jnp.int32)

    xa, xb = split(key_field, value_field, ((0, 3), (3, 3)))
    ra1, la1 = from_behind(xa, 1), from_behind(xa, -1)
    rb1, lb1 = from_behind(xb, 1), from_behind(xb, -1)
    ra2, la2 = from_behind(ra1, 1), from_behind(la1, -1)
    rb2, lb2 = from_behind(rb1[:2], 1), from_behind(lb1[:2], -1)
    rc1, lc1 = lax.optimization_barrier((rb1[2:], lb1[2:], ra2, la2))[:2]
    rc2, lc2 = from_behind(rc1, 1), from_behind(lc1, -1)

    half_freq = FREQ // 2
    frequencies = jnp.exp(-math.log(10000.0) * jnp.arange(half_freq, dtype=jnp.float32) / half_freq)
    angles = timesteps.astype(jnp.float32)[:, None] * frequencies[None, :]
    embedding = jnp.concatenate([jnp.cos(angles), jnp.sin(angles)], axis=1)
    gate_rows = jnp.dot(
        embedding, gate_weight, precision=lax.Precision.HIGHEST, preferred_element_type=jnp.float32
    ).reshape(tiles, heads, HD)

    far, near = pack("pack0", place, [xa, xb])
    far0, near0 = far_gather(far).reshape((2,) + far.shape[1:]), near_swap(near)
    attn = functools.partial(attend, s=tile_offsets, place=place, q=query_field)
    arrays = dict(xa=xa, xb=xb, far0=far0, near0=near0)
    sides = [([("xa", 0, 3), ("xb", 3, 6)], ("far0", None, 0), ("near0", 0, 0))]
    state = attn("own", 0, 0, heads, arrays=arrays, sides=sides)

    pa, pb, qa, qb, state = lax.optimization_barrier((ra1, rb1, la1, lb1, state))
    far, near = pack("pack1", place, [pa, pb], [qa, qb])
    far1, near1 = far_swap(far), near_swap(near)
    arrays = dict(ra1=ra1, rb1=rb1, la1=la1, lb1=lb1, far1=far1, near1=near1)
    sides = [([("ra1", 0, 3), ("rb1", 3, 6)], ("far1", 0, 0), ("near1", 0, 0)),
             ([("la1", 0, 3), ("lb1", 3, 6)], ("far1", 1, 0), ("near1", 1, 0))]
    state = attn("next", 1, 0, heads, arrays=arrays, sides=sides, state=state)

    out = None
    for name, a, n, l1, r2, l2 in (("last_a", 0, 3, la1, ra2, la2), ("last_b", 3, 2, lb1, rb2, lb2), ("last_c", 5, 1, lb1, rc2, lc2)):
        if a == 3:
            r2, l2, state = lax.optimization_barrier((r2, l2, state))
        if a == 5:
            r2, l2, out = lax.optimization_barrier((r2, l2, out))
        far, near = pack("pack_" + name, place, [r2], [l2])
        arrays = dict(l1=l1, far1=far1, near1=near1, r2=r2, l2=l2, far2=far_swap(far), near2=near_swap(near))
        b = a - a % 3
        sides = [([("r2", a, a + n)], ("far2", 0, a), ("near2", 0, a)),
                 ([("l2", a, a + n)], ("far2", 1, a), ("near2", 1, a)),
                 ([("l1", b, b + 3)], ("far1", 1, 0), ("near1", 1, 0))]
        out = attn(name, 2, a, n, arrays=arrays, sides=sides, state=state, gate=gate_rows, prev=out)
    return out


def solution(mesh):
    return jax.shard_map(
        local,
        mesh=mesh,
        in_specs=(
            P("tm", None, "lon", "head"),
            P("tm", None, "lon", "head"),
            P("tm", None, "lon", "head"),
            P("tm", "lon"),
            P("tm"),
            P(None, "head"),
        ),
        out_specs=P("tm", None, "lon", "head"),
        check_vma=False,
    )
```

time: 482 us -> 216 us (0.45)
  waiting for transfers between devices: 313 us -> 77.9 us
  Pallas kernels: 0 us -> 73 us
  local copies, waits for them, and re-layouts: 63.2 us -> 13.9 us
  loops' own time: 31.9 us -> 0 us
  matrix products: 31.4 us -> 0.45 us
  other arithmetic: 24.2 us -> 0.68 us
  starting transfers between devices: 15.8 us -> 33.5 us
  between operations: 0.17 us -> 13.7 us
    ppermute x6 -> x19, waiting for transfers between devices: 313 us -> 60.6 us  [the longest x10 53.7 us: from_behind(): lax.ppermute(block, 'lon', [((i - distance) % size, i) for i in range(siz...]
    pallas_call x0 -> x11, Pallas kernels: none -> 73 us  [the longest x5 50.8 us: attend(): pl.pallas_call(functools.partial(attn_kernel, plan, first, count), out_sh...]
    another operation x1 -> x0, loops' own time: 31.9 us -> none  [local(): lax.map(one_pair, jnp.arange(tiles_here * heads_here, dtype=jnp.int32))]
    dot_general x24 -> x0, matrix products: 30.9 us -> none  [the longest x12 18.5 us: one_pair(): weighted = jnp.dot(weights, value_rows, preferred_element_type=jnp.float32)]
    dynamic_slice x24 -> x0, local copies, waits for them, and re-layouts: 17.9 us -> none  [the longest x12 10.9 us: one_pair(): lax.dynamic_slice(query_tiles, start_at(tile_index, 0, 0, 0, head_index *...]
    ppermute x6 -> x19, starting transfers between devices: 15.8 us -> 33.5 us  [the longest x10 17.7 us: from_behind(): lax.ppermute(block, 'lon', [((i - distance) % size, i) for i in range(siz...]
    all_gather x0 -> x1, waiting for transfers between devices: none -> 17.3 us  [far_gather(): return lax.all_gather(x, 'tm', axis_index_groups=pairs(1))]
    slice x12 -> x4, local copies, waits for them, and re-layouts: 21.7 us -> 6.96 us  [the longest x2 4.15 us: local(): rb2, lb2 = (from_behind(rb1[:2], 1), from_behind(lb1[:2], -1))]
  transfers between devices with their start and end apart: 6 -> 20, of which waited for: 4 -> 7; matrix products, arithmetic and copies ran while one was open for 2% -> 4% of each run, Pallas kernels for 0% -> 25%
where the time goes in v1:
time: 216 us; the launch traced here: 213 us
  waiting for transfers between devices  77.9 us (36%)
  Pallas kernels  73 us (34%)
  starting transfers between devices  33.5 us (16%)
  local copies, waits for them, and re-layouts  13.9 us (6%)
  between operations  13.7 us (6%)
    ppermute x10, waiting for transfers between devices, from_behind(): lax.ppermute(block, 'lon', [((i - distance) % size, i) for i in range(siz...  53.7 us
    pallas_call x5, Pallas kernels, attend(): pl.pallas_call(functools.partial(attn_kernel, plan, first, count), out_sh...  50.8 us
    pallas_call x5, Pallas kernels, pack(): pl.pallas_call(functools.partial(pack_kernel, rows), out_shape=[shape, sh...  18.8 us
    ppermute x10, starting transfers between devices, from_behind(): lax.ppermute(block, 'lon', [((i - distance) % size, i) for i in range(siz...  17.7 us
    all_gather x1, waiting for transfers between devices, far_gather(): return lax.all_gather(x, 'tm', axis_index_groups=pairs(1))  17.3 us
    ppermute x4, starting transfers between devices, far_swap(): return lax.ppermute(x, 'tm', route)  11.3 us
    ppermute x4, waiting for transfers between devices, far_swap(): return lax.ppermute(x, 'tm', route)  6.86 us
    unnamed x27, local copies, waits for them, and re-layouts  6.35 us
  transfers between devices with their start and end apart: 20, of which 7 were waited for; matrix products, arithmetic and copies ran while one was open for 4% of the time, Pallas kernels for 25%

profile of v1, /device:TPU:17, one launch (start us, length us, event | category | flops | bytes accessed | tf_op | source)
XLA Modules:
  0.0 213.2 jit_solution(11164172027560565660)
XLA Ops:
  6.5 3.5 %split_0.1 = (bf16[3,2,2,6,8,8,128]{6,5,4,3,2,1,0:T(8,128)(2,1)}, bf16[3,2,2,6,8,8,128]{6,5,4,3,2,1,0:T(8,128)(2,1)}) custom-call(bf16[12,8,8,768]{3,2,1,0:T(8,128)(2,1)} %k_ref.1, bf16[12,8,8,768]{3,2,1,0:T(8,128)(2,1)} %v_ref.1), custom_call_target="tpu_custom_call" | custom-call | bytes 1024 | tf_op jit(solution)/shard_map/split_0/pallas_call | solution.py:44
  10.6 3.7 %pack0.1 = (bf16[1,6,2,384,128]{4,3,2,1,0:T(8,128)(2,1)}, bf16[1,6,2,384,128]{4,3,2,1,0:T(8,128)(2,1)}) custom-call(s32[3]{0:T(128)} %pad_add_fusion.place_ref, bf16[3,2,2,384,128]{4,3,2,1,0:T(8,128)(2,1)} %bitcast.6, bf16[3,2,2,384,128]{4,3,2,1,0:T(8,128)(2,1)} %bitcast.3.refs_1_), custom_call_target="tpu_custom_call" | custom-call | bytes 1024 | tf_op jit(solution)/shard_map/pack0/pallas_call | solution.py:75
  15.1 8.1 %collective-permute-start = (bf16[3,2,2,384,128]{4,3,2,1,0:T(8,128)(2,1)}, bf16[3,2,2,384,128]{4,3,2,1,0:T(8,128)(2,1)S(1)}, u32[]{:S(2)}, u32[]{:S(2)}) collective-permute-start(bf16[3,2,2,384,128]{4,3,2,1,0:T(8,128)(2,1)} %bitcast.3.refs_1_), channel_id=1, source_target_pairs={{2,0},{4,2},{6,4},{8,6},{10,8},{12,10},{14,12},{16,14},{18,16},{20... | collective-permute-start | bytes 3538952 | tf_op jit(solution)/shard_map/ppermute | solution.py:264
  23.2 5.1 %collective-permute-start.3 = (bf16[3,2,2,384,128]{4,3,2,1,0:T(8,128)(2,1)}, bf16[3,2,2,384,128]{4,3,2,1,0:T(8,128)(2,1)S(1)}, u32[]{:S(2)}, u32[]{:S(2)}) collective-permute-start(bf16[3,2,2,384,128]{4,3,2,1,0:T(8,128)(2,1)} %bitcast.7), channel_id=1, source_target_pairs={{2,0},{4,2},{6,4},{8,6},{10,8},{12,10},{14,12},{16,14},{18,16},{20... | collective-permute-start | bytes 3538952 | tf_op jit(solution)/shard_map/ppermute | solution.py:264
  28.9 17.3 %all-gather.3.cloned.1.call-done.refs_2_ = bf16[2,6,2,384,128]{4,3,2,1,0:T(8,128)(2,1)} async-done(((bf16[1,6,2,384,128]{4,3,2,1,0:T(8,128)(2,1)}), bf16[2,6,2,384,128]{4,3,2,1,0:T(8,128)(2,1)}) %all-gather.3.cloned.1.call-update) | async-done | bytes 2359312 | tf_op jit(solution)/shard_map/all_gather | solution.py:277
  46.2 14.6 %own.1.refs_6_ = f32[6,2,384,384]{3,2,1,0:T(8,128)} custom-call(s32[2,1]{1,0:T(2,128)} %copy.23.s_ref, s32[3]{0:T(128)} %pad_add_fusion.place_ref, bf16[12,8,8,768]{3,2,1,0:T(8,128)(2,1)} %q_ref.9, bf16[3,2,2,384,128]{4,3,2,1,0:T(8,128)(2,1)} %bitcast.9, bf16[3,2,2,384,128]{4,3,2,1,0:T(8,128)(2,1)} %bitcast.3.refs_1_, ...), custom_call_target="tpu_custom_call" | custom-call | bytes 1024 | tf_op jit(solution)/shard_map/own/pallas_call | solution.py:240
  60.9 13.2 %collective-permute-done.3.refs_2_.refs_0_ = bf16[3,2,2,384,128]{4,3,2,1,0:T(8,128)(2,1)S(1)} collective-permute-done((bf16[3,2,2,384,128]{4,3,2,1,0:T(8,128)(2,1)}, bf16[3,2,2,384,128]{4,3,2,1,0:T(8,128)(2,1)S(1)}, u32[]{:S(2)}, u32[]{:S(2)}) %collective-permute-start.3) | collective-permute-done | bytes 1179680 | tf_op jit(solution)/shard_map/ppermute | solution.py:264
  74.1 5.5 %collective-permute-done.1.refs_0_ = bf16[3,2,2,384,128]{4,3,2,1,0:T(8,128)(2,1)} collective-permute-done((bf16[3,2,2,384,128]{4,3,2,1,0:T(8,128)(2,1)}, bf16[3,2,2,384,128]{4,3,2,1,0:T(8,128)(2,1)}, u32[]{:S(2)}, u32[]{:S(2)}) %collective-permute-start.1) | collective-permute-done | bytes 1179680 | tf_op jit(solution)/shard_map/ppermute | solution.py:264
  79.6 5.2 %pack1.1 = (bf16[2,6,2,384,128]{4,3,2,1,0:T(8,128)(2,1)}, bf16[2,6,2,384,128]{4,3,2,1,0:T(8,128)(2,1)}) custom-call(s32[3]{0:T(128)} %pad_add_fusion.place_ref, bf16[3,2,2,384,128]{4,3,2,1,0:T(8,128)(2,1)} %collective-permute-done.1.refs_0_, bf16[3,2,2,384,128]{4,3,2,1,0:T(8,128)(2,1)} %collective-permute-done.2.refs_1_, ...), custom_call_target="tpu_custom_call" | custom-call | bytes 1024 | tf_op jit(solution)/shard_map/pack1/pallas_call | solution.py:75
  84.8 4.0 %collective-permute-start.5 = (bf16[2,6,2,384,128]{4,3,2,1,0:T(8,128)(2,1)}, bf16[2,6,2,384,128]{4,3,2,1,0:T(8,128)(2,1)S(1)}, u32[]{:S(2)}, u32[]{:S(2)}) collective-permute-start(bf16[2,6,2,384,128]{4,3,2,1,0:T(8,128)(2,1)} %get-tuple-element.38), channel_id=1, source_target_pairs={{32,64},{64,32},{96,128},{128,96},{160,192},{192,160},{33,65},{65,... | collective-permute-start | bytes 7077896 | tf_op jit(solution)/shard_map/ppermute | solution.py:282
  88.9 1.0 collective-permute-start.8
  90.4 26.0 %collective-permute-done.8.refs_1_.refs_4_ = bf16[3,2,2,384,128]{4,3,2,1,0:T(8,128)(2,1)} collective-permute-done((bf16[3,2,2,384,128]{4,3,2,1,0:T(8,128)(2,1)}, bf16[3,2,2,384,128]{4,3,2,1,0:T(8,128)(2,1)}, u32[]{:S(2)}, u32[]{:S(2)}) %collective-permute-start.8) | collective-permute-done | bytes 1179680 | tf_op jit(solution)/shard_map/ppermute | solution.py:264
  116.4 4.2 %collective-permute-done.7.refs_0_.refs_3_ = bf16[3,2,2,384,128]{4,3,2,1,0:T(8,128)(2,1)} collective-permute-done((bf16[3,2,2,384,128]{4,3,2,1,0:T(8,128)(2,1)}, bf16[3,2,2,384,128]{4,3,2,1,0:T(8,128)(2,1)}, u32[]{:S(2)}, u32[]{:S(2)}) %collective-permute-start.7) | collective-permute-done | bytes 1179680 | tf_op jit(solution)/shard_map/ppermute | solution.py:264
  120.6 3.7 %pack_last_a.1 = (bf16[2,3,2,384,128]{4,3,2,1,0:T(8,128)(2,1)}, bf16[2,3,2,384,128]{4,3,2,1,0:T(8,128)(2,1)}) custom-call(s32[3]{0:T(128)} %pad_add_fusion.place_ref, bf16[3,2,2,384,128]{4,3,2,1,0:T(8,128)(2,1)} %collective-permute-done.7.refs_0_.refs_3_, bf16[3,2,2,384,128]{4,3,2,1,0:T(8,128)(2,1)} %collective-permute-done.8.refs_1_.refs_4_), custom_call_target="tpu_custom_call" | custom-call | bytes 1024 | tf_op jit(solution)/shard_map/pack_last_a/pallas_call | solution.py:75
  124.3 3.4 %collective-permute-start.15 = (bf16[2,3,2,384,128]{4,3,2,1,0:T(8,128)(2,1)}, bf16[2,3,2,384,128]{4,3,2,1,0:T(8,128)(2,1)}, u32[]{:S(2)}, u32[]{:S(2)}) collective-permute-start(bf16[2,3,2,384,128]{4,3,2,1,0:T(8,128)(2,1)} %get-tuple-element.48), channel_id=1, source_target_pairs={{32,64},{64,32},{96,128},{128,96},{160,192},{192,160},{33,65},{65,... | collective-permute-start | bytes 3538952 | tf_op jit(solution)/shard_map/ppermute | solution.py:282
  127.8 2.1 slice.19
  129.9 2.1 slice.18
  131.9 1.5 collective-permute-start.11
  134.8 14.9 %next.1.refs_7_ = f32[6,2,384,384]{3,2,1,0:T(8,128)} custom-call(s32[2,1]{1,0:T(2,128)} %copy.23.s_ref, s32[3]{0:T(128)} %pad_add_fusion.place_ref, bf16[12,8,8,768]{3,2,1,0:T(8,128)(2,1)} %q_ref.9, bf16[3,2,2,384,128]{4,3,2,1,0:T(8,128)(2,1)} %collective-permute-done.1.refs_0_, bf16[3,2,2,384,128]{4,3,2,1,0:T(8,128)(2,1)} %collective-permute-done.2.refs_1_, ...), custom_call_target="tpu_custom_call" | custom-call | bytes 1024 | tf_op jit(solution)/shard_map/next/pallas_call | solution.py:240
  149.8 4.9 %collective-permute-done.11.refs_0_.refs_3_ = bf16[2,2,2,384,128]{4,3,2,1,0:T(8,128)(2,1)} collective-permute-done((bf16[2,2,2,384,128]{4,3,2,1,0:T(8,128)(2,1)}, bf16[2,2,2,384,128]{4,3,2,1,0:T(8,128)(2,1)}, u32[]{:S(2)}, u32[]{:S(2)}) %collective-permute-start.11) | collective-permute-done | bytes 786464 | tf_op jit(solution)/shard_map/ppermute | solution.py:264
  154.7 3.3 %pack_last_b.1 = (bf16[2,2,2,384,128]{4,3,2,1,0:T(8,128)(2,1)}, bf16[2,2,2,384,128]{4,3,2,1,0:T(8,128)(2,1)}) custom-call(s32[3]{0:T(128)} %pad_add_fusion.place_ref, bf16[2,2,2,384,128]{4,3,2,1,0:T(8,128)(2,1)} %collective-permute-done.11.refs_0_.refs_3_, bf16[2,2,2,384,128]{4,3,2,1,0:T(8,128)(2,1)} %copy-done.4), custom_call_target="tpu_custom_call" | custom-call | bytes 1024 | tf_op jit(solution)/shard_map/pack_last_b/pallas_call | solution.py:75
  157.9 2.0 collective-permute-start.13
  159.9 2.3 %collective-permute-start.14 = (bf16[2,2,2,384,128]{4,3,2,1,0:T(8,128)(2,1)}, bf16[2,2,2,384,128]{4,3,2,1,0:T(8,128)(2,1)S(1)}, u32[]{:S(2)}, u32[]{:S(2)}) collective-permute-start(bf16[2,2,2,384,128]{4,3,2,1,0:T(8,128)(2,1)} %get-tuple-element.46), channel_id=1, source_target_pairs={{0,32},{32,0},{64,96},{96,64},{128,160},{160,128},{192,224},{224,1... | collective-permute-start | bytes 2359304 | tf_op jit(solution)/shard_map/ppermute | solution.py:291
  162.2 1.8 slice.17
  164.0 1.0 slice.16
  165.2 1.4 collective-permute-start.9
  167.8 9.4 %last_a.1.refs_9_ = bf16[12,8,8,768]{3,2,1,0:T(8,128)(2,1)} custom-call(s32[2,1]{1,0:T(2,128)} %copy.23.s_ref, s32[3]{0:T(128)} %pad_add_fusion.place_ref, bf16[12,8,8,768]{3,2,1,0:T(8,128)(2,1)} %q_ref.9, bf16[3,2,2,384,128]{4,3,2,1,0:T(8,128)(2,1)} %copy-done.3, bf16[2,6,2,384,128]{4,3,2,1,0:T(8,128)(2,1)} %copy-done.1, ...), custom_call_target="tpu_custom_call" | custom-call | bytes 1024 | tf_op jit(solution)/shard_map/last_a/pallas_call | solution.py:240
  179.0 7.1 %last_b.1.refs_9_ = bf16[12,8,8,768]{3,2,1,0:T(8,128)(2,1)} custom-call(s32[2,1]{1,0:T(2,128)} %copy.23.s_ref, s32[3]{0:T(128)} %pad_add_fusion.place_ref, bf16[12,8,8,768]{3,2,1,0:T(8,128)(2,1)} %q_ref.9, bf16[3,2,2,384,128]{4,3,2,1,0:T(8,128)(2,1)} %copy-done.2, bf16[2,6,2,384,128]{4,3,2,1,0:T(8,128)(2,1)} %copy-done.1, ...), custom_call_target="tpu_custom_call", output_to_operand_aliasing={{}: (12, {})} | custom-call | bytes 1024 | tf_op jit(solution)/shard_map/last_b/pallas_call | solution.py:240
  187.7 2.9 %pack_last_c.1 = (bf16[2,1,2,384,128]{4,3,2,1,0:T(8,128)(2,1)}, bf16[2,1,2,384,128]{4,3,2,1,0:T(8,128)(2,1)}) custom-call(s32[3]{0:T(128)} %pad_add_fusion.place_ref, bf16[1,2,2,384,128]{4,3,2,1,0:T(8,128)(2,1)} %copy-done.6, bf16[1,2,2,384,128]{4,3,2,1,0:T(8,128)(2,1)} %copy-done.5), custom_call_target="tpu_custom_call" | custom-call | bytes 1024 | tf_op jit(solution)/shard_map/pack_last_c/pallas_call | solution.py:75
  190.6 1.9 collective-permute-start.17
  193.2 6.8 %collective-permute-done.17.refs_5_ = bf16[2,1,2,384,128]{4,3,2,1,0:T(8,128)(2,1)S(1)} collective-permute-done((bf16[2,1,2,384,128]{4,3,2,1,0:T(8,128)(2,1)}, bf16[2,1,2,384,128]{4,3,2,1,0:T(8,128)(2,1)S(1)}, u32[]{:S(2)}, u32[]{:S(2)}) %collective-permute-start.17) | collective-permute-done | bytes 393248 | tf_op jit(solution)/shard_map/ppermute | solution.py:282
  201.7 4.7 %last_c.1 = bf16[12,8,8,768]{3,2,1,0:T(8,128)(2,1)} custom-call(s32[2,1]{1,0:T(2,128)} %copy.23.s_ref, s32[3]{0:T(128)} %pad_add_fusion.place_ref, bf16[12,8,8,768]{3,2,1,0:T(8,128)(2,1)} %q_ref.9, bf16[3,2,2,384,128]{4,3,2,1,0:T(8,128)(2,1)} %copy-done.2, bf16[2,6,2,384,128]{4,3,2,1,0:T(8,128)(2,1)} %copy-done.1, ...), custom_call_target="tpu_custom_call", output_to_operand_aliasing={{}: (12, {})} | custom-call | bytes 1024 | tf_op jit(solution)/shard_map/last_c/pallas_call | solution.py:240
  (57 shorter events, 11.0 us)
Async XLA Ops:
  6.5 160.2 %copy-start = (f32[256,768]{1,0:T(8,128)S(1)}, f32[256,768]{1,0:T(8,128)}, u32[]{:S(2)}) copy-start(f32[256,768]{1,0:T(8,128)} %param.11) | copy-start | bytes 2359300
  6.5 39.7 %all-gather.3.cloned.1.call-start = ((), (), s32[]{:S(2)}) async-start(), calls=%async_computation | async-start | bytes 3538944 | tf_op jit(solution)/shard_map/all_gather | solution.py:277
  14.3 13.9 %copy-start.11 = (s32[2,1]{0,1:T(1,128)S(1)}, s32[2,1]{0,1:T(1,128)}, u32[]{:S(2)}) copy-start(s32[2,1]{0,1:T(1,128)} %param.9) | copy-start | bytes 28
  14.3 14.6 %collective-permute-start.4 = (bf16[1,6,2,384,128]{4,3,2,1,0:T(8,128)(2,1)}, bf16[1,6,2,384,128]{4,3,2,1,0:T(8,128)(2,1)}, u32[]{:S(2)}, u32[]{:S(2)}) collective-permute-start(bf16[1,6,2,384,128]{4,3,2,1,0:T(8,128)(2,1)} %get-tuple-element.33), channel_id=1, source_target_pairs={{0,32},{32,0},{64,96},{96,64},{128,160},{160,128},{192,224},{224,1... | collective-permute-start | bytes 3538952 | tf_op jit(solution)/shard_map/ppermute | solution.py:291
  15.1 45.7 %collective-permute-start = (bf16[3,2,2,384,128]{4,3,2,1,0:T(8,128)(2,1)}, bf16[3,2,2,384,128]{4,3,2,1,0:T(8,128)(2,1)S(1)}, u32[]{:S(2)}, u32[]{:S(2)}) collective-permute-start(bf16[3,2,2,384,128]{4,3,2,1,0:T(8,128)(2,1)} %bitcast.3.refs_1_), channel_id=1, source_target_pairs={{2,0},{4,2},{6,4},{8,6},{10,8},{12,10},{14,12},{16,14},{18,16},{20... | collective-permute-start | bytes 3538952 | tf_op jit(solution)/shard_map/ppermute | solution.py:264
  23.2 37.7 %collective-permute-start.2 = (bf16[3,2,2,384,128]{4,3,2,1,0:T(8,128)(2,1)}, bf16[3,2,2,384,128]{4,3,2,1,0:T(8,128)(2,1)}, u32[]{:S(2)}, u32[]{:S(2)}) collective-permute-start(bf16[3,2,2,384,128]{4,3,2,1,0:T(8,128)(2,1)} %bitcast.3.refs_1_), channel_id=1, source_target_pairs={{30,0},{0,2},{2,4},{4,6},{6,8},{8,10},{10,12},{12,14},{14,16},{16,... | collective-permute-start | bytes 3538952 | tf_op jit(solution)/shard_map/ppermute | solution.py:264
  23.2 50.9 %collective-permute-start.3 = (bf16[3,2,2,384,128]{4,3,2,1,0:T(8,128)(2,1)}, bf16[3,2,2,384,128]{4,3,2,1,0:T(8,128)(2,1)S(1)}, u32[]{:S(2)}, u32[]{:S(2)}) collective-permute-start(bf16[3,2,2,384,128]{4,3,2,1,0:T(8,128)(2,1)} %bitcast.7), channel_id=1, source_target_pairs={{2,0},{4,2},{6,4},{8,6},{10,8},{12,10},{14,12},{16,14},{18,16},{20... | collective-permute-start | bytes 3538952 | tf_op jit(solution)/shard_map/ppermute | solution.py:264
  28.2 51.3 %collective-permute-start.1 = (bf16[3,2,2,384,128]{4,3,2,1,0:T(8,128)(2,1)}, bf16[3,2,2,384,128]{4,3,2,1,0:T(8,128)(2,1)}, u32[]{:S(2)}, u32[]{:S(2)}) collective-permute-start(bf16[3,2,2,384,128]{4,3,2,1,0:T(8,128)(2,1)} %bitcast.8), channel_id=1, source_target_pairs={{30,0},{0,2},{2,4},{4,6},{6,8},{8,10},{10,12},{12,14},{14,16},{16,... | collective-permute-start | bytes 3538952 | tf_op jit(solution)/shard_map/ppermute | solution.py:264
  60.9 18.7 %copy-start.2 = (bf16[3,2,2,384,128]{4,3,2,1,0:T(8,128)(2,1)}, bf16[3,2,2,384,128]{4,3,2,1,0:T(8,128)(2,1)S(1)}, u32[]{:S(2)}) copy-start(bf16[3,2,2,384,128]{4,3,2,1,0:T(8,128)(2,1)S(1)} %collective-permute-done.refs_3_.refs_0_) | copy-start | bytes 3538948
  74.1 5.5 %copy-start.3 = (bf16[3,2,2,384,128]{4,3,2,1,0:T(8,128)(2,1)}, bf16[3,2,2,384,128]{4,3,2,1,0:T(8,128)(2,1)S(1)}, u32[]{:S(2)}) copy-start(bf16[3,2,2,384,128]{4,3,2,1,0:T(8,128)(2,1)S(1)} %collective-permute-done.3.refs_2_.refs_0_) | copy-start | bytes 3538948
  84.8 48.6 %collective-permute-start.5 = (bf16[2,6,2,384,128]{4,3,2,1,0:T(8,128)(2,1)}, bf16[2,6,2,384,128]{4,3,2,1,0:T(8,128)(2,1)S(1)}, u32[]{:S(2)}, u32[]{:S(2)}) collective-permute-start(bf16[2,6,2,384,128]{4,3,2,1,0:T(8,128)(2,1)} %get-tuple-element.38), channel_id=1, source_target_pairs={{32,64},{64,32},{96,128},{128,96},{160,192},{192,160},{33,65},{65,... | collective-permute-start | bytes 7077896 | tf_op jit(solution)/shard_map/ppermute | solution.py:282
  88.8 45.3 %collective-permute-start.6 = (bf16[2,6,2,384,128]{4,3,2,1,0:T(8,128)(2,1)}, bf16[2,6,2,384,128]{4,3,2,1,0:T(8,128)(2,1)}, u32[]{:S(2)}, u32[]{:S(2)}) collective-permute-start(bf16[2,6,2,384,128]{4,3,2,1,0:T(8,128)(2,1)} %get-tuple-element.39), channel_id=1, source_target_pairs={{0,32},{32,0},{64,96},{96,64},{128,160},{160,128},{192,224},{224,1... | collective-permute-start | bytes 7077896 | tf_op jit(solution)/shard_map/ppermute | solution.py:291
  88.9 27.5 %collective-permute-start.8 = (bf16[3,2,2,384,128]{4,3,2,1,0:T(8,128)(2,1)}, bf16[3,2,2,384,128]{4,3,2,1,0:T(8,128)(2,1)}, u32[]{:S(2)}, u32[]{:S(2)}) collective-permute-start(bf16[3,2,2,384,128]{4,3,2,1,0:T(8,128)(2,1)} %copy-done.3), channel_id=1, source_target_pairs={{2,0},{4,2},{6,4},{8,6},{10,8},{12,10},{14,12},{16,14},{18,16},{20... | collective-permute-start | bytes 3538952 | tf_op jit(solution)/shard_map/ppermute | solution.py:264
  89.9 30.7 %collective-permute-start.7 = (bf16[3,2,2,384,128]{4,3,2,1,0:T(8,128)(2,1)}, bf16[3,2,2,384,128]{4,3,2,1,0:T(8,128)(2,1)}, u32[]{:S(2)}, u32[]{:S(2)}) collective-permute-start(bf16[3,2,2,384,128]{4,3,2,1,0:T(8,128)(2,1)} %collective-permute-done.1.refs_0_), channel_id=1, source_target_pairs={{30,0},{0,2},{2,4},{4,6},{6,8},{8,10},{10,12},{12,14},{14,16},{16,... | collective-permute-start | bytes 3538952 | tf_op jit(solution)/shard_map/ppermute | solution.py:264
  124.3 40.8 %collective-permute-start.15 = (bf16[2,3,2,384,128]{4,3,2,1,0:T(8,128)(2,1)}, bf16[2,3,2,384,128]{4,3,2,1,0:T(8,128)(2,1)}, u32[]{:S(2)}, u32[]{:S(2)}) collective-permute-start(bf16[2,3,2,384,128]{4,3,2,1,0:T(8,128)(2,1)} %get-tuple-element.48), channel_id=1, source_target_pairs={{32,64},{64,32},{96,128},{128,96},{160,192},{192,160},{33,65},{65,... | collective-permute-start | bytes 3538952 | tf_op jit(solution)/shard_map/ppermute | solution.py:282
  129.9 19.9 %collective-permute-start.12 = (bf16[2,2,2,384,128]{4,3,2,1,0:T(8,128)(2,1)}, bf16[2,2,2,384,128]{4,3,2,1,0:T(8,128)(2,1)S(1)}, u32[]{:S(2)}, u32[]{:S(2)}) collective-permute-start(bf16[2,2,2,384,128]{4,3,2,1,0:T(8,128)(2,1)} %slice.19), channel_id=1, source_target_pairs={{2,0},{4,2},{6,4},{8,6},{10,8},{12,10},{14,12},{16,14},{18,16},{20... | collective-permute-start | bytes 2359304 | tf_op jit(solution)/shard_map/ppermute | solution.py:264
  131.9 22.7 %collective-permute-start.11 = (bf16[2,2,2,384,128]{4,3,2,1,0:T(8,128)(2,1)}, bf16[2,2,2,384,128]{4,3,2,1,0:T(8,128)(2,1)}, u32[]{:S(2)}, u32[]{:S(2)}) collective-permute-start(bf16[2,2,2,384,128]{4,3,2,1,0:T(8,128)(2,1)} %slice.18), channel_id=1, source_target_pairs={{30,0},{0,2},{2,4},{4,6},{6,8},{8,10},{10,12},{12,14},{14,16},{16,... | collective-permute-start | bytes 2359304 | tf_op jit(solution)/shard_map/ppermute | solution.py:264
  133.4 1.4 copy-start.1
  133.4 34.4 %collective-permute-start.16 = (bf16[2,3,2,384,128]{4,3,2,1,0:T(8,128)(2,1)}, bf16[2,3,2,384,128]{4,3,2,1,0:T(8,128)(2,1)}, u32[]{:S(2)}, u32[]{:S(2)}) collective-permute-start(bf16[2,3,2,384,128]{4,3,2,1,0:T(8,128)(2,1)} %get-tuple-element.49), channel_id=1, source_target_pairs={{0,32},{32,0},{64,96},{96,64},{128,160},{160,128},{192,224},{224,1... | collective-permute-start | bytes 3538952 | tf_op jit(solution)/shard_map/ppermute | solution.py:291
  149.8 12.5 %copy-start.12 = (s32[2]{0:T(128)S(1)}, s32[2]{0:T(128)}, u32[]{:S(2)}) copy-start(s32[2]{0:T(128)} %param.10) | copy-start | bytes 28
  149.8 4.9 %copy-start.4 = (bf16[2,2,2,384,128]{4,3,2,1,0:T(8,128)(2,1)}, bf16[2,2,2,384,128]{4,3,2,1,0:T(8,128)(2,1)S(1)}, u32[]{:S(2)}) copy-start(bf16[2,2,2,384,128]{4,3,2,1,0:T(8,128)(2,1)S(1)} %collective-permute-done.12.refs_1_.refs_4_) | copy-start | bytes 2359300
  157.9 19.3 %collective-permute-start.13 = (bf16[2,2,2,384,128]{4,3,2,1,0:T(8,128)(2,1)}, bf16[2,2,2,384,128]{4,3,2,1,0:T(8,128)(2,1)S(1)}, u32[]{:S(2)}, u32[]{:S(2)}) collective-permute-start(bf16[2,2,2,384,128]{4,3,2,1,0:T(8,128)(2,1)} %get-tuple-element.45), channel_id=1, source_target_pairs={{32,64},{64,32},{96,128},{128,96},{160,192},{192,160},{33,65},{65,... | collective-permute-start | bytes 2359304 | tf_op jit(solution)/shard_map/ppermute | solution.py:282
  159.9 17.3 %collective-permute-start.14 = (bf16[2,2,2,384,128]{4,3,2,1,0:T(8,128)(2,1)}, bf16[2,2,2,384,128]{4,3,2,1,0:T(8,128)(2,1)S(1)}, u32[]{:S(2)}, u32[]{:S(2)}) collective-permute-start(bf16[2,2,2,384,128]{4,3,2,1,0:T(8,128)(2,1)} %get-tuple-element.46), channel_id=1, source_target_pairs={{0,32},{32,0},{64,96},{96,64},{128,160},{160,128},{192,224},{224,1... | collective-permute-start | bytes 2359304 | tf_op jit(solution)/shard_map/ppermute | solution.py:291
  165.1 21.1 %collective-permute-start.10 = (bf16[1,2,2,384,128]{4,3,2,1,0:T(8,128)(2,1)}, bf16[1,2,2,384,128]{4,3,2,1,0:T(8,128)(2,1)S(1)}, u32[]{:S(2)}, u32[]{:S(2)}) collective-permute-start(bf16[1,2,2,384,128]{4,3,2,1,0:T(8,128)(2,1)} %slice.17), channel_id=1, source_target_pairs={{2,0},{4,2},{6,4},{8,6},{10,8},{12,10},{14,12},{16,14},{18,16},{20... | collective-permute-start | bytes 1179656 | tf_op jit(solution)/shard_map/ppermute | solution.py:264
  165.2 21.0 %collective-permute-start.9 = (bf16[1,2,2,384,128]{4,3,2,1,0:T(8,128)(2,1)S(1)}, bf16[1,2,2,384,128]{4,3,2,1,0:T(8,128)(2,1)S(1)}, u32[]{:S(2)}, u32[]{:S(2)}) collective-permute-start(bf16[1,2,2,384,128]{4,3,2,1,0:T(8,128)(2,1)S(1)} %slice.16), channel_id=1, source_target_pairs={{30,0},{0,2},{2,4},{4,6},{6,8},{8,10},{10,12},{12,14},{14,16},{16,... | collective-permute-start | bytes 1179656 | tf_op jit(solution)/shard_map/ppermute | solution.py:264
  177.3 0.9 copy-start.7
  178.1 0.9 copy-start.8
  186.2 0.8 copy-start.5
  190.6 9.5 %collective-permute-start.17 = (bf16[2,1,2,384,128]{4,3,2,1,0:T(8,128)(2,1)}, bf16[2,1,2,384,128]{4,3,2,1,0:T(8,128)(2,1)S(1)}, u32[]{:S(2)}, u32[]{:S(2)}) collective-permute-start(bf16[2,1,2,384,128]{4,3,2,1,0:T(8,128)(2,1)} %get-tuple-element.52), channel_id=1, source_target_pairs={{32,64},{64,32},{96,128},{128,96},{160,192},{192,160},{33,65},{65,... | collective-permute-start | bytes 1179656 | tf_op jit(solution)/shard_map/ppermute | solution.py:282
  192.5 7.6 %collective-permute-start.18 = (bf16[2,1,2,384,128]{4,3,2,1,0:T(8,128)(2,1)}, bf16[2,1,2,384,128]{4,3,2,1,0:T(8,128)(2,1)S(1)}, u32[]{:S(2)}, u32[]{:S(2)}) collective-permute-start(bf16[2,1,2,384,128]{4,3,2,1,0:T(8,128)(2,1)} %get-tuple-element.53), channel_id=1, source_target_pairs={{0,32},{32,0},{64,96},{96,64},{128,160},{160,128},{192,224},{224,1... | collective-permute-start | bytes 1179656 | tf_op jit(solution)/shard_map/ppermute | solution.py:291
  200.1 0.8 copy-start.9
  200.9 0.8 copy-start.10
  (1 other events, 0.7 us)
Sparse Core Ops, SparseCore 0:
  14.5 31.6 all-gather.2

commit v2 on v1

v2 whole, which is shorter than its diff:
```python
import functools
import itertools
import math

import jax
import jax.numpy as jnp
from jax import lax
from jax.experimental import pallas as pl
from jax.experimental.pallas import tpu as pltpu
from jax.sharding import PartitionSpec as P

HD = 128
FREQ = 256
ROWS = 384
TT = 6
SCALE = math.log2(math.e) / math.sqrt(HD)
ANY = pl.BlockSpec(memory_space=pltpu.HBM)
SMALL = pl.CostEstimate(flops=0, bytes_accessed=1024, transcendentals=0)
VMEM = pl.BlockSpec(memory_space=pltpu.VMEM)
SMEM = pl.BlockSpec(memory_space=pltpu.SMEM)


PICKS = (lambda s: 0 * s, lambda s: jnp.where(s > 0, 1, 0), lambda s: jnp.where(s == 0, 2, jnp.where(s > 0, 1, 0)))


def run_copies(copies):
    for copy in copies:
        copy.start()
    for copy in copies:
        copy.wait()


def split_kernel(k_ref, v_ref, out, sem):
    copies = []
    for t in range(2):
        for i in range(out.shape[0]):
            for which, ref in enumerate((k_ref, v_ref)):
                source = ref.at[pl.ds(t * TT, TT), :, :, pl.ds(i * HD, HD)]
                copies.append(pltpu.make_async_copy(source, out.at[i, t, which], sem.at[len(copies)]))
    run_copies(copies)


def split(k, v):
    n = k.shape[3] // HD
    x = pl.pallas_call(
        split_kernel,
        out_shape=jax.ShapeDtypeStruct((n, 2, 2, TT, 8, 8, HD), k.dtype),
        in_specs=[ANY, ANY],
        out_specs=VMEM,
        scratch_shapes=[pltpu.SemaphoreType.DMA((4 * n,))],
        cost_estimate=SMALL,
        compiler_params=pltpu.CompilerParams(vmem_limit_bytes=60 * 2**20),
        name="split",
    )(k, v)
    return x.reshape(x.shape[:3] + (ROWS, HD))


def pack_kernel(cuts, pick, place_ref, *refs):
    n = len(refs) - 2 * len(cuts) - 1
    ins, far, near, sem = refs[:n], refs[n:n + len(cuts)], refs[n + len(cuts):-1], refs[-1]
    core = place_ref[0]
    for w, (outs, tile, side) in enumerate(((far, core, pick(place_ref[2])), (near, 1 - core, pick(place_ref[3])))):
        for c, ref in enumerate(ins):
            @pl.when(side == c)
            def _():
                for i, (out, (first, count)) in enumerate(zip(outs, cuts)):
                    pltpu.make_async_copy(ref.at[pl.ds(first, count), tile], out, sem.at[w, i]).start()
    for w, outs in enumerate((far, near)):
        for i, out in enumerate(outs):
            pltpu.make_async_copy(out, out, sem.at[w, i]).wait()


def pack(name, phase, place, xs, cuts):
    shapes = [jax.ShapeDtypeStruct((count,) + xs[0].shape[2:], xs[0].dtype) for _, count in cuts]
    outs = pl.pallas_call(
        functools.partial(pack_kernel, cuts, PICKS[phase]),
        out_shape=shapes + shapes,
        in_specs=[SMEM] + [ANY] * len(xs),
        out_specs=[VMEM] * (2 * len(cuts)),
        scratch_shapes=[pltpu.SemaphoreType.DMA((2, len(cuts)))],
        cost_estimate=SMALL,
        compiler_params=pltpu.CompilerParams(vmem_limit_bytes=60 * 2**20),
        name=name,
    )(place, *xs)
    return outs[:len(cuts)], outs[len(cuts):]


def attn_kernel(plan, first, count, s_ref, place_ref, q_ref, *refs):
    names, starts, finishes, sides, pick, halo_first = plan
    ops = dict(zip(names, refs))
    out_ref, kv, qv, sc0, sc1, top0, top1, si, so, ov, ksem, qsem, isem, osem = refs[len(refs) - 14:]
    core, cut = place_ref[0], place_ref[1]

    def fill(i, slot):
        h = first + i
        for t in range(2):
            side = pick(s_ref[t, 0])
            halo = kv.at[slot, t, 2 * t]
            for c, (name, low) in enumerate(sides):
                own = ops[name].at[h - low]

                @pl.when(side == c)
                def _():
                    pltpu.make_async_copy(own, kv.at[slot, t, pl.ds(1 - t, 2)], ksem.at[slot, t]).start()

                @pl.when((side == c) & (core == t) & (cut != 0))
                def _():
                    pltpu.make_async_copy(own.at[t], halo, ksem.at[slot, t]).start()

            @pl.when((core == t) & (cut == 0))
            def _():
                pltpu.make_async_copy(ops["far"].at[h - halo_first], halo, ksem.at[slot, t]).start()

            @pl.when(core != t)
            def _():
                pltpu.make_async_copy(ops["near"].at[h - halo_first], halo, ksem.at[slot, t]).start()
        q_copy(i, slot).start()
        if not starts:
            state_in(i, slot).start()

    def filled(i, slot):
        for t in range(2):
            pltpu.make_async_copy(kv.at[slot, t], kv.at[slot, t], ksem.at[slot, t]).wait()
        q_copy(i, slot).wait()
        if not starts:
            state_in(i, slot).wait()

    def lanes(i):
        return pl.ds(pl.multiple_of((first + i) * HD, HD), HD)

    def q_copy(i, slot):
        return pltpu.make_async_copy(q_ref.at[:, :, :, lanes(i)], qv.at[slot], qsem.at[slot])

    def state_in(i, slot):
        return pltpu.make_async_copy(ops["state"].at[first + i], si.at[slot], isem.at[slot])

    def result(i):
        slot = lax.rem(i, 2)
        if finishes:
            return pltpu.make_async_copy(ov.at[slot], out_ref.at[:, :, :, lanes(i)], osem.at[slot])
        return pltpu.make_async_copy(so.at[slot], out_ref.at[first + i], osem.at[slot])

    def scores(slot, t, sc, top):
        q = qv[slot, pl.ds(t * TT, TT)].reshape(ROWS, HD)
        m = None
        for j in range(3):
            s = lax.dot_general(q, kv[slot, t, j, 0], (((1,), (1,)), ((), ())), preferred_element_type=jnp.float32)
            sc[j] = s
            mj = jnp.maximum(jnp.maximum(s[:, :128], s[:, 128:256]), s[:, 256:])
            m = mj if m is None else jnp.maximum(m, mj)
            yield
        m = jnp.broadcast_to(jnp.max(m, axis=1, keepdims=True), (ROWS, HD))
        if not starts:
            m = jnp.maximum(m, si[slot, t, :, 2 * HD:])
        top[...] = m
        yield

    def weigh(i, slot, t, sc, top):
        to = lax.rem(i, 2)
        m1 = top[...]
        m = jnp.concatenate([m1] * 3, axis=1)
        acc = None
        if not starts:
            fade = jnp.exp2((si[slot, t, :, 2 * HD:] - m1) * SCALE)
            acc = si[slot, t, :, :2 * HD] * jnp.concatenate([fade, fade], axis=1)
        for j in range(3):
            p = jnp.exp2((sc[j] - m) * SCALE).astype(jnp.bfloat16)
            v2 = jnp.concatenate([kv[slot, t, j, 1], jnp.ones((ROWS, HD), jnp.bfloat16)], axis=1)
            if j == 2 * t:
                v2 = jnp.where((cut != 0) & (core == t), jnp.zeros_like(v2), v2)
            part = jnp.dot(p, v2, preferred_element_type=jnp.float32)
            acc = part if acc is None else acc + part
            yield
        if finishes:
            o = acc[:, :HD] / acc[:, HD:] * ops["gate"][t, first + i]
            ov[to, pl.ds(t * TT, TT)] = o.astype(jnp.bfloat16).reshape(TT, 8, 8, HD)
        else:
            so[to, t, :, :2 * HD] = acc
            so[to, t, :, 2 * HD:] = m1
        yield

    def both(*steps):
        for _ in itertools.zip_longest(*steps):
            pass

    def head(i, last):
        slot, ahead = lax.rem(i, 3), lax.rem(i + 1, 3)
        if not last:
            @pl.when(i + 2 < count)
            def _():
                fill(i + 2, lax.rem(i + 2, 3))

        @pl.when(i >= 2)
        def _():
            result(i - 2).wait()
        both(weigh(i, slot, 0, sc0, top0), scores(slot, 1, sc1, top1))
        if last:
            both(weigh(i, slot, 1, sc1, top1))
        else:
            filled(i + 1, ahead)
            both(weigh(i, slot, 1, sc1, top1), scores(ahead, 0, sc0, top0))
        result(i).start()

    fill(0, 0)
    if count > 1:
        fill(1, 1)
    filled(0, 0)
    both(scores(0, 0, sc0, top0))

    def step(i, _):
        head(i, False)
        return 0
    lax.fori_loop(0, count - 1, step, 0)
    head(jnp.int32(count - 1), True)
    for i in range(max(0, count - 2), count):
        result(i).wait()


def attend(name, phase, first, count, *, s, place, q, columns, halos, halo_first=0, state=None, gate=None, prev=None):
    arrays = {f"column{i}": x for i, (x, _) in enumerate(columns)}
    sides = tuple((f"column{i}", low) for i, (_, low) in enumerate(columns))
    arrays["far"], arrays["near"] = halos
    if state is not None:
        arrays["state"] = state
    if gate is not None:
        arrays["gate"] = gate
    if prev is not None:
        arrays["prev"] = prev
    names = tuple(arrays)
    heads = q.shape[3] // HD
    plan = (names, phase == 0, phase == 2, sides, PICKS[phase], halo_first)
    final = phase == 2
    shape = jax.ShapeDtypeStruct(q.shape, q.dtype) if final else jax.ShapeDtypeStruct((heads, 2, ROWS, 3 * HD), jnp.float32)
    aliases = {3 + names.index("prev"): 0} if prev is not None else {}
    return pl.pallas_call(
        functools.partial(attn_kernel, plan, first, count),
        out_shape=shape,
        in_specs=[SMEM, SMEM, ANY] + [VMEM if n == "gate" else ANY for n in names],
        out_specs=ANY,
        input_output_aliases=aliases,
        scratch_shapes=[
            pltpu.VMEM((3, 2, 3, 2, ROWS, HD), jnp.bfloat16),
            pltpu.VMEM((3, 12, 8, 8, HD), jnp.bfloat16),
            pltpu.VMEM((3, ROWS, ROWS), jnp.float32), pltpu.VMEM((3, ROWS, ROWS), jnp.float32),
            pltpu.VMEM((ROWS, HD), jnp.float32), pltpu.VMEM((ROWS, HD), jnp.float32),
            pltpu.VMEM((3, 2, ROWS, 3 * HD), jnp.float32),
            pltpu.VMEM((2, 2, ROWS, 3 * HD), jnp.float32),
            pltpu.VMEM((2, 12, 8, 8, HD), jnp.bfloat16),
            pltpu.SemaphoreType.DMA((3, 2)), pltpu.SemaphoreType.DMA((3,)),
            pltpu.SemaphoreType.DMA((3,)), pltpu.SemaphoreType.DMA((2,))],
        compiler_params=pltpu.CompilerParams(vmem_limit_bytes=60 * 2**20),
        cost_estimate=SMALL,
        name=name,
    )(s, place, q, *arrays.values())


def from_behind(block, distance):
    size = lax.axis_size("lon")
    return lax.ppermute(block, "lon", [((i - distance) % size, i) for i in range(size)])


def pairs(off):
    size = lax.axis_size("tm")
    return [[i + off, (i + off + 1) % size] for i in range(0, size, 2)]


def far_swap(x):
    route = [r for a, b in pairs(1)[:-1] for r in ((a, b), (b, a))]
    return lax.ppermute(x, "tm", route)


def near_swap(x):
    route = [r for a, b in pairs(0) for r in ((a, b), (b, a))]
    return lax.ppermute(x, "tm", route)


LAST = ((0, 3), (3, 3))


def local(query_field, key_field, value_field, tile_offsets, timesteps, gate_weight):
    heads = query_field.shape[3] // HD
    tiles = query_field.shape[0] // TT
    tm, size = lax.axis_index("tm"), lax.axis_size("tm")
    core = tm % 2
    cut = ((tm == 0) | (tm == size - 1)).astype(jnp.int32)
    shifts = tile_offsets[:, 0]
    mine = jnp.where(core == 0, shifts, shifts[::-1])
    place = jnp.stack([core, cut, far_swap(mine[:1])[0], near_swap(mine[1:])[0]])

    x = split(key_field, value_field)
    r1, l1 = from_behind(x, 1), from_behind(x, -1)

    half_freq = FREQ // 2
    frequencies = jnp.exp(-math.log(10000.0) * jnp.arange(half_freq, dtype=jnp.float32) / half_freq)
    angles = timesteps.astype(jnp.float32)[:, None] * frequencies[None, :]
    embedding = jnp.concatenate([jnp.cos(angles), jnp.sin(angles)], axis=1)
    gate_rows = jnp.dot(
        embedding, gate_weight, precision=lax.Precision.HIGHEST, preferred_element_type=jnp.float32
    ).reshape(tiles, heads, HD)

    attn = functools.partial(attend, s=tile_offsets, place=place, q=query_field)
    whole = ((0, heads),)

    (far,), (near,) = pack("edges0", 0, place, [x], whole)
    state = attn("own", 0, 0, heads, columns=[(x, 0)], halos=(far_swap(far), near_swap(near)))

    ra, la, state = lax.optimization_barrier((r1, l1, state))
    r2, l2 = from_behind(ra, 1), from_behind(la, -1)

    (far,), (near,) = pack("edges1", 1, place, [ra, la], whole)
    state = attn("next", 1, 0, heads, columns=[(r1, 0), (l1, 0)], halos=(far_swap(far), near_swap(near)), state=state)

    r2, l2, state = lax.optimization_barrier((r2, l2, state))
    fars, nears = pack("edges2", 2, place, [r2, l2, l1], LAST)
    out = None
    for (a, n), far, near in zip(LAST, fars, nears):
        out = attn(f"last_{a}", 2, a, n, columns=[(r2, 0), (l2, 0), (l1, 0)], halos=(far_swap(far), near_swap(near)),
                   halo_first=a, state=state, gate=gate_rows, prev=out)
    return out


def solution(mesh):
    return jax.shard_map(
        local,
        mesh=mesh,
        in_specs=(
            P("tm", None, "lon", "head"),
            P("tm", None, "lon", "head"),
            P("tm", None, "lon", "head"),
            P("tm", "lon"),
            P("tm"),
            P(None, "head"),
        ),
        out_specs=P("tm", None, "lon", "head"),
        check_vma=False,
    )
```

time: 216 us -> 163 us (0.75)
  waiting for transfers between devices: 77.9 us -> 56.7 us
  between operations: 13.7 us -> 0.37 us
  Pallas kernels: 73 us -> 62.6 us
  local copies, waits for them, and re-layouts: 13.9 us -> 5.33 us
    ppermute x10 -> x4, waiting for transfers between devices: 53.7 us -> 22.8 us  [from_behind(): lax.ppermute(block, 'lon', [((i - distance) % size, i) for i in range(siz...]
    ppermute x4 -> x5, waiting for transfers between devices: 6.86 us -> 34 us  [far_swap(): return lax.ppermute(x, 'tm', route)]
    all_gather x1 -> x0, waiting for transfers between devices: 17.3 us -> none  [far_gather(): return lax.all_gather(x, 'tm', axis_index_groups=pairs(1))]
    ppermute x4 -> x5, starting transfers between devices: 11.3 us -> 19.9 us  [far_swap(): return lax.ppermute(x, 'tm', route)]
    pallas_call x6 -> x4, Pallas kernels: 22.2 us -> 14.7 us  [the longest x3 11.2 us: pack(): pl.pallas_call(functools.partial(pack_kernel, cuts, PICKS[phase]), out_sh...]
    slice x4 -> x1, local copies, waits for them, and re-layouts: 6.96 us -> 0.62 us  [local(): mine[:1]]
    ppermute x10 -> x4, starting transfers between devices: 17.7 us -> 13.2 us  [from_behind(): lax.ppermute(block, 'lon', [((i - distance) % size, i) for i in range(siz...]
    ppermute x5, starting transfers between devices: 4.49 us -> 1.3 us  [near_swap(): return lax.ppermute(x, 'tm', route)]
  transfers between devices with their start and end apart: 20 -> 14, of which waited for: 7 -> 7; matrix products, arithmetic and copies ran while one was open for 4% -> 3% of each run, Pallas kernels for 25% -> 28%
where the time goes in v2:
time: 163 us; the launch traced here: 162 us
  Pallas kernels  62.6 us (38%)
  waiting for transfers between devices  56.7 us (35%)
  starting transfers between devices  34.4 us (21%)
  local copies, waits for them, and re-layouts  5.33 us (3%)
  other arithmetic  1.99 us (1%)
    pallas_call x4, Pallas kernels, attend(): pl.pallas_call(functools.partial(attn_kernel, plan, first, count), out_sh...  47.9 us
    ppermute x5, waiting for transfers between devices, far_swap(): return lax.ppermute(x, 'tm', route)  34 us
    ppermute x4, waiting for transfers between devices, from_behind(): lax.ppermute(block, 'lon', [((i - distance) % size, i) for i in range(siz...  22.8 us
    ppermute x5, starting transfers between devices, far_swap(): return lax.ppermute(x, 'tm', route)  19.9 us
    ppermute x4, starting transfers between devices, from_behind(): lax.ppermute(block, 'lon', [((i - distance) % size, i) for i in range(siz...  13.2 us
    pallas_call x3, Pallas kernels, pack(): pl.pallas_call(functools.partial(pack_kernel, cuts, PICKS[phase]), out_sh...  11.2 us
    unnamed x17, local copies, waits for them, and re-layouts  3.98 us
    pallas_call x1, Pallas kernels, split(): pl.pallas_call(split_kernel, out_shape=jax.ShapeDtypeStruct((n, 2, 2, TT,...  3.49 us
  transfers between devices with their start and end apart: 14, of which 7 were waited for; matrix products, arithmetic and copies ran while one was open for 3% of the time, Pallas kernels for 28%

profile of v2, /device:TPU:17, one launch (start us, length us, event | category | flops | bytes accessed | tf_op | source)
XLA Modules:
  0.0 161.9 jit_solution(12522474460756359152)
XLA Ops:
  0.0 3.5 %split.1 = bf16[6,2,2,6,8,8,128]{6,5,4,3,2,1,0:T(8,128)(2,1)} custom-call(bf16[12,8,8,768]{3,2,1,0:T(8,128)(2,1)} %k_ref.1, bf16[12,8,8,768]{3,2,1,0:T(8,128)(2,1)} %v_ref.1), custom_call_target="tpu_custom_call" | custom-call | bytes 1024 | tf_op jit(solution)/shard_map/split/pallas_call | solution.py:45
  3.5 8.1 %collective-permute-start.3 = (bf16[6,2,2,384,128]{4,3,2,1,0:T(8,128)(2,1)}, bf16[6,2,2,384,128]{4,3,2,1,0:T(8,128)(2,1)S(1)}, u32[]{:S(2)}, u32[]{:S(2)}) collective-permute-start(bf16[6,2,2,384,128]{4,3,2,1,0:T(8,128)(2,1)} %bitcast.6), channel_id=1, source_target_pairs={{2,0},{4,2},{6,4},{8,6},{10,8},{12,10},{14,12},{16,14},{18,16},{20... | collective-permute-start | bytes 7077896 | tf_op jit(solution)/shard_map/ppermute | solution.py:259
  11.7 0.6 fusion.5
  12.3 3.7 %collective-permute-start = (s32[1]{0:T(128)}, s32[1]{0:T(128)}, u32[]{:S(2)}, u32[]{:S(2)}) collective-permute-start(s32[1]{0:T(128)} %get-tuple-element.35), channel_id=1, source_target_pairs={{32,64},{64,32},{96,128},{128,96},{160,192},{192,160},{33,65},{65,... | collective-permute-start | bytes 20 | tf_op jit(solution)/shard_map/ppermute | solution.py:269
  16.2 1.6 collective-permute-done
  17.8 1.9 %pad_add_fusion.place_ref = s32[4]{0:T(128)} fusion(s32[1]{0:T(128)} %collective-permute-done.1, s32[1]{0:T(128)} %collective-permute-done, s32[1]{0:T(128)} %bitcast.1, s32[1]{0:T(128)} %bitcast), kind=kLoop, calls=%fused_computation.7 | loop fusion | flops 12 | bytes 32 | tf_op jit(solution)/shard_map/stack | solution.py:288
  19.7 3.7 %edges0.1 = (bf16[6,2,384,128]{3,2,1,0:T(8,128)(2,1)}, bf16[6,2,384,128]{3,2,1,0:T(8,128)(2,1)}) custom-call(s32[4]{0:T(128)} %pad_add_fusion.place_ref, bf16[6,2,2,384,128]{4,3,2,1,0:T(8,128)(2,1)} %bitcast.8), custom_call_target="tpu_custom_call" | custom-call | bytes 1024 | tf_op jit(solution)/shard_map/edges0/pallas_call | solution.py:75
  23.4 3.3 %collective-permute-start.4 = (bf16[6,2,384,128]{3,2,1,0:T(8,128)(2,1)}, bf16[6,2,384,128]{3,2,1,0:T(8,128)(2,1)}, u32[]{:S(2)}, u32[]{:S(2)}) collective-permute-start(bf16[6,2,384,128]{3,2,1,0:T(8,128)(2,1)} %get-tuple-element.19), channel_id=1, source_target_pairs={{32,64},{64,32},{96,128},{128,96},{160,192},{192,160},{33,65},{65,... | collective-permute-start | bytes 3538952 | tf_op jit(solution)/shard_map/ppermute | solution.py:269
  26.8 0.6 copy.15.s_ref
  27.4 14.1 %collective-permute-done.4.refs_1_ = bf16[6,2,384,128]{3,2,1,0:T(8,128)(2,1)} collective-permute-done((bf16[6,2,384,128]{3,2,1,0:T(8,128)(2,1)}, bf16[6,2,384,128]{3,2,1,0:T(8,128)(2,1)}, u32[]{:S(2)}, u32[]{:S(2)}) %collective-permute-start.4) | collective-permute-done | bytes 1179680 | tf_op jit(solution)/shard_map/ppermute | solution.py:269
  41.6 14.5 %own.1.refs_4_ = f32[6,2,384,384]{3,2,1,0:T(8,128)} custom-call(s32[2,1]{1,0:T(2,128)} %copy.15.s_ref, s32[4]{0:T(128)} %pad_add_fusion.place_ref, bf16[12,8,8,768]{3,2,1,0:T(8,128)(2,1)} %q_ref.7, bf16[6,2,2,384,128]{4,3,2,1,0:T(8,128)(2,1)} %bitcast.9, bf16[6,2,384,128]{3,2,1,0:T(8,128)(2,1)} %collective-permute-done.4.refs_1_, ...), custom_call_target="tpu_custom_call" | custom-call | bytes 1024 | tf_op jit(solution)/shard_map/own/pallas_call | solution.py:235
  56.1 5.8 %collective-permute-done.3.refs_1_.refs_2_ = bf16[6,2,2,384,128]{4,3,2,1,0:T(8,128)(2,1)S(1)} collective-permute-done((bf16[6,2,2,384,128]{4,3,2,1,0:T(8,128)(2,1)}, bf16[6,2,2,384,128]{4,3,2,1,0:T(8,128)(2,1)S(1)}, u32[]{:S(2)}, u32[]{:S(2)}) %collective-permute-start.3) | collective-permute-done | bytes 2359328 | tf_op jit(solution)/shard_map/ppermute | solution.py:259
  61.9 5.5 %collective-permute-done.2.refs_0_ = bf16[6,2,2,384,128]{4,3,2,1,0:T(8,128)(2,1)} collective-permute-done((bf16[6,2,2,384,128]{4,3,2,1,0:T(8,128)(2,1)}, bf16[6,2,2,384,128]{4,3,2,1,0:T(8,128)(2,1)}, u32[]{:S(2)}, u32[]{:S(2)}) %collective-permute-start.2) | collective-permute-done | bytes 2359328 | tf_op jit(solution)/shard_map/ppermute | solution.py:259
  67.3 5.1 %collective-permute-start.7 = (bf16[6,2,2,384,128]{4,3,2,1,0:T(8,128)(2,1)S(1)}, bf16[6,2,2,384,128]{4,3,2,1,0:T(8,128)(2,1)}, u32[]{:S(2)}, u32[]{:S(2)}) collective-permute-start(bf16[6,2,2,384,128]{4,3,2,1,0:T(8,128)(2,1)S(1)} %collective-permute-done.3.refs_1_.refs_2_), channel_id=1, source_target_pairs={{2,0},{4,2},{6,4},{8,6},{10,8},{12,10},{14,12},{16,14},{18,16},{20... | collective-permute-start | bytes 7077896 | tf_op jit(solution)/shard_map/ppermute | solution.py:259
  72.4 3.8 %edges1.1 = (bf16[6,2,384,128]{3,2,1,0:T(8,128)(2,1)}, bf16[6,2,384,128]{3,2,1,0:T(8,128)(2,1)}) custom-call(s32[4]{0:T(128)} %pad_add_fusion.place_ref, bf16[6,2,2,384,128]{4,3,2,1,0:T(8,128)(2,1)} %collective-permute-done.2.refs_0_, bf16[6,2,2,384,128]{4,3,2,1,0:T(8,128)(2,1)} %copy-done.1), custom_call_target="tpu_custom_call" | custom-call | bytes 1024 | tf_op jit(solution)/shard_map/edges1/pallas_call | solution.py:75
  76.2 5.2 %collective-permute-start.8 = (bf16[6,2,384,128]{3,2,1,0:T(8,128)(2,1)}, bf16[6,2,384,128]{3,2,1,0:T(8,128)(2,1)}, u32[]{:S(2)}, u32[]{:S(2)}) collective-permute-start(bf16[6,2,384,128]{3,2,1,0:T(8,128)(2,1)} %get-tuple-element.23), channel_id=1, source_target_pairs={{32,64},{64,32},{96,128},{128,96},{160,192},{192,160},{33,65},{65,... | collective-permute-start | bytes 3538952 | tf_op jit(solution)/shard_map/ppermute | solution.py:269
  81.5 14.4 %collective-permute-done.8.refs_2_ = bf16[6,2,384,128]{3,2,1,0:T(8,128)(2,1)} collective-permute-done((bf16[6,2,384,128]{3,2,1,0:T(8,128)(2,1)}, bf16[6,2,384,128]{3,2,1,0:T(8,128)(2,1)}, u32[]{:S(2)}, u32[]{:S(2)}) %collective-permute-start.8) | collective-permute-done | bytes 1179680 | tf_op jit(solution)/shard_map/ppermute | solution.py:269
  95.9 14.7 %next.1.refs_5_ = f32[6,2,384,384]{3,2,1,0:T(8,128)} custom-call(s32[2,1]{1,0:T(2,128)} %copy.15.s_ref, s32[4]{0:T(128)} %pad_add_fusion.place_ref, bf16[12,8,8,768]{3,2,1,0:T(8,128)(2,1)} %q_ref.7, bf16[6,2,2,384,128]{4,3,2,1,0:T(8,128)(2,1)} %collective-permute-done.2.refs_0_, bf16[6,2,2,384,128]{4,3,2,1,0:T(8,128)(2,1)} %copy-done.1, ...), custom_call_target="tpu_custom_call" | custom-call | bytes 1024 | tf_op jit(solution)/shard_map/next/pallas_call | solution.py:235
  110.7 11.5 %collective-permute-done.6.refs_0_ = bf16[6,2,2,384,128]{4,3,2,1,0:T(8,128)(2,1)} collective-permute-done((bf16[6,2,2,384,128]{4,3,2,1,0:T(8,128)(2,1)}, bf16[6,2,2,384,128]{4,3,2,1,0:T(8,128)(2,1)}, u32[]{:S(2)}, u32[]{:S(2)}) %collective-permute-start.6) | collective-permute-done | bytes 2359328 | tf_op jit(solution)/shard_map/ppermute | solution.py:259
  122.2 3.7 %edges2.1 = (bf16[3,2,384,128]{3,2,1,0:T(8,128)(2,1)}, bf16[3,2,384,128]{3,2,1,0:T(8,128)(2,1)}, bf16[3,2,384,128]{3,2,1,0:T(8,128)(2,1)}, bf16[3,2,384,128]{3,2,1,0:T(8,128)(2,1)}) custom-call(s32[4]{0:T(128)} %pad_add_fusion.place_ref, bf16[6,2,2,384,128]{4,3,2,1,0:T(8,128)(2,1)} %collective-permute-done.6.refs_0_, ...), custom_call_target="tpu_custom_call" | custom-call | bytes 1024 | tf_op jit(solution)/shard_map/edges2/pallas_call | solution.py:75
  125.9 5.8 %collective-permute-start.12 = (bf16[3,2,384,128]{3,2,1,0:T(8,128)(2,1)}, bf16[3,2,384,128]{3,2,1,0:T(8,128)(2,1)S(1)}, u32[]{:S(2)}, u32[]{:S(2)}) collective-permute-start(bf16[3,2,384,128]{3,2,1,0:T(8,128)(2,1)} %get-tuple-element.31), channel_id=1, source_target_pairs={{32,64},{64,32},{96,128},{128,96},{160,192},{192,160},{33,65},{65,... | collective-permute-start | bytes 1769480 | tf_op jit(solution)/shard_map/ppermute | solution.py:269
  131.8 1.9 %collective-permute-start.10 = (bf16[3,2,384,128]{3,2,1,0:T(8,128)(2,1)}, bf16[3,2,384,128]{3,2,1,0:T(8,128)(2,1)S(1)}, u32[]{:S(2)}, u32[]{:S(2)}) collective-permute-start(bf16[3,2,384,128]{3,2,1,0:T(8,128)(2,1)} %get-tuple-element.28), channel_id=1, source_target_pairs={{32,64},{64,32},{96,128},{128,96},{160,192},{192,160},{33,65},{65,... | collective-permute-start | bytes 1769480 | tf_op jit(solution)/shard_map/ppermute | solution.py:269
  133.7 0.9 collective-permute-start.11
  134.8 0.5 fusion
  135.2 0.6 reshape.13.refs_6_
  135.9 3.9 %collective-permute-done.12.refs_3_ = bf16[3,2,384,128]{3,2,1,0:T(8,128)(2,1)S(1)} collective-permute-done((bf16[3,2,384,128]{3,2,1,0:T(8,128)(2,1)}, bf16[3,2,384,128]{3,2,1,0:T(8,128)(2,1)S(1)}, u32[]{:S(2)}, u32[]{:S(2)}) %collective-permute-start.12) | collective-permute-done | bytes 589856 | tf_op jit(solution)/shard_map/ppermute | solution.py:269
  139.7 0.8 copy-done.2
  140.6 0.9 copy-done.3
  141.4 9.3 %last_0.1.refs_7_ = bf16[12,8,8,768]{3,2,1,0:T(8,128)(2,1)} custom-call(s32[2,1]{1,0:T(2,128)} %copy.15.s_ref, s32[4]{0:T(128)} %pad_add_fusion.place_ref, bf16[12,8,8,768]{3,2,1,0:T(8,128)(2,1)} %q_ref.7, bf16[6,2,2,384,128]{4,3,2,1,0:T(8,128)(2,1)} %collective-permute-done.6.refs_0_, bf16[6,2,2,384,128]{4,3,2,1,0:T(8,128)(2,1)} %collective-permute-done.7.refs_1_, ...), custom_call_target="tpu_custom_call" | custom-call | bytes 1024 | tf_op jit(solution)/shard_map/last_0/pallas_call | solution.py:235
  150.8 0.8 copy-done.4
  151.6 0.9 copy-done.5
  152.5 9.3 %last_3.1 = bf16[12,8,8,768]{3,2,1,0:T(8,128)(2,1)} custom-call(s32[2,1]{1,0:T(2,128)} %copy.15.s_ref, s32[4]{0:T(128)} %pad_add_fusion.place_ref, bf16[12,8,8,768]{3,2,1,0:T(8,128)(2,1)} %q_ref.7, bf16[6,2,2,384,128]{4,3,2,1,0:T(8,128)(2,1)} %collective-permute-done.6.refs_0_, ...), custom_call_target="tpu_custom_call", output_to_operand_aliasing={{}: (10, {})} | custom-call | bytes 1024 | tf_op jit(solution)/shard_map/last_3/pallas_call | solution.py:235
  (30 shorter events, 0.6 us)
Async XLA Ops:
  0.0 134.8 %copy-start = (f32[256,768]{1,0:T(8,128)S(1)}, f32[256,768]{1,0:T(8,128)}, u32[]{:S(2)}) copy-start(f32[256,768]{1,0:T(8,128)} %param.11) | copy-start | bytes 2359300
  0.0 11.6 %copy-start.6 = (s32[2,1]{0,1:T(1,128)S(1)}, s32[2,1]{0,1:T(1,128)}, u32[]{:S(2)}) copy-start(s32[2,1]{0,1:T(1,128)} %param.9) | copy-start | bytes 28
  3.5 58.3 %collective-permute-start.3 = (bf16[6,2,2,384,128]{4,3,2,1,0:T(8,128)(2,1)}, bf16[6,2,2,384,128]{4,3,2,1,0:T(8,128)(2,1)S(1)}, u32[]{:S(2)}, u32[]{:S(2)}) collective-permute-start(bf16[6,2,2,384,128]{4,3,2,1,0:T(8,128)(2,1)} %bitcast.6), channel_id=1, source_target_pairs={{2,0},{4,2},{6,4},{8,6},{10,8},{12,10},{14,12},{16,14},{18,16},{20... | collective-permute-start | bytes 7077896 | tf_op jit(solution)/shard_map/ppermute | solution.py:259
  11.6 55.7 %collective-permute-start.2 = (bf16[6,2,2,384,128]{4,3,2,1,0:T(8,128)(2,1)}, bf16[6,2,2,384,128]{4,3,2,1,0:T(8,128)(2,1)}, u32[]{:S(2)}, u32[]{:S(2)}) collective-permute-start(bf16[6,2,2,384,128]{4,3,2,1,0:T(8,128)(2,1)} %bitcast.7), channel_id=1, source_target_pairs={{30,0},{0,2},{2,4},{4,6},{6,8},{8,10},{10,12},{12,14},{14,16},{16,... | collective-permute-start | bytes 7077896 | tf_op jit(solution)/shard_map/ppermute | solution.py:259
  12.3 5.5 %collective-permute-start = (s32[1]{0:T(128)}, s32[1]{0:T(128)}, u32[]{:S(2)}, u32[]{:S(2)}) collective-permute-start(s32[1]{0:T(128)} %get-tuple-element.35), channel_id=1, source_target_pairs={{32,64},{64,32},{96,128},{128,96},{160,192},{192,160},{33,65},{65,... | collective-permute-start | bytes 20 | tf_op jit(solution)/shard_map/ppermute | solution.py:269
  16.1 1.7 %collective-permute-start.1 = (s32[1]{0:T(128)}, s32[1]{0:T(128)}, u32[]{:S(2)}, u32[]{:S(2)}) collective-permute-start(s32[1]{0:T(128)} %get-tuple-element.36), channel_id=1, source_target_pairs={{0,32},{32,0},{64,96},{96,64},{128,160},{160,128},{192,224},{224,1... | collective-permute-start | bytes 20 | tf_op jit(solution)/shard_map/ppermute | solution.py:274
  23.4 18.1 %collective-permute-start.4 = (bf16[6,2,384,128]{3,2,1,0:T(8,128)(2,1)}, bf16[6,2,384,128]{3,2,1,0:T(8,128)(2,1)}, u32[]{:S(2)}, u32[]{:S(2)}) collective-permute-start(bf16[6,2,384,128]{3,2,1,0:T(8,128)(2,1)} %get-tuple-element.19), channel_id=1, source_target_pairs={{32,64},{64,32},{96,128},{128,96},{160,192},{192,160},{33,65},{65,... | collective-permute-start | bytes 3538952 | tf_op jit(solution)/shard_map/ppermute | solution.py:269
  26.7 14.8 %collective-permute-start.5 = (bf16[6,2,384,128]{3,2,1,0:T(8,128)(2,1)}, bf16[6,2,384,128]{3,2,1,0:T(8,128)(2,1)}, u32[]{:S(2)}, u32[]{:S(2)}) collective-permute-start(bf16[6,2,384,128]{3,2,1,0:T(8,128)(2,1)} %get-tuple-element.20), channel_id=1, source_target_pairs={{0,32},{32,0},{64,96},{96,64},{128,160},{160,128},{192,224},{224,1... | collective-permute-start | bytes 3538952 | tf_op jit(solution)/shard_map/ppermute | solution.py:274
  61.8 10.6 %copy-start.1 = (bf16[6,2,2,384,128]{4,3,2,1,0:T(8,128)(2,1)}, bf16[6,2,2,384,128]{4,3,2,1,0:T(8,128)(2,1)S(1)}, u32[]{:S(2)}) copy-start(bf16[6,2,2,384,128]{4,3,2,1,0:T(8,128)(2,1)S(1)} %collective-permute-done.3.refs_1_.refs_2_) | copy-start | bytes 7077892
  67.3 54.8 %collective-permute-start.6 = (bf16[6,2,2,384,128]{4,3,2,1,0:T(8,128)(2,1)}, bf16[6,2,2,384,128]{4,3,2,1,0:T(8,128)(2,1)}, u32[]{:S(2)}, u32[]{:S(2)}) collective-permute-start(bf16[6,2,2,384,128]{4,3,2,1,0:T(8,128)(2,1)} %collective-permute-done.2.refs_0_), channel_id=1, source_target_pairs={{30,0},{0,2},{2,4},{4,6},{6,8},{8,10},{10,12},{12,14},{14,16},{16,... | collective-permute-start | bytes 7077896 | tf_op jit(solution)/shard_map/ppermute | solution.py:259
  67.3 54.8 %collective-permute-start.7 = (bf16[6,2,2,384,128]{4,3,2,1,0:T(8,128)(2,1)S(1)}, bf16[6,2,2,384,128]{4,3,2,1,0:T(8,128)(2,1)}, u32[]{:S(2)}, u32[]{:S(2)}) collective-permute-start(bf16[6,2,2,384,128]{4,3,2,1,0:T(8,128)(2,1)S(1)} %collective-permute-done.3.refs_1_.refs_2_), channel_id=1, source_target_pairs={{2,0},{4,2},{6,4},{8,6},{10,8},{12,10},{14,12},{16,14},{18,16},{20... | collective-permute-start | bytes 7077896 | tf_op jit(solution)/shard_map/ppermute | solution.py:259
  76.2 19.7 %collective-permute-start.8 = (bf16[6,2,384,128]{3,2,1,0:T(8,128)(2,1)}, bf16[6,2,384,128]{3,2,1,0:T(8,128)(2,1)}, u32[]{:S(2)}, u32[]{:S(2)}) collective-permute-start(bf16[6,2,384,128]{3,2,1,0:T(8,128)(2,1)} %get-tuple-element.23), channel_id=1, source_target_pairs={{32,64},{64,32},{96,128},{128,96},{160,192},{192,160},{33,65},{65,... | collective-permute-start | bytes 3538952 | tf_op jit(solution)/shard_map/ppermute | solution.py:269
  81.4 14.5 %collective-permute-start.9 = (bf16[6,2,384,128]{3,2,1,0:T(8,128)(2,1)}, bf16[6,2,384,128]{3,2,1,0:T(8,128)(2,1)}, u32[]{:S(2)}, u32[]{:S(2)}) collective-permute-start(bf16[6,2,384,128]{3,2,1,0:T(8,128)(2,1)} %get-tuple-element.24), channel_id=1, source_target_pairs={{0,32},{32,0},{64,96},{96,64},{128,160},{160,128},{192,224},{224,1... | collective-permute-start | bytes 3538952 | tf_op jit(solution)/shard_map/ppermute | solution.py:274
  110.6 24.0 %copy-start.7 = (s32[2]{0:T(128)S(1)}, s32[2]{0:T(128)}, u32[]{:S(2)}) copy-start(s32[2]{0:T(128)} %param.10) | copy-start | bytes 28
  125.9 13.8 %collective-permute-start.12 = (bf16[3,2,384,128]{3,2,1,0:T(8,128)(2,1)}, bf16[3,2,384,128]{3,2,1,0:T(8,128)(2,1)S(1)}, u32[]{:S(2)}, u32[]{:S(2)}) collective-permute-start(bf16[3,2,384,128]{3,2,1,0:T(8,128)(2,1)} %get-tuple-element.31), channel_id=1, source_target_pairs={{32,64},{64,32},{96,128},{128,96},{160,192},{192,160},{33,65},{65,... | collective-permute-start | bytes 1769480 | tf_op jit(solution)/shard_map/ppermute | solution.py:269
  131.7 8.1 %collective-permute-start.13 = (bf16[3,2,384,128]{3,2,1,0:T(8,128)(2,1)}, bf16[3,2,384,128]{3,2,1,0:T(8,128)(2,1)S(1)}, u32[]{:S(2)}, u32[]{:S(2)}) collective-permute-start(bf16[3,2,384,128]{3,2,1,0:T(8,128)(2,1)} %get-tuple-element.32), channel_id=1, source_target_pairs={{0,32},{32,0},{64,96},{96,64},{128,160},{160,128},{192,224},{224,1... | collective-permute-start | bytes 1769480 | tf_op jit(solution)/shard_map/ppermute | solution.py:274
  131.8 19.0 %collective-permute-start.10 = (bf16[3,2,384,128]{3,2,1,0:T(8,128)(2,1)}, bf16[3,2,384,128]{3,2,1,0:T(8,128)(2,1)S(1)}, u32[]{:S(2)}, u32[]{:S(2)}) collective-permute-start(bf16[3,2,384,128]{3,2,1,0:T(8,128)(2,1)} %get-tuple-element.28), channel_id=1, source_target_pairs={{32,64},{64,32},{96,128},{128,96},{160,192},{192,160},{33,65},{65,... | collective-permute-start | bytes 1769480 | tf_op jit(solution)/shard_map/ppermute | solution.py:269
  133.7 17.1 %collective-permute-start.11 = (bf16[3,2,384,128]{3,2,1,0:T(8,128)(2,1)}, bf16[3,2,384,128]{3,2,1,0:T(8,128)(2,1)S(1)}, u32[]{:S(2)}, u32[]{:S(2)}) collective-permute-start(bf16[3,2,384,128]{3,2,1,0:T(8,128)(2,1)} %get-tuple-element.29), channel_id=1, source_target_pairs={{0,32},{32,0},{64,96},{96,64},{128,160},{160,128},{192,224},{224,1... | collective-permute-start | bytes 1769480 | tf_op jit(solution)/shard_map/ppermute | solution.py:274
  139.7 0.8 copy-start.2
  140.6 0.9 copy-start.3
  150.8 0.8 copy-start.4
  151.6 0.9 copy-start.5

commit v3 on v2

--- a/solution.py
+++ b/solution.py
@@ -23,70 +23,76 @@
 PICKS = (lambda s: 0 * s, lambda s: jnp.where(s > 0, 1, 0), lambda s: jnp.where(s == 0, 2, jnp.where(s > 0, 1, 0)))
 
 
-def run_copies(copies):
+def split_kernel(place_ref, k_ref, v_ref, far, near, hold, into, out_of):
+    core = place_ref[0]
+    count = far.shape[0]
+    copies, last = [], []
+    for w, out in enumerate((far, near)):
+        first = (core if w == 0 else 1 - core) * TT
+        for i in range(count):
+            for which, ref in enumerate((k_ref, v_ref)):
+                source = ref.at[pl.ds(first, TT), :, :, pl.ds(i * HD, HD)]
+                copies.append(pltpu.make_async_copy(source, hold.at[w, i, which], into.at[w, i, which]))
+            last.append(pltpu.make_async_copy(hold.at[w, i], out.at[i], out_of.at[w, i]))
     for copy in copies:
         copy.start()
-    for copy in copies:
+    for n, copy in enumerate(last):
+        copies[2 * n].wait()
+        copies[2 * n + 1].wait()
+        copy.start()
+    for copy in last:
         copy.wait()
 
 
-def split_kernel(k_ref, v_ref, out, sem):
-    copies = []
-    for t in range(2):
-        for i in range(out.shape[0]):
-            for which, ref in enumerate((k_ref, v_ref)):
-                source = ref.at[pl.ds(t * TT, TT), :, :, pl.ds(i * HD, HD)]
-                copies.append(pltpu.make_async_copy(source, out.at[i, t, which], sem.at[len(copies)]))
-    run_copies(copies)
-
-
-def split(k, v):
+def split(place, k, v):
     n = k.shape[3] // HD
-    x = pl.pallas_call(
+    shape = jax.ShapeDtypeStruct((n, 2, TT, 8, 8, HD), k.dtype)
+    parts = pl.pallas_call(
         split_kernel,
-        out_shape=jax.ShapeDtypeStruct((n, 2, 2, TT, 8, 8, HD), k.dtype),
-        in_specs=[ANY, ANY],
-        out_specs=VMEM,
-        scratch_shapes=[pltpu.SemaphoreType.DMA((4 * n,))],
+        out_shape=[shape, shape],
+        in_specs=[SMEM, ANY, ANY],
+        out_specs=[ANY, ANY],
+        scratch_shapes=[pltpu.VMEM((2,) + shape.shape, k.dtype), pltpu.SemaphoreType.DMA((2, n, 2)), pltpu.SemaphoreType.DMA((2, n))],
         cost_estimate=SMALL,
         compiler_params=pltpu.CompilerParams(vmem_limit_bytes=60 * 2**20),
         name="split",
-    )(k, v)
-    return x.reshape(x.shape[:3] + (ROWS, HD))
-
-
-def pack_kernel(cuts, pick, place_ref, *refs):
-    n = len(refs) - 2 * len(cuts) - 1
-    ins, far, near, sem = refs[:n], refs[n:n + len(cuts)], refs[n + len(cuts):-1], refs[-1]
-    core = place_ref[0]
-    for w, (outs, tile, side) in enumerate(((far, core, pick(place_ref[2])), (near, 1 - core, pick(place_ref[3])))):
-        for c, ref in enumerate(ins):
-            @pl.when(side == c)
-            def _():
-                for i, (out, (first, count)) in enumerate(zip(outs, cuts)):
-                    pltpu.make_async_copy(ref.at[pl.ds(first, count), tile], out, sem.at[w, i]).start()
-    for w, outs in enumerate((far, near)):
-        for i, out in enumerate(outs):
-            pltpu.make_async_copy(out, out, sem.at[w, i]).wait()
-
-
-def pack(name, phase, place, xs, cuts):
-    shapes = [jax.ShapeDtypeStruct((count,) + xs[0].shape[2:], xs[0].dtype) for _, count in cuts]
-    outs = pl.pallas_call(
-        functools.partial(pack_kernel, cuts, PICKS[phase]),
-        out_shape=shapes + shapes,
+    )(place, k, v)
+    return [x.reshape(x.shape[:2] + (ROWS, HD)) for x in parts]
+
+
+def choose_kernel(pick, slot, place_ref, *refs):
+    ins, (out, hold, into, out_of) = refs[:-4], refs[-4:]
+    side = pick(place_ref[slot])
+    count = out.shape[0]
+    for c, ref in enumerate(ins):
+        @pl.when(side == c)
+        def _():
+            for i in range(count):
+                pltpu.make_async_copy(ref.at[i], hold.at[i], into.at[i]).start()
+    last = [pltpu.make_async_copy(hold.at[i], out.at[i], out_of.at[i]) for i in range(count)]
+    for i, copy in enumerate(last):
+        pltpu.make_async_copy(hold.at[i], hold.at[i], into.at[i]).wait()
+        copy.start()
+    for copy in last:
+        copy.wait()
+
+
+def choose(name, phase, slot, place, xs):
+    x = xs[0]
+    return pl.pallas_call(
+        functools.partial(choose_kernel, PICKS[phase], slot),
+        out_shape=jax.ShapeDtypeStruct(x.shape, x.dtype),
         in_specs=[SMEM] + [ANY] * len(xs),
-        out_specs=[VMEM] * (2 * len(cuts)),
-        scratch_shapes=[pltpu.SemaphoreType.DMA((2, len(cuts)))],
+        out_specs=ANY,
+        scratch_shapes=[pltpu.VMEM(x.shape, x.dtype), pltpu.SemaphoreType.DMA(x.shape[:1]), pltpu.SemaphoreType.DMA(x.shape[:1])],
         cost_estimate=SMALL,
         compiler_params=pltpu.CompilerParams(vmem_limit_bytes=60 * 2**20),
         name=name,
     )(place, *xs)
-    return outs[:len(cuts)], outs[len(cuts):]
 
 
 def attn_kernel(plan, first, count, s_ref, place_ref, q_ref, *refs):
-    names, starts, finishes, sides, pick, halo_first = plan
+    names, starts, finishes, sides, pick = plan
     ops = dict(zip(names, refs))
     out_ref, kv, qv, sc0, sc1, top0, top1, si, so, ov, ksem, qsem, isem, osem = refs[len(refs) - 14:]
     core, cut = place_ref[0], place_ref[1]
@@ -96,24 +102,25 @@
         for t in range(2):
             side = pick(s_ref[t, 0])
             halo = kv.at[slot, t, 2 * t]
-            for c, (name, low) in enumerate(sides):
-                own = ops[name].at[h - low]
+            for c in range(sides):
+                far, near = ops[f"far{c}"].at[h], ops[f"near{c}"].at[h]
 
                 @pl.when(side == c)
                 def _():
-                    pltpu.make_async_copy(own, kv.at[slot, t, pl.ds(1 - t, 2)], ksem.at[slot, t]).start()
+                    pltpu.make_async_copy(far, kv.at[slot, t, 1 - t + core], ksem.at[slot, t]).start()
+                    pltpu.make_async_copy(near, kv.at[slot, t, 2 - t - core], ksem.at[slot, t]).start()
 
                 @pl.when((side == c) & (core == t) & (cut != 0))
                 def _():
-                    pltpu.make_async_copy(own.at[t], halo, ksem.at[slot, t]).start()
+                    pltpu.make_async_copy(far, halo, ksem.at[slot, t]).start()
 
             @pl.when((core == t) & (cut == 0))
             def _():
-                pltpu.make_async_copy(ops["far"].at[h - halo_first], halo, ksem.at[slot, t]).start()
+                pltpu.make_async_copy(ops["far"].at[h], halo, ksem.at[slot, t]).start()
 
             @pl.when(core != t)
             def _():
-                pltpu.make_async_copy(ops["near"].at[h - halo_first], halo, ksem.at[slot, t]).start()
+                pltpu.make_async_copy(ops["near"].at[h], halo, ksem.at[slot, t]).start()
         q_copy(i, slot).start()
         if not starts:
             state_in(i, slot).start()
@@ -216,9 +223,10 @@
         result(i).wait()
 
 
-def attend(name, phase, first, count, *, s, place, q, columns, halos, halo_first=0, state=None, gate=None, prev=None):
-    arrays = {f"column{i}": x for i, (x, _) in enumerate(columns)}
-    sides = tuple((f"column{i}", low) for i, (_, low) in enumerate(columns))
+def attend(name, phase, first, count, *, s, place, q, columns, halos, state=None, gate=None, prev=None):
+    arrays, sides = {}, len(columns)
+    for c, (far, near) in enumerate(columns):
+        arrays[f"far{c}"], arrays[f"near{c}"] = far, near
     arrays["far"], arrays["near"] = halos
     if state is not None:
         arrays["state"] = state
@@ -228,7 +236,7 @@
         arrays["prev"] = prev
     names = tuple(arrays)
     heads = q.shape[3] // HD
-    plan = (names, phase == 0, phase == 2, sides, PICKS[phase], halo_first)
+    plan = (names, phase == 0, phase == 2, sides, PICKS[phase])
     final = phase == 2
     shape = jax.ShapeDtypeStruct(q.shape, q.dtype) if final else jax.ShapeDtypeStruct((heads, 2, ROWS, 3 * HD), jnp.float32)
     aliases = {3 + names.index("prev"): 0} if prev is not None else {}
@@ -274,9 +282,6 @@
     return lax.ppermute(x, "tm", route)
 
 
-LAST = ((0, 3), (3, 3))
-
-
 def local(query_field, key_field, value_field, tile_offsets, timesteps, gate_weight):
     heads = query_field.shape[3] // HD
     tiles = query_field.shape[0] // TT
@@ -287,8 +292,11 @@
     mine = jnp.where(core == 0, shifts, shifts[::-1])
     place = jnp.stack([core, cut, far_swap(mine[:1])[0], near_swap(mine[1:])[0]])
 
-    x = split(key_field, value_field)
-    r1, l1 = from_behind(x, 1), from_behind(x, -1)
+    xf, xn = split(jnp.stack([core]), key_field, value_field)
+    rf, lf = from_behind(xf, 1), from_behind(xf, -1)
+    rn, ln = from_behind(xn, 1), from_behind(xn, -1)
+    r2f, l2f = from_behind(rf, 1), from_behind(lf, -1)
+    r2n, l2n = from_behind(rn, 1), from_behind(ln, -1)
 
     half_freq = FREQ // 2
     frequencies = jnp.exp(-math.log(10000.0) * jnp.arange(half_freq, dtype=jnp.float32) / half_freq)
@@ -299,24 +307,19 @@
     ).reshape(tiles, heads, HD)
 
     attn = functools.partial(attend, s=tile_offsets, place=place, q=query_field)
-    whole = ((0, heads),)
-
-    (far,), (near,) = pack("edges0", 0, place, [x], whole)
-    state = attn("own", 0, 0, heads, columns=[(x, 0)], halos=(far_swap(far), near_swap(near)))
-
-    ra, la, state = lax.optimization_barrier((r1, l1, state))
-    r2, l2 = from_behind(ra, 1), from_behind(la, -1)
-
-    (far,), (near,) = pack("edges1", 1, place, [ra, la], whole)
-    state = attn("next", 1, 0, heads, columns=[(r1, 0), (l1, 0)], halos=(far_swap(far), near_swap(near)), state=state)
-
-    r2, l2, state = lax.optimization_barrier((r2, l2, state))
-    fars, nears = pack("edges2", 2, place, [r2, l2, l1], LAST)
-    out = None
-    for (a, n), far, near in zip(LAST, fars, nears):
-        out = attn(f"last_{a}", 2, a, n, columns=[(r2, 0), (l2, 0), (l1, 0)], halos=(far_swap(far), near_swap(near)),
-                   halo_first=a, state=state, gate=gate_rows, prev=out)
-    return out
+    state = attn("own", 0, 0, heads, columns=[(xf, xn)], halos=(far_swap(xf), near_swap(xn)))
+
+    rf_, lf_, rn_, ln_, state = lax.optimization_barrier((rf, lf, rn, ln, state))
+    far = far_swap(choose("far1", 1, 2, place, [rf_, lf_]))
+    near = near_swap(choose("near1", 1, 3, place, [rn_, ln_]))
+    far2 = choose("far2", 2, 2, place, [r2f, l2f, lf])
+    state, far2, gate_rows = lax.optimization_barrier((state, far2, gate_rows))
+    state = attn("next", 1, 0, heads, columns=[(rf, rn), (lf, ln)], halos=(far, near), state=state)
+
+    r2n_, l2n_, state = lax.optimization_barrier((r2n, l2n, state))
+    near2, far2 = lax.optimization_barrier((choose("near2", 2, 3, place, [r2n_, l2n_, ln]), far_swap(far2)))
+    return attn("last", 2, 0, heads, columns=[(r2f, r2n), (l2f, l2n), (lf, ln)], halos=(far2, near_swap(near2)),
+                state=state, gate=gate_rows)
 
 
 def solution(mesh):

time: 163 us -> 142 us (0.87)
  waiting for transfers between devices: 56.7 us -> 39.7 us
  Pallas kernels: 62.6 us -> 58.6 us
    ppermute x5 -> x4, waiting for transfers between devices: 34 us -> 3.38 us  [far_swap(): return lax.ppermute(x, 'tm', route)]
    ppermute x4 -> x8, waiting for transfers between devices: 22.8 us -> 32.6 us  [from_behind(): lax.ppermute(block, 'lon', [((i - distance) % size, i) for i in range(siz...]
    ppermute x4 -> x8, starting transfers between devices: 13.2 us -> 22.8 us  [from_behind(): lax.ppermute(block, 'lon', [((i - distance) % size, i) for i in range(siz...]
    ppermute x5 -> x4, starting transfers between devices: 19.9 us -> 12.1 us  [far_swap(): return lax.ppermute(x, 'tm', route)]
    ppermute x5 -> x4, waiting for transfers between devices: 0.01 us -> 3.77 us  [near_swap(): return lax.ppermute(x, 'tm', route)]
    pallas_call x4 -> x3, Pallas kernels: 47.9 us -> 44.3 us  [attend(): pl.pallas_call(functools.partial(attn_kernel, plan, first, count), out_sh...]
    pallas_call x4 -> x5, Pallas kernels: 14.7 us -> 14.2 us  [the longest x4 11.4 us: choose(): pl.pallas_call(functools.partial(choose_kernel, PICKS[phase], slot), out_...]
  transfers between devices with their start and end apart: 14 -> 16, of which waited for: 7 -> 8; matrix products, arithmetic and copies ran while one was open for 3% -> 3% of each run, Pallas kernels for 28% -> 29%
where the time goes in v3:
time: 142 us; the launch traced here: 141 us
  Pallas kernels  58.6 us (41%)
  waiting for transfers between devices  39.7 us (28%)
  starting transfers between devices  35.9 us (25%)
  local copies, waits for them, and re-layouts  4.11 us (3%)
  other arithmetic  2.08 us (1%)
    pallas_call x3, Pallas kernels, attend(): pl.pallas_call(functools.partial(attn_kernel, plan, first, count), out_sh...  44.3 us
    ppermute x8, waiting for transfers between devices, from_behind(): lax.ppermute(block, 'lon', [((i - distance) % size, i) for i in range(siz...  32.6 us
    ppermute x8, starting transfers between devices, from_behind(): lax.ppermute(block, 'lon', [((i - distance) % size, i) for i in range(siz...  22.8 us
    ppermute x4, starting transfers between devices, far_swap(): return lax.ppermute(x, 'tm', route)  12.1 us
    pallas_call x4, Pallas kernels, choose(): pl.pallas_call(functools.partial(choose_kernel, PICKS[phase], slot), out_...  11.4 us
    ppermute x4, waiting for transfers between devices, near_swap(): return lax.ppermute(x, 'tm', route)  3.77 us
    ppermute x4, waiting for transfers between devices, far_swap(): return lax.ppermute(x, 'tm', route)  3.38 us
  transfers between devices with their start and end apart: 16, of which 8 were waited for; matrix products, arithmetic and copies ran while one was open for 3% of the time, Pallas kernels for 29%

profile of v3, /device:TPU:17, one launch (start us, length us, event | category | flops | bytes accessed | tf_op | source)
XLA Modules:
  0.0 141.2 jit_solution(4599502280864005722)
XLA Ops:
  0.0 2.8 %split.1 = (bf16[6,2,6,8,8,128]{5,4,3,2,1,0:T(8,128)(2,1)}, bf16[6,2,6,8,8,128]{5,4,3,2,1,0:T(8,128)(2,1)}) custom-call(s32[1]{0:T(128)} %bitcast.place_ref, bf16[12,8,8,768]{3,2,1,0:T(8,128)(2,1)} %k_ref.1, bf16[12,8,8,768]{3,2,1,0:T(8,128)(2,1)} %v_ref.1), custom_call_target="tpu_custom_call" | custom-call | bytes 1024 | tf_op jit(solution)/shard_map/split/pallas_call | solution.py:50
  2.8 3.5 %collective-permute-start.10 = (bf16[6,2,384,128]{3,2,1,0:T(8,128)(2,1)}, bf16[6,2,384,128]{3,2,1,0:T(8,128)(2,1)}, u32[]{:S(2)}, u32[]{:S(2)}) collective-permute-start(bf16[6,2,384,128]{3,2,1,0:T(8,128)(2,1)} %bitcast.11), channel_id=1, source_target_pairs={{32,64},{64,32},{96,128},{128,96},{160,192},{192,160},{33,65},{65,... | collective-permute-start | bytes 3538952 | tf_op jit(solution)/shard_map/ppermute | solution.py:277
  6.3 1.7 %collective-permute-start.2 = (bf16[6,2,384,128]{3,2,1,0:T(8,128)(2,1)}, bf16[6,2,384,128]{3,2,1,0:T(8,128)(2,1)}, u32[]{:S(2)}, u32[]{:S(2)}) collective-permute-start(bf16[6,2,384,128]{3,2,1,0:T(8,128)(2,1)} %bitcast.12), channel_id=1, source_target_pairs={{30,0},{0,2},{2,4},{4,6},{6,8},{8,10},{10,12},{12,14},{14,16},{16,... | collective-permute-start | bytes 3538952 | tf_op jit(solution)/shard_map/ppermute | solution.py:267
  8.0 6.5 %collective-permute-start.6 = (bf16[6,2,384,128]{3,2,1,0:T(8,128)(2,1)}, bf16[6,2,384,128]{3,2,1,0:T(8,128)(2,1)S(1)}, u32[]{:S(2)}, u32[]{:S(2)}) collective-permute-start(bf16[6,2,384,128]{3,2,1,0:T(8,128)(2,1)} %bitcast.13), channel_id=1, source_target_pairs={{2,0},{4,2},{6,4},{8,6},{10,8},{12,10},{14,12},{16,14},{18,16},{20... | collective-permute-start | bytes 3538952 | tf_op jit(solution)/shard_map/ppermute | solution.py:267
  14.6 0.6 fusion.5
  15.2 2.4 %collective-permute-start = (s32[1]{0:T(128)}, s32[1]{0:T(128)}, u32[]{:S(2)}, u32[]{:S(2)}) collective-permute-start(s32[1]{0:T(128)} %get-tuple-element.37), channel_id=1, source_target_pairs={{32,64},{64,32},{96,128},{128,96},{160,192},{192,160},{33,65},{65,... | collective-permute-start | bytes 20 | tf_op jit(solution)/shard_map/ppermute | solution.py:277
  17.6 3.4 %collective-permute-done = s32[1]{0:T(128)} collective-permute-done((s32[1]{0:T(128)}, s32[1]{0:T(128)}, u32[]{:S(2)}, u32[]{:S(2)}) %collective-permute-start) | collective-permute-done | bytes 36 | tf_op jit(solution)/shard_map/ppermute | solution.py:277
  21.4 1.0 collective-permute-done.1
  22.4 1.6 %collective-permute-start.4 = (bf16[6,2,384,128]{3,2,1,0:T(8,128)(2,1)}, bf16[6,2,384,128]{3,2,1,0:T(8,128)(2,1)}, u32[]{:S(2)}, u32[]{:S(2)}) collective-permute-start(bf16[6,2,384,128]{3,2,1,0:T(8,128)(2,1)} %bitcast.8), channel_id=1, source_target_pairs={{30,0},{0,2},{2,4},{4,6},{6,8},{8,10},{10,12},{12,14},{14,16},{16,... | collective-permute-start | bytes 3538952 | tf_op jit(solution)/shard_map/ppermute | solution.py:267
  24.0 6.4 %collective-permute-start.8 = (bf16[6,2,384,128]{3,2,1,0:T(8,128)(2,1)}, bf16[6,2,384,128]{3,2,1,0:T(8,128)(2,1)S(1)}, u32[]{:S(2)}, u32[]{:S(2)}) collective-permute-start(bf16[6,2,384,128]{3,2,1,0:T(8,128)(2,1)} %bitcast.9), channel_id=1, source_target_pairs={{2,0},{4,2},{6,4},{8,6},{10,8},{12,10},{14,12},{16,14},{18,16},{20... | collective-permute-start | bytes 3538952 | tf_op jit(solution)/shard_map/ppermute | solution.py:267
  30.4 10.8 %collective-permute-done.2.refs_0_ = bf16[6,2,384,128]{3,2,1,0:T(8,128)(2,1)} collective-permute-done((bf16[6,2,384,128]{3,2,1,0:T(8,128)(2,1)}, bf16[6,2,384,128]{3,2,1,0:T(8,128)(2,1)}, u32[]{:S(2)}, u32[]{:S(2)}) %collective-permute-start.2) | collective-permute-done | bytes 1179680 | tf_op jit(solution)/shard_map/ppermute | solution.py:267
  41.2 5.1 %collective-permute-start.7 = (bf16[6,2,384,128]{3,2,1,0:T(8,128)(2,1)S(1)}, bf16[6,2,384,128]{3,2,1,0:T(8,128)(2,1)}, u32[]{:S(2)}, u32[]{:S(2)}) collective-permute-start(bf16[6,2,384,128]{3,2,1,0:T(8,128)(2,1)S(1)} %collective-permute-done.6.refs_1_.refs_2_.refs_4_), channel_id=1, source_target_pairs={{2,0},{4,2},{6,4},{8,6},{10,8},{12,10},{14,12},{16,14},{18,16},{20... | collective-permute-start | bytes 3538952 | tf_op jit(solution)/shard_map/ppermute | solution.py:267
  46.3 0.7 copy.12.s_ref
  47.6 0.6 reshape.17.refs_9_
  48.2 1.9 %pad_add_fusion.place_ref = s32[4]{0:T(128)} fusion(s32[1]{0:T(128)} %collective-permute-done.1, s32[1]{0:T(128)} %collective-permute-done, s32[1]{0:T(128)} %bitcast.1, s32[1]{0:T(128)} %bitcast.place_ref), kind=kLoop, calls=%fused_computation.7 | loop fusion | flops 12 | bytes 32 | tf_op jit(solution)/shard_map/stack | solution.py:293
  50.2 14.7 %own.1.refs_6_ = f32[6,2,384,384]{3,2,1,0:T(8,128)} custom-call(s32[2,1]{1,0:T(2,128)} %copy.12.s_ref, s32[4]{0:T(128)} %pad_add_fusion.place_ref, bf16[12,8,8,768]{3,2,1,0:T(8,128)(2,1)} %q_ref.5, bf16[6,2,384,128]{3,2,1,0:T(8,128)(2,1)} %bitcast.14, bf16[6,2,384,128]{3,2,1,0:T(8,128)(2,1)} %bitcast.10, ...), custom_call_target="tpu_custom_call" | custom-call | bytes 1024 | tf_op jit(solution)/shard_map/own/pallas_call | solution.py:243
  64.8 1.7 %collective-permute-done.4.refs_0_.refs_1_ = bf16[6,2,384,128]{3,2,1,0:T(8,128)(2,1)} collective-permute-done((bf16[6,2,384,128]{3,2,1,0:T(8,128)(2,1)}, bf16[6,2,384,128]{3,2,1,0:T(8,128)(2,1)}, u32[]{:S(2)}, u32[]{:S(2)}) %collective-permute-start.4) | collective-permute-done | bytes 1179680 | tf_op jit(solution)/shard_map/ppermute | solution.py:267
  66.5 1.0 copy-done.2
  67.5 2.8 %near1.1 = bf16[6,2,384,128]{3,2,1,0:T(8,128)(2,1)} custom-call(s32[4]{0:T(128)} %pad_add_fusion.place_ref, bf16[6,2,384,128]{3,2,1,0:T(8,128)(2,1)} %collective-permute-done.4.refs_0_.refs_1_, bf16[6,2,384,128]{3,2,1,0:T(8,128)(2,1)} %copy-done.2), custom_call_target="tpu_custom_call" | custom-call | bytes 1024 | tf_op jit(solution)/shard_map/near1/pallas_call | solution.py:82
  70.5 2.9 %far1.1 = bf16[6,2,384,128]{3,2,1,0:T(8,128)(2,1)} custom-call(s32[4]{0:T(128)} %pad_add_fusion.place_ref, bf16[6,2,384,128]{3,2,1,0:T(8,128)(2,1)} %collective-permute-done.2.refs_0_, bf16[6,2,384,128]{3,2,1,0:T(8,128)(2,1)} %copy-done.1), custom_call_target="tpu_custom_call" | custom-call | bytes 1024 | tf_op jit(solution)/shard_map/far1/pallas_call | solution.py:82
  73.4 2.8 %collective-permute-start.12 = (bf16[6,2,384,128]{3,2,1,0:T(8,128)(2,1)}, bf16[6,2,384,128]{3,2,1,0:T(8,128)(2,1)}, u32[]{:S(2)}, u32[]{:S(2)}) collective-permute-start(bf16[6,2,384,128]{3,2,1,0:T(8,128)(2,1)} %far1.1), channel_id=1, source_target_pairs={{32,64},{64,32},{96,128},{128,96},{160,192},{192,160},{33,65},{65,... | collective-permute-start | bytes 3538952 | tf_op jit(solution)/shard_map/ppermute | solution.py:277
  76.3 15.5 %collective-permute-done.3.refs_0_ = bf16[6,2,384,128]{3,2,1,0:T(8,128)(2,1)} collective-permute-done((bf16[6,2,384,128]{3,2,1,0:T(8,128)(2,1)}, bf16[6,2,384,128]{3,2,1,0:T(8,128)(2,1)}, u32[]{:S(2)}, u32[]{:S(2)}) %collective-permute-start.3) | collective-permute-done | bytes 1179680 | tf_op jit(solution)/shard_map/ppermute | solution.py:267
  91.8 1.4 %collective-permute-start.9 = (bf16[6,2,384,128]{3,2,1,0:T(8,128)(2,1)S(1)}, bf16[6,2,384,128]{3,2,1,0:T(8,128)(2,1)}, u32[]{:S(2)}, u32[]{:S(2)}) collective-permute-start(bf16[6,2,384,128]{3,2,1,0:T(8,128)(2,1)S(1)} %copy-done.3), channel_id=1, source_target_pairs={{2,0},{4,2},{6,4},{8,6},{10,8},{12,10},{14,12},{16,14},{18,16},{20... | collective-permute-start | bytes 3538952 | tf_op jit(solution)/shard_map/ppermute | solution.py:267
  93.2 2.8 %far2.1 = bf16[6,2,384,128]{3,2,1,0:T(8,128)(2,1)} custom-call(s32[4]{0:T(128)} %pad_add_fusion.place_ref, bf16[6,2,384,128]{3,2,1,0:T(8,128)(2,1)} %collective-permute-done.3.refs_0_, bf16[6,2,384,128]{3,2,1,0:T(8,128)(2,1)} %collective-permute-done.7.refs_1_.refs_2_, bf16[6,2,384,128]{3,2,1,0:T(8,128)(2,1)} %copy-done.1), custom_call_target="tpu_custom_call" | custom-call | bytes 1024 | tf_op jit(solution)/shard_map/far2/pallas_call | solution.py:82
  96.0 3.6 %collective-permute-start.14 = (bf16[6,2,384,128]{3,2,1,0:T(8,128)(2,1)}, bf16[6,2,384,128]{3,2,1,0:T(8,128)(2,1)S(1)}, u32[]{:S(2)}, u32[]{:S(2)}) collective-permute-start(bf16[6,2,384,128]{3,2,1,0:T(8,128)(2,1)} %far2.1), channel_id=1, source_target_pairs={{32,64},{64,32},{96,128},{128,96},{160,192},{192,160},{33,65},{65,... | collective-permute-start | bytes 3538952 | tf_op jit(solution)/shard_map/ppermute | solution.py:277
  99.6 14.9 %next.1.refs_8_ = f32[6,2,384,384]{3,2,1,0:T(8,128)} custom-call(s32[2,1]{1,0:T(2,128)} %copy.12.s_ref, s32[4]{0:T(128)} %pad_add_fusion.place_ref, bf16[12,8,8,768]{3,2,1,0:T(8,128)(2,1)} %q_ref.5, bf16[6,2,384,128]{3,2,1,0:T(8,128)(2,1)} %collective-permute-done.2.refs_0_, bf16[6,2,384,128]{3,2,1,0:T(8,128)(2,1)} %collective-permute-done.4.refs_0_.refs_1_, ...), custom_call_target="tpu_custom_call" | custom-call | bytes 1024 | tf_op jit(solution)/shard_map/next/pallas_call | solution.py:243
  114.5 1.6 %collective-permute-done.5.refs_0_.refs_1_ = bf16[6,2,384,128]{3,2,1,0:T(8,128)(2,1)} collective-permute-done((bf16[6,2,384,128]{3,2,1,0:T(8,128)(2,1)}, bf16[6,2,384,128]{3,2,1,0:T(8,128)(2,1)}, u32[]{:S(2)}, u32[]{:S(2)}) %collective-permute-start.5) | collective-permute-done | bytes 1179680 | tf_op jit(solution)/shard_map/ppermute | solution.py:267
  116.1 3.0 %collective-permute-done.9.refs_1_.refs_3_ = bf16[6,2,384,128]{3,2,1,0:T(8,128)(2,1)} collective-permute-done((bf16[6,2,384,128]{3,2,1,0:T(8,128)(2,1)S(1)}, bf16[6,2,384,128]{3,2,1,0:T(8,128)(2,1)}, u32[]{:S(2)}, u32[]{:S(2)}) %collective-permute-start.9) | collective-permute-done | bytes 1179680 | tf_op jit(solution)/shard_map/ppermute | solution.py:267
  119.1 2.9 %near2.1 = bf16[6,2,384,128]{3,2,1,0:T(8,128)(2,1)} custom-call(s32[4]{0:T(128)} %pad_add_fusion.place_ref, bf16[6,2,384,128]{3,2,1,0:T(8,128)(2,1)} %collective-permute-done.5.refs_0_.refs_1_, bf16[6,2,384,128]{3,2,1,0:T(8,128)(2,1)} %collective-permute-done.9.refs_1_.refs_3_, bf16[6,2,384,128]{3,2,1,0:T(8,128)(2,1)} %copy-done.2), custom_call_target="tpu_custom_call" | custom-call | bytes 1024 | tf_op jit(solution)/shard_map/near2/pallas_call | solution.py:82
  122.4 2.7 %collective-permute-done.15.refs_7_ = bf16[6,2,384,128]{3,2,1,0:T(8,128)(2,1)S(1)} collective-permute-done((bf16[6,2,384,128]{3,2,1,0:T(8,128)(2,1)}, bf16[6,2,384,128]{3,2,1,0:T(8,128)(2,1)S(1)}, u32[]{:S(2)}, u32[]{:S(2)}) %collective-permute-start.15) | collective-permute-done | bytes 1179680 | tf_op jit(solution)/shard_map/ppermute | solution.py:282
  125.2 1.1 copy-done.5
  126.3 14.7 %last.1 = bf16[12,8,8,768]{3,2,1,0:T(8,128)(2,1)} custom-call(s32[2,1]{1,0:T(2,128)} %copy.12.s_ref, s32[4]{0:T(128)} %pad_add_fusion.place_ref, bf16[12,8,8,768]{3,2,1,0:T(8,128)(2,1)} %q_ref.5, bf16[6,2,384,128]{3,2,1,0:T(8,128)(2,1)} %collective-permute-done.3.refs_0_, bf16[6,2,384,128]{3,2,1,0:T(8,128)(2,1)} %collective-permute-done.5.refs_0_.refs_1_, ...), custom_call_target="tpu_custom_call" | custom-call | bytes 1024 | tf_op jit(solution)/shard_map/last/pallas_call | solution.py:243
  (34 shorter events, 1.7 us)
Async XLA Ops:
  0.0 47.1 %copy-start = (f32[256,768]{1,0:T(8,128)S(1)}, f32[256,768]{1,0:T(8,128)}, u32[]{:S(2)}) copy-start(f32[256,768]{1,0:T(8,128)} %param.11) | copy-start | bytes 2359300
  0.0 14.5 %copy-start.6 = (s32[2,1]{0,1:T(1,128)S(1)}, s32[2,1]{0,1:T(1,128)}, u32[]{:S(2)}) copy-start(s32[2,1]{0,1:T(1,128)} %param.9) | copy-start | bytes 28
  0.0 47.0 %copy-start.7 = (s32[2]{0:T(128)S(1)}, s32[2]{0:T(128)}, u32[]{:S(2)}) copy-start(s32[2]{0:T(128)} %param.10) | copy-start | bytes 28
  2.8 21.2 %collective-permute-start.10 = (bf16[6,2,384,128]{3,2,1,0:T(8,128)(2,1)}, bf16[6,2,384,128]{3,2,1,0:T(8,128)(2,1)}, u32[]{:S(2)}, u32[]{:S(2)}) collective-permute-start(bf16[6,2,384,128]{3,2,1,0:T(8,128)(2,1)} %bitcast.11), channel_id=1, source_target_pairs={{32,64},{64,32},{96,128},{128,96},{160,192},{192,160},{33,65},{65,... | collective-permute-start | bytes 3538952 | tf_op jit(solution)/shard_map/ppermute | solution.py:277
  6.3 34.9 %collective-permute-start.2 = (bf16[6,2,384,128]{3,2,1,0:T(8,128)(2,1)}, bf16[6,2,384,128]{3,2,1,0:T(8,128)(2,1)}, u32[]{:S(2)}, u32[]{:S(2)}) collective-permute-start(bf16[6,2,384,128]{3,2,1,0:T(8,128)(2,1)} %bitcast.12), channel_id=1, source_target_pairs={{30,0},{0,2},{2,4},{4,6},{6,8},{8,10},{10,12},{12,14},{14,16},{16,... | collective-permute-start | bytes 3538952 | tf_op jit(solution)/shard_map/ppermute | solution.py:267
  8.0 33.2 %collective-permute-start.6 = (bf16[6,2,384,128]{3,2,1,0:T(8,128)(2,1)}, bf16[6,2,384,128]{3,2,1,0:T(8,128)(2,1)S(1)}, u32[]{:S(2)}, u32[]{:S(2)}) collective-permute-start(bf16[6,2,384,128]{3,2,1,0:T(8,128)(2,1)} %bitcast.13), channel_id=1, source_target_pairs={{2,0},{4,2},{6,4},{8,6},{10,8},{12,10},{14,12},{16,14},{18,16},{20... | collective-permute-start | bytes 3538952 | tf_op jit(solution)/shard_map/ppermute | solution.py:267
  14.5 35.6 %collective-permute-start.11 = (bf16[6,2,384,128]{3,2,1,0:T(8,128)(2,1)}, bf16[6,2,384,128]{3,2,1,0:T(8,128)(2,1)}, u32[]{:S(2)}, u32[]{:S(2)}) collective-permute-start(bf16[6,2,384,128]{3,2,1,0:T(8,128)(2,1)} %bitcast.7), channel_id=1, source_target_pairs={{0,32},{32,0},{64,96},{96,64},{128,160},{160,128},{192,224},{224,1... | collective-permute-start | bytes 3538952 | tf_op jit(solution)/shard_map/ppermute | solution.py:282
  15.2 5.7 %collective-permute-start = (s32[1]{0:T(128)}, s32[1]{0:T(128)}, u32[]{:S(2)}, u32[]{:S(2)}) collective-permute-start(s32[1]{0:T(128)} %get-tuple-element.37), channel_id=1, source_target_pairs={{32,64},{64,32},{96,128},{128,96},{160,192},{192,160},{33,65},{65,... | collective-permute-start | bytes 20 | tf_op jit(solution)/shard_map/ppermute | solution.py:277
  21.0 1.4 collective-permute-start.1
  22.4 44.1 %collective-permute-start.4 = (bf16[6,2,384,128]{3,2,1,0:T(8,128)(2,1)}, bf16[6,2,384,128]{3,2,1,0:T(8,128)(2,1)}, u32[]{:S(2)}, u32[]{:S(2)}) collective-permute-start(bf16[6,2,384,128]{3,2,1,0:T(8,128)(2,1)} %bitcast.8), channel_id=1, source_target_pairs={{30,0},{0,2},{2,4},{4,6},{6,8},{8,10},{10,12},{12,14},{14,16},{16,... | collective-permute-start | bytes 3538952 | tf_op jit(solution)/shard_map/ppermute | solution.py:267
  24.0 42.5 %collective-permute-start.8 = (bf16[6,2,384,128]{3,2,1,0:T(8,128)(2,1)}, bf16[6,2,384,128]{3,2,1,0:T(8,128)(2,1)S(1)}, u32[]{:S(2)}, u32[]{:S(2)}) collective-permute-start(bf16[6,2,384,128]{3,2,1,0:T(8,128)(2,1)} %bitcast.9), channel_id=1, source_target_pairs={{2,0},{4,2},{6,4},{8,6},{10,8},{12,10},{14,12},{16,14},{18,16},{20... | collective-permute-start | bytes 3538952 | tf_op jit(solution)/shard_map/ppermute | solution.py:267
  41.2 50.6 %collective-permute-start.3 = (bf16[6,2,384,128]{3,2,1,0:T(8,128)(2,1)}, bf16[6,2,384,128]{3,2,1,0:T(8,128)(2,1)}, u32[]{:S(2)}, u32[]{:S(2)}) collective-permute-start(bf16[6,2,384,128]{3,2,1,0:T(8,128)(2,1)} %collective-permute-done.2.refs_0_), channel_id=1, source_target_pairs={{30,0},{0,2},{2,4},{4,6},{6,8},{8,10},{10,12},{12,14},{14,16},{16,... | collective-permute-start | bytes 3538952 | tf_op jit(solution)/shard_map/ppermute | solution.py:267
  41.2 23.6 %copy-start.1 = (bf16[6,2,384,128]{3,2,1,0:T(8,128)(2,1)}, bf16[6,2,384,128]{3,2,1,0:T(8,128)(2,1)S(1)}, u32[]{:S(2)}) copy-start(bf16[6,2,384,128]{3,2,1,0:T(8,128)(2,1)S(1)} %collective-permute-done.6.refs_1_.refs_2_.refs_4_) | copy-start | bytes 3538948
  41.2 52.0 %collective-permute-start.7 = (bf16[6,2,384,128]{3,2,1,0:T(8,128)(2,1)S(1)}, bf16[6,2,384,128]{3,2,1,0:T(8,128)(2,1)}, u32[]{:S(2)}, u32[]{:S(2)}) collective-permute-start(bf16[6,2,384,128]{3,2,1,0:T(8,128)(2,1)S(1)} %collective-permute-done.6.refs_1_.refs_2_.refs_4_), channel_id=1, source_target_pairs={{2,0},{4,2},{6,4},{8,6},{10,8},{12,10},{14,12},{16,14},{18,16},{20... | collective-permute-start | bytes 3538952 | tf_op jit(solution)/shard_map/ppermute | solution.py:267
  66.5 1.0 copy-start.2
  70.4 21.4 %copy-start.3 = (bf16[6,2,384,128]{3,2,1,0:T(8,128)(2,1)S(1)}, bf16[6,2,384,128]{3,2,1,0:T(8,128)(2,1)}, u32[]{:S(2)}) copy-start(bf16[6,2,384,128]{3,2,1,0:T(8,128)(2,1)} %copy-done.2) | copy-start | bytes 3538948
  70.4 29.2 %collective-permute-start.13 = (bf16[6,2,384,128]{3,2,1,0:T(8,128)(2,1)}, bf16[6,2,384,128]{3,2,1,0:T(8,128)(2,1)}, u32[]{:S(2)}, u32[]{:S(2)}) collective-permute-start(bf16[6,2,384,128]{3,2,1,0:T(8,128)(2,1)} %near1.1), channel_id=1, source_target_pairs={{0,32},{32,0},{64,96},{96,64},{128,160},{160,128},{192,224},{224,1... | collective-permute-start | bytes 3538952 | tf_op jit(solution)/shard_map/ppermute | solution.py:282
  73.4 26.2 %collective-permute-start.12 = (bf16[6,2,384,128]{3,2,1,0:T(8,128)(2,1)}, bf16[6,2,384,128]{3,2,1,0:T(8,128)(2,1)}, u32[]{:S(2)}, u32[]{:S(2)}) collective-permute-start(bf16[6,2,384,128]{3,2,1,0:T(8,128)(2,1)} %far1.1), channel_id=1, source_target_pairs={{32,64},{64,32},{96,128},{128,96},{160,192},{192,160},{33,65},{65,... | collective-permute-start | bytes 3538952 | tf_op jit(solution)/shard_map/ppermute | solution.py:277
  76.2 39.9 %collective-permute-start.5 = (bf16[6,2,384,128]{3,2,1,0:T(8,128)(2,1)}, bf16[6,2,384,128]{3,2,1,0:T(8,128)(2,1)}, u32[]{:S(2)}, u32[]{:S(2)}) collective-permute-start(bf16[6,2,384,128]{3,2,1,0:T(8,128)(2,1)} %collective-permute-done.4.refs_0_.refs_1_), channel_id=1, source_target_pairs={{30,0},{0,2},{2,4},{4,6},{6,8},{8,10},{10,12},{12,14},{14,16},{16,... | collective-permute-start | bytes 3538952 | tf_op jit(solution)/shard_map/ppermute | solution.py:267
  91.8 27.4 %collective-permute-start.9 = (bf16[6,2,384,128]{3,2,1,0:T(8,128)(2,1)S(1)}, bf16[6,2,384,128]{3,2,1,0:T(8,128)(2,1)}, u32[]{:S(2)}, u32[]{:S(2)}) collective-permute-start(bf16[6,2,384,128]{3,2,1,0:T(8,128)(2,1)S(1)} %copy-done.3), channel_id=1, source_target_pairs={{2,0},{4,2},{6,4},{8,6},{10,8},{12,10},{14,12},{16,14},{18,16},{20... | collective-permute-start | bytes 3538952 | tf_op jit(solution)/shard_map/ppermute | solution.py:267
  96.0 26.0 %collective-permute-start.14 = (bf16[6,2,384,128]{3,2,1,0:T(8,128)(2,1)}, bf16[6,2,384,128]{3,2,1,0:T(8,128)(2,1)S(1)}, u32[]{:S(2)}, u32[]{:S(2)}) collective-permute-start(bf16[6,2,384,128]{3,2,1,0:T(8,128)(2,1)} %far2.1), channel_id=1, source_target_pairs={{32,64},{64,32},{96,128},{128,96},{160,192},{192,160},{33,65},{65,... | collective-permute-start | bytes 3538952 | tf_op jit(solution)/shard_map/ppermute | solution.py:277
  122.0 3.2 %copy-start.4 = (bf16[6,2,384,128]{3,2,1,0:T(8,128)(2,1)}, bf16[6,2,384,128]{3,2,1,0:T(8,128)(2,1)S(1)}, u32[]{:S(2)}) copy-start(bf16[6,2,384,128]{3,2,1,0:T(8,128)(2,1)S(1)} %collective-permute-done.14.refs_6_) | copy-start | bytes 3538948
  122.0 3.1 %collective-permute-start.15 = (bf16[6,2,384,128]{3,2,1,0:T(8,128)(2,1)}, bf16[6,2,384,128]{3,2,1,0:T(8,128)(2,1)S(1)}, u32[]{:S(2)}, u32[]{:S(2)}) collective-permute-start(bf16[6,2,384,128]{3,2,1,0:T(8,128)(2,1)} %near2.1), channel_id=1, source_target_pairs={{0,32},{32,0},{64,96},{96,64},{128,160},{160,128},{192,224},{224,1... | collective-permute-start | bytes 3538952 | tf_op jit(solution)/shard_map/ppermute | solution.py:282
  125.2 1.1 copy-start.5

commit v4 on v3

v4 whole, which is shorter than its diff:
```python
import functools
import itertools
import math

import jax
import jax.numpy as jnp
from jax import lax
from jax.experimental import pallas as pl
from jax.experimental.pallas import tpu as pltpu
from jax.sharding import PartitionSpec as P

HD = 128
FREQ = 256
ROWS = 384
TT = 6
SCALE = math.log2(math.e) / math.sqrt(HD)
ANY = pl.BlockSpec(memory_space=pltpu.HBM)
SMALL = pl.CostEstimate(flops=0, bytes_accessed=1024, transcendentals=0)
VMEM = pl.BlockSpec(memory_space=pltpu.VMEM)
SMEM = pl.BlockSpec(memory_space=pltpu.SMEM)


PICKS = (lambda s: 0 * s, lambda s: jnp.where(s > 0, 1, 0), lambda s: jnp.where(s == 0, 2, jnp.where(s > 0, 1, 0)))


def split_kernel(far, place_ref, k_ref, v_ref, out, hold, into, out_of):
    core = place_ref[0]
    first = (core if far else 1 - core) * TT
    count = out.shape[0]
    last = []
    for i in range(count):
        for which, ref in enumerate((k_ref, v_ref)):
            source = ref.at[pl.ds(first, TT), :, :, pl.ds(i * HD, HD)]
            pltpu.make_async_copy(source, hold.at[i, which], into.at[i]).start()
        last.append(pltpu.make_async_copy(hold.at[i], out.at[i], out_of.at[i]))
    for i, copy in enumerate(last):
        pltpu.make_async_copy(hold.at[i], hold.at[i], into.at[i]).wait()
        copy.start()
    for copy in last:
        copy.wait()


def split(name, far, place, k, v):
    n = k.shape[3] // HD
    x = pl.pallas_call(
        functools.partial(split_kernel, far),
        out_shape=jax.ShapeDtypeStruct((n, 2, TT, 8, 8, HD), k.dtype),
        in_specs=[SMEM, ANY, ANY],
        out_specs=ANY,
        scratch_shapes=[pltpu.VMEM((n, 2, TT, 8, 8, HD), k.dtype), pltpu.SemaphoreType.DMA((n,)), pltpu.SemaphoreType.DMA((n,))],
        cost_estimate=SMALL,
        compiler_params=pltpu.CompilerParams(vmem_limit_bytes=60 * 2**20),
        name=name,
    )(place, k, v)
    return x.reshape(n, 2, ROWS, HD)


def hand_on_kernel(x_ref, *refs):
    out = refs[-1]
    for i in range(out.shape[0]):
        out[i] = x_ref[i]


def hand_on(x, *others):
    return pl.pallas_call(
        hand_on_kernel,
        out_shape=jax.ShapeDtypeStruct(x.shape, x.dtype),
        in_specs=[SMEM] + [ANY] * len(others),
        out_specs=SMEM,
        cost_estimate=SMALL,
        compiler_params=pltpu.CompilerParams(vmem_limit_bytes=60 * 2**20),
        name="hand_on",
    )(x, *others)


def choose_kernel(pick, slot, place_ref, *refs):
    ins, (out, hold, into, out_of) = refs[:-4], refs[-4:]
    side = pick(place_ref[slot])
    count = out.shape[0]
    for c, ref in enumerate(ins):
        @pl.when(side == c)
        def _():
            for i in range(count):
                pltpu.make_async_copy(ref.at[i], hold.at[i], into.at[i]).start()
    last = [pltpu.make_async_copy(hold.at[i], out.at[i], out_of.at[i]) for i in range(count)]
    for i, copy in enumerate(last):
        pltpu.make_async_copy(hold.at[i], hold.at[i], into.at[i]).wait()
        copy.start()
    for copy in last:
        copy.wait()


def choose(name, phase, slot, place, xs):
    x = xs[0]
    return pl.pallas_call(
        functools.partial(choose_kernel, PICKS[phase], slot),
        out_shape=jax.ShapeDtypeStruct(x.shape, x.dtype),
        in_specs=[SMEM] + [ANY] * len(xs),
        out_specs=ANY,
        scratch_shapes=[pltpu.VMEM(x.shape, x.dtype), pltpu.SemaphoreType.DMA(x.shape[:1]), pltpu.SemaphoreType.DMA(x.shape[:1])],
        cost_estimate=SMALL,
        compiler_params=pltpu.CompilerParams(vmem_limit_bytes=60 * 2**20),
        name=name,
    )(place, *xs)


def attn_kernel(plan, first, count, s_ref, place_ref, q_ref, *refs):
    names, starts, finishes, phases = plan
    blocks = [[(phase, b) for phase in phases for b in letters] for letters in ("EFN", "FNM")]
    ops = dict(zip(names, refs))
    out_ref, kv, qv, sc, top, si, so, ov, ksem, qsem, isem, osem = refs[len(refs) - 12:]
    core, cut = place_ref[0], place_ref[1]
    tiles = (core, 1 - core)
    width = [len(b) * ROWS for b in blocks]
    base = (0, len(blocks[0]))

    def fill(i, slot):
        h = first + i
        for u in range(2):
            for j, ((phase, sides), block) in enumerate(blocks[u]):
                side = PICKS[phase](s_ref[tiles[u], 0])
                to = kv.at[slot, :, base[u] + j]
                sem = ksem.at[slot, u]
                if block == "M":
                    pltpu.make_async_copy(ops[f"M{phase}"].at[h], to, sem).start()
                    continue
                if block == "E":
                    @pl.when(cut == 0)
                    def _():
                        pltpu.make_async_copy(ops[f"E{phase}"].at[h], to, sem).start()
                for c in range(sides):
                    name = f"{'N' if block == 'N' else 'F'}{phase}{c}"

                    @pl.when((side == c) & ((cut != 0) if block == "E" else True))
                    def _():
                        pltpu.make_async_copy(ops[name].at[h], to, sem).start()
        q_copy(i, slot).start()
        if not starts:
            state_in(i, slot).start()

    def filled(i, slot):
        for u in range(2):
            whole = kv.at[slot, :, pl.ds(base[u], len(blocks[u]))]
            pltpu.make_async_copy(whole, whole, ksem.at[slot, u]).wait()
        q_copy(i, slot).wait()
        if not starts:
            state_in(i, slot).wait()

    def lanes(i):
        return pl.ds(pl.multiple_of((first + i) * HD, HD), HD)

    def q_copy(i, slot):
        return pltpu.make_async_copy(q_ref.at[:, :, :, lanes(i)], qv.at[slot], qsem.at[slot])

    def state_in(i, slot):
        return pltpu.make_async_copy(ops["state"].at[first + i], si.at[slot], isem.at[slot])

    def result(i):
        slot = lax.rem(i, 2)
        if finishes:
            return pltpu.make_async_copy(ov.at[slot], out_ref.at[:, :, :, lanes(i)], osem.at[slot])
        return pltpu.make_async_copy(so.at[slot], out_ref.at[first + i], osem.at[slot])

    def stacked(slot, which, u):
        return kv[slot, which, base[u]:base[u] + len(blocks[u])].reshape(width[u], HD)

    def scores(slot, u, sc, top):
        k = stacked(slot, 0, u)
        step = ROWS
        for r in range(0, ROWS, step):
            q = qv[slot, pl.ds(tiles[u] * TT + r // 64, step // 64)].reshape(step, HD)
            s = lax.dot_general(q, k, (((1,), (1,)), ((), ())), preferred_element_type=jnp.float32)
            sc[r:r + step, :width[u]] = s
            m = s[:, :HD]
            for c in range(HD, width[u], HD):
                m = jnp.maximum(m, s[:, c:c + HD])
            m = jnp.broadcast_to(jnp.max(m, axis=1, keepdims=True), (step, HD))
            if not starts:
                m = jnp.maximum(m, jnp.broadcast_to(si[slot, u, r:r + step, HD:HD + 1], (step, HD)))
            top[r:r + step] = m
            yield

    def weigh(i, slot, u, sc, top):
        to = lax.rem(i, 2)
        v2 = []
        for j, (_, block) in enumerate(blocks[u]):
            v = jnp.concatenate([kv[slot, 1, base[u] + j], jnp.ones((ROWS, HD), jnp.bfloat16)], axis=1)
            v2.append(jnp.where(cut != 0, jnp.zeros_like(v), v) if block == "E" else v)
        v2 = jnp.concatenate(v2, axis=0)
        step = ROWS
        for r in range(0, ROWS, step):
            m1 = top[r:r + step]
            m = jnp.concatenate([m1] * (width[u] // HD), axis=1)
            p = jnp.exp2((sc[r:r + step, :width[u]] - m) * SCALE).astype(jnp.bfloat16)
            acc = jnp.dot(p, v2, preferred_element_type=jnp.float32)
            if not starts:
                old = si[slot, u, r:r + step, HD:]
                fade = jnp.exp2((jnp.broadcast_to(old[:, :1], (step, HD)) - m1) * SCALE)
                total = jnp.broadcast_to(old[:, HD - 1:], (step, HD))
                acc += jnp.concatenate([si[slot, u, r:r + step, :HD], total], axis=1) * jnp.concatenate([fade, fade], axis=1)
            if finishes:
                o = acc[:, :HD] / acc[:, HD:] * ops["gate"][tiles[u], first + i]
                ov[to, pl.ds(tiles[u] * TT + r // 64, step // 64)] = o.astype(jnp.bfloat16).reshape(step // 64, 8, 8, HD)
            else:
                lane = lax.broadcasted_iota(jnp.int32, (step, HD), 1)
                so[to, u, r:r + step, :HD] = acc[:, :HD]
                so[to, u, r:r + step, HD:] = jnp.where(lane < HD // 2, m1, acc[:, HD:])
            yield

    def both(*steps):
        for _ in itertools.zip_longest(*steps):
            pass

    def head(i, par, last):
        slot, ahead = lax.rem(i, 3), lax.rem(i + 1, 3)
        if not last:
            @pl.when(i + 2 < count)
            def _():
                fill(i + 2, lax.rem(i + 2, 3))

        @pl.when(i >= 2)
        def _():
            result(i - 2).wait()
        steps = [weigh(i, slot, u, sc.at[par, u], top.at[par, u]) for u in range(2)]
        if not last:
            filled(i + 1, ahead)
            steps += [scores(ahead, u, sc.at[1 - par, u], top.at[1 - par, u]) for u in range(2)]
        both(*steps)
        result(i).start()

    fill(0, 0)
    if count > 1:
        fill(1, 1)
    filled(0, 0)
    both(*[scores(0, u, sc.at[0, u], top.at[0, u]) for u in range(2)])

    def pair(p, _):
        head(2 * p, 0, False)
        head(2 * p + 1, 1, False)
        return 0
    lax.fori_loop(0, (count - 1) // 2, pair, 0)
    if count % 2 == 0:
        head(jnp.int32(count - 2), 0, False)
    head(jnp.int32(count - 1), (count - 1) % 2, True)
    for i in range(max(0, count - 2), count):
        result(i).wait()


def attend(name, parts, *, s, place, q, state=None, gate=None):
    arrays, phases = {}, []
    for phase, columns, halos in parts:
        phases.append((phase, len(columns)))
        for c, (far, near) in enumerate(columns):
            arrays[f"F{phase}{c}"], arrays[f"N{phase}{c}"] = far, near
        arrays[f"E{phase}"], arrays[f"M{phase}"] = halos
    arrays.update(state=state, gate=gate)
    arrays = {n: x for n, x in arrays.items() if x is not None}
    names = tuple(arrays)
    heads = q.shape[3] // HD
    plan = (names, state is None, gate is not None, phases)
    shape = jax.ShapeDtypeStruct((heads, 2, ROWS, 2 * HD), jnp.float32)
    if gate is not None:
        shape = jax.ShapeDtypeStruct(q.shape, q.dtype)
    blocks = 3 * len(phases)
    return pl.pallas_call(
        functools.partial(attn_kernel, plan, 0, heads),
        out_shape=shape,
        in_specs=[SMEM, SMEM, ANY] + [VMEM if n == "gate" else ANY for n in names],
        out_specs=ANY,
        scratch_shapes=[
            pltpu.VMEM((3, 2, 2 * blocks, ROWS, HD), jnp.bfloat16),
            pltpu.VMEM((3, 12, 8, 8, HD), jnp.bfloat16),
            pltpu.VMEM((2, 2, ROWS, blocks * ROWS), jnp.float32),
            pltpu.VMEM((2, 2, ROWS, HD), jnp.float32),
            pltpu.VMEM((3, 2, ROWS, 2 * HD), jnp.float32),
            pltpu.VMEM((2, 2, ROWS, 2 * HD), jnp.float32),
            pltpu.VMEM((2, 12, 8, 8, HD), jnp.bfloat16),
            pltpu.SemaphoreType.DMA((3, 2)), pltpu.SemaphoreType.DMA((3,)),
            pltpu.SemaphoreType.DMA((3,)), pltpu.SemaphoreType.DMA((2,))],
        compiler_params=pltpu.CompilerParams(vmem_limit_bytes=60 * 2**20),
        cost_estimate=SMALL,
        name=name,
    )(s, place, q, *arrays.values())


def from_behind(block, distance):
    size = lax.axis_size("lon")
    return lax.ppermute(block, "lon", [((i - distance) % size, i) for i in range(size)])


def pairs(off):
    size = lax.axis_size("tm")
    return [[i + off, (i + off + 1) % size] for i in range(0, size, 2)]


def far_swap(x):
    route = [r for a, b in pairs(1)[:-1] for r in ((a, b), (b, a))]
    return lax.ppermute(x, "tm", route)


def near_swap(x):
    route = [r for a, b in pairs(0) for r in ((a, b), (b, a))]
    return lax.ppermute(x, "tm", route)


def local(query_field, key_field, value_field, tile_offsets, timesteps, gate_weight):
    heads = query_field.shape[3] // HD
    tiles = query_field.shape[0] // TT
    tm, size = lax.axis_index("tm"), lax.axis_size("tm")
    core = tm % 2
    cut = ((tm == 0) | (tm == size - 1)).astype(jnp.int32)
    shifts = tile_offsets[:, 0]
    mine = jnp.where(core == 0, shifts, shifts[::-1])
    place = jnp.stack([core, cut, far_swap(mine[:1])[0], near_swap(mine[1:])[0]])

    at = jnp.stack([core])
    xf = split("split_far", True, at, key_field, value_field)
    rf, lf = from_behind(xf, 1), from_behind(xf, -1)
    xn = split("split_near", False, at, key_field, value_field)
    rn, ln = from_behind(xn, 1), from_behind(xn, -1)
    r2f, l2f = from_behind(rf, 1), from_behind(lf, -1)
    r2n, l2n = from_behind(rn, 1), from_behind(ln, -1)

    half_freq = FREQ // 2
    frequencies = jnp.exp(-math.log(10000.0) * jnp.arange(half_freq, dtype=jnp.float32) / half_freq)
    angles = timesteps.astype(jnp.float32)[:, None] * frequencies[None, :]
    embedding = jnp.concatenate([jnp.cos(angles), jnp.sin(angles)], axis=1)
    gate_rows = jnp.dot(
        embedding, gate_weight, precision=lax.Precision.HIGHEST, preferred_element_type=jnp.float32
    ).reshape(tiles, heads, HD)

    attn = functools.partial(attend, s=tile_offsets, place=place, q=query_field)
    far0, near0 = far_swap(xf), near_swap(xn)
    later = hand_on(place, far0, near0)
    far1 = far_swap(choose("far1", 1, 2, later, [rf, lf]))
    near1 = near_swap(choose("near1", 1, 3, later, [rn, ln]))
    far2 = choose("far2", 2, 2, place, [r2f, l2f, lf])
    far1, far2, gate_rows = lax.optimization_barrier((far1, far2, gate_rows))
    parts = [(0, [(xf, xn)], (far0, near0)), (1, [(rf, rn), (lf, ln)], (far1, near1))]
    state = attn("first", parts)

    r2n_, l2n_, state = lax.optimization_barrier((r2n, l2n, state))
    near2, far2 = lax.optimization_barrier((choose("near2", 2, 3, place, [r2n_, l2n_, ln]), far_swap(far2)))
    parts = [(2, [(r2f, r2n), (l2f, l2n), (lf, ln)], (far2, near_swap(near2)))]
    return attn("last", parts, state=state, gate=gate_rows)


def solution(mesh):
    return jax.shard_map(
        local,
        mesh=mesh,
        in_specs=(
            P("tm", None, "lon", "head"),
            P("tm", None, "lon", "head"),
            P("tm", None, "lon", "head"),
            P("tm", "lon"),
            P("tm"),
            P(None, "head"),
        ),
        out_specs=P("tm", None, "lon", "head"),
        check_vma=False,
    )
```

time: 142 us -> 139 us (0.979)
  Pallas kernels: 58.6 us -> 46.3 us
  waiting for transfers between devices: 39.7 us -> 50.3 us
  starting transfers between devices: 35.9 us -> 34.4 us
    pallas_call x4 -> x5, Pallas kernels: 47.1 us -> 34.9 us  [the longest x2 29.4 us: attend(): pl.pallas_call(functools.partial(attn_kernel, plan, 0, heads), out_shape=...]
    ppermute x8, waiting for transfers between devices: 32.6 us -> 43.3 us  [from_behind(): lax.ppermute(block, 'lon', [((i - distance) % size, i) for i in range(siz...]
    ppermute x8, starting transfers between devices: 22.8 us -> 20.9 us  [from_behind(): lax.ppermute(block, 'lon', [((i - distance) % size, i) for i in range(siz...]
  transfers between devices with their start and end apart: 16 -> 16, of which waited for: 8 -> 7; matrix products, arithmetic and copies ran while one was open for 3% -> 3% of each run, Pallas kernels for 29% -> 23%
where the time goes in v4:
time: 139 us; the launch traced here: 138 us
  waiting for transfers between devices  50.3 us (36%)
  Pallas kernels  46.3 us (33%)
  starting transfers between devices  34.4 us (25%)
  local copies, waits for them, and re-layouts  4.12 us (3%)
  other arithmetic  2.17 us (2%)
    ppermute x8, waiting for transfers between devices, from_behind(): lax.ppermute(block, 'lon', [((i - distance) % size, i) for i in range(siz...  43.3 us
    pallas_call x2, Pallas kernels, attend(): pl.pallas_call(functools.partial(attn_kernel, plan, 0, heads), out_shape=...  29.4 us
    ppermute x8, starting transfers between devices, from_behind(): lax.ppermute(block, 'lon', [((i - distance) % size, i) for i in range(siz...  20.9 us
    ppermute x4, starting transfers between devices, far_swap(): return lax.ppermute(x, 'tm', route)  12.7 us
    pallas_call x4, Pallas kernels, choose(): pl.pallas_call(functools.partial(choose_kernel, PICKS[phase], slot), out_...  11.4 us
    pallas_call x2, Pallas kernels, split(): pl.pallas_call(functools.partial(split_kernel, far), out_shape=jax.ShapeD...  4.37 us
    ppermute x4, waiting for transfers between devices, near_swap(): return lax.ppermute(x, 'tm', route)  3.86 us
    ppermute x4, waiting for transfers between devices, far_swap(): return lax.ppermute(x, 'tm', route)  3.09 us
  transfers between devices with their start and end apart: 16, of which 7 were waited for; matrix products, arithmetic and copies ran while one was open for 3% of the time, Pallas kernels for 23%

profile of v4, /device:TPU:17, one launch (start us, length us, event | category | flops | bytes accessed | tf_op | source)
XLA Modules:
  0.0 138.2 jit_solution(13860284806044377199)
XLA Ops:
  0.0 2.2 %split_far.1 = bf16[6,2,6,8,8,128]{5,4,3,2,1,0:T(8,128)(2,1)} custom-call(s32[1]{0:T(128)} %bitcast.place_ref, bf16[12,8,8,768]{3,2,1,0:T(8,128)(2,1)} %k_ref.3, bf16[12,8,8,768]{3,2,1,0:T(8,128)(2,1)} %v_ref.3), custom_call_target="tpu_custom_call" | custom-call | bytes 1024 | tf_op jit(solution)/shard_map/split_far/pallas_call | solution.py:45
  2.2 3.5 %collective-permute-start.10 = (bf16[6,2,384,128]{3,2,1,0:T(8,128)(2,1)}, bf16[6,2,384,128]{3,2,1,0:T(8,128)(2,1)}, u32[]{:S(2)}, u32[]{:S(2)}) collective-permute-start(bf16[6,2,384,128]{3,2,1,0:T(8,128)(2,1)} %bitcast.7), channel_id=1, source_target_pairs={{32,64},{64,32},{96,128},{128,96},{160,192},{192,160},{33,65},{65,... | collective-permute-start | bytes 3538952 | tf_op jit(solution)/shard_map/ppermute | solution.py:298
  5.7 1.7 %collective-permute-start.2 = (bf16[6,2,384,128]{3,2,1,0:T(8,128)(2,1)}, bf16[6,2,384,128]{3,2,1,0:T(8,128)(2,1)}, u32[]{:S(2)}, u32[]{:S(2)}) collective-permute-start(bf16[6,2,384,128]{3,2,1,0:T(8,128)(2,1)} %bitcast.8), channel_id=1, source_target_pairs={{30,0},{0,2},{2,4},{4,6},{6,8},{8,10},{10,12},{12,14},{14,16},{16,... | collective-permute-start | bytes 3538952 | tf_op jit(solution)/shard_map/ppermute | solution.py:288
  7.4 6.5 %collective-permute-start.6 = (bf16[6,2,384,128]{3,2,1,0:T(8,128)(2,1)}, bf16[6,2,384,128]{3,2,1,0:T(8,128)(2,1)S(1)}, u32[]{:S(2)}, u32[]{:S(2)}) collective-permute-start(bf16[6,2,384,128]{3,2,1,0:T(8,128)(2,1)} %bitcast.9), channel_id=1, source_target_pairs={{2,0},{4,2},{6,4},{8,6},{10,8},{12,10},{14,12},{16,14},{18,16},{20... | collective-permute-start | bytes 3538952 | tf_op jit(solution)/shard_map/ppermute | solution.py:288
  13.9 2.2 %split_near.1 = bf16[6,2,6,8,8,128]{5,4,3,2,1,0:T(8,128)(2,1)} custom-call(s32[1]{0:T(128)} %bitcast.place_ref, bf16[12,8,8,768]{3,2,1,0:T(8,128)(2,1)} %k_ref.3, bf16[12,8,8,768]{3,2,1,0:T(8,128)(2,1)} %v_ref.3), custom_call_target="tpu_custom_call" | custom-call | bytes 1024 | tf_op jit(solution)/shard_map/split_near/pallas_call | solution.py:45
  16.3 0.7 fusion.5
  17.0 2.4 %collective-permute-start = (s32[1]{0:T(128)}, s32[1]{0:T(128)}, u32[]{:S(2)}, u32[]{:S(2)}) collective-permute-start(s32[1]{0:T(128)} %get-tuple-element.23), channel_id=1, source_target_pairs={{32,64},{64,32},{96,128},{128,96},{160,192},{192,160},{33,65},{65,... | collective-permute-start | bytes 20 | tf_op jit(solution)/shard_map/ppermute | solution.py:298
  19.3 3.1 %collective-permute-done = s32[1]{0:T(128)} collective-permute-done((s32[1]{0:T(128)}, s32[1]{0:T(128)}, u32[]{:S(2)}, u32[]{:S(2)}) %collective-permute-start) | collective-permute-done | bytes 36 | tf_op jit(solution)/shard_map/ppermute | solution.py:298
  22.4 1.2 collective-permute-done.1
  23.6 6.1 %collective-permute-start.8 = (bf16[6,2,384,128]{3,2,1,0:T(8,128)(2,1)}, bf16[6,2,384,128]{3,2,1,0:T(8,128)(2,1)S(1)}, u32[]{:S(2)}, u32[]{:S(2)}) collective-permute-start(bf16[6,2,384,128]{3,2,1,0:T(8,128)(2,1)} %bitcast.13), channel_id=1, source_target_pairs={{2,0},{4,2},{6,4},{8,6},{10,8},{12,10},{14,12},{16,14},{18,16},{20... | collective-permute-start | bytes 3538952 | tf_op jit(solution)/shard_map/ppermute | solution.py:288
  29.7 2.0 %pad_add_fusion.x_ref.place_ref = s32[4]{0:T(128)} fusion(s32[1]{0:T(128)} %collective-permute-done.1, s32[1]{0:T(128)} %collective-permute-done, s32[1]{0:T(128)} %bitcast.1, s32[1]{0:T(128)} %bitcast.place_ref), kind=kLoop, calls=%fused_computation.7 | loop fusion | flops 12 | bytes 32 | tf_op jit(solution)/shard_map/stack | solution.py:314
  31.7 8.9 %collective-permute-done.2.refs_0_.refs_4_ = bf16[6,2,384,128]{3,2,1,0:T(8,128)(2,1)} collective-permute-done((bf16[6,2,384,128]{3,2,1,0:T(8,128)(2,1)}, bf16[6,2,384,128]{3,2,1,0:T(8,128)(2,1)}, u32[]{:S(2)}, u32[]{:S(2)}) %collective-permute-start.2) | collective-permute-done | bytes 1179680 | tf_op jit(solution)/shard_map/ppermute | solution.py:288
  40.6 5.1 %collective-permute-start.7 = (bf16[6,2,384,128]{3,2,1,0:T(8,128)(2,1)S(1)}, bf16[6,2,384,128]{3,2,1,0:T(8,128)(2,1)}, u32[]{:S(2)}, u32[]{:S(2)}) collective-permute-start(bf16[6,2,384,128]{3,2,1,0:T(8,128)(2,1)S(1)} %collective-permute-done.6.refs_1_.refs_2_.refs_6_.refs_4_), channel_id=1, source_target_pairs={{2,0},{4,2},{6,4},{8,6},{10,8},{12,10},{14,12},{16,14},{18,16},{20... | collective-permute-start | bytes 3538952 | tf_op jit(solution)/shard_map/ppermute | solution.py:288
  45.7 1.2 hand_on.1.place_ref
  46.9 3.0 %far1.1 = bf16[6,2,384,128]{3,2,1,0:T(8,128)(2,1)} custom-call(s32[4]{0:T(128)} %hand_on.1.place_ref, bf16[6,2,384,128]{3,2,1,0:T(8,128)(2,1)} %collective-permute-done.2.refs_0_.refs_4_, bf16[6,2,384,128]{3,2,1,0:T(8,128)(2,1)} %copy-done.1), custom_call_target="tpu_custom_call" | custom-call | bytes 1024 | tf_op jit(solution)/shard_map/far1/pallas_call | solution.py:95
  49.9 3.3 %collective-permute-start.12 = (bf16[6,2,384,128]{3,2,1,0:T(8,128)(2,1)}, bf16[6,2,384,128]{3,2,1,0:T(8,128)(2,1)}, u32[]{:S(2)}, u32[]{:S(2)}) collective-permute-start(bf16[6,2,384,128]{3,2,1,0:T(8,128)(2,1)} %far1.1), channel_id=1, source_target_pairs={{32,64},{64,32},{96,128},{128,96},{160,192},{192,160},{33,65},{65,... | collective-permute-start | bytes 3538952 | tf_op jit(solution)/shard_map/ppermute | solution.py:298
  53.8 12.1 %collective-permute-done.4.refs_0_.refs_5_ = bf16[6,2,384,128]{3,2,1,0:T(8,128)(2,1)} collective-permute-done((bf16[6,2,384,128]{3,2,1,0:T(8,128)(2,1)}, bf16[6,2,384,128]{3,2,1,0:T(8,128)(2,1)}, u32[]{:S(2)}, u32[]{:S(2)}) %collective-permute-start.4) | collective-permute-done | bytes 1179680 | tf_op jit(solution)/shard_map/ppermute | solution.py:288
  65.9 1.0 copy-done.2
  66.9 2.8 %near1.1 = bf16[6,2,384,128]{3,2,1,0:T(8,128)(2,1)} custom-call(s32[4]{0:T(128)} %hand_on.1.place_ref, bf16[6,2,384,128]{3,2,1,0:T(8,128)(2,1)} %collective-permute-done.4.refs_0_.refs_5_, bf16[6,2,384,128]{3,2,1,0:T(8,128)(2,1)} %copy-done.2), custom_call_target="tpu_custom_call" | custom-call | bytes 1024 | tf_op jit(solution)/shard_map/near1/pallas_call | solution.py:95
  69.9 0.6 reshape.17.refs_9_
  70.5 20.6 %collective-permute-done.3.refs_0_ = bf16[6,2,384,128]{3,2,1,0:T(8,128)(2,1)} collective-permute-done((bf16[6,2,384,128]{3,2,1,0:T(8,128)(2,1)}, bf16[6,2,384,128]{3,2,1,0:T(8,128)(2,1)}, u32[]{:S(2)}, u32[]{:S(2)}) %collective-permute-start.3) | collective-permute-done | bytes 1179680 | tf_op jit(solution)/shard_map/ppermute | solution.py:288
  91.1 1.5 %collective-permute-start.9 = (bf16[6,2,384,128]{3,2,1,0:T(8,128)(2,1)}, bf16[6,2,384,128]{3,2,1,0:T(8,128)(2,1)}, u32[]{:S(2)}, u32[]{:S(2)}) collective-permute-start(bf16[6,2,384,128]{3,2,1,0:T(8,128)(2,1)} %copy-done.2), channel_id=1, source_target_pairs={{2,0},{4,2},{6,4},{8,6},{10,8},{12,10},{14,12},{16,14},{18,16},{20... | collective-permute-start | bytes 3538952 | tf_op jit(solution)/shard_map/ppermute | solution.py:288
  92.6 2.8 %far2.1 = bf16[6,2,384,128]{3,2,1,0:T(8,128)(2,1)} custom-call(s32[4]{0:T(128)} %pad_add_fusion.x_ref.place_ref, bf16[6,2,384,128]{3,2,1,0:T(8,128)(2,1)} %collective-permute-done.3.refs_0_, bf16[6,2,384,128]{3,2,1,0:T(8,128)(2,1)} %collective-permute-done.7.refs_1_.refs_2_, bf16[6,2,384,128]{3,2,1,0:T(8,128)(2,1)} %copy-done.1), custom_call_target="tpu_custom_call" | custom-call | bytes 1024 | tf_op jit(solution)/shard_map/far2/pallas_call | solution.py:95
  95.4 3.6 %collective-permute-start.14 = (bf16[6,2,384,128]{3,2,1,0:T(8,128)(2,1)}, bf16[6,2,384,128]{3,2,1,0:T(8,128)(2,1)S(1)}, u32[]{:S(2)}, u32[]{:S(2)}) collective-permute-start(bf16[6,2,384,128]{3,2,1,0:T(8,128)(2,1)} %far2.1), channel_id=1, source_target_pairs={{32,64},{64,32},{96,128},{128,96},{160,192},{192,160},{33,65},{65,... | collective-permute-start | bytes 3538952 | tf_op jit(solution)/shard_map/ppermute | solution.py:298
  99.0 0.7 copy.10.s_ref
  99.7 17.3 %first.1.refs_8_ = f32[6,2,384,256]{3,2,1,0:T(8,128)} custom-call(s32[2,1]{1,0:T(2,128)} %copy.10.s_ref, s32[4]{0:T(128)} %pad_add_fusion.x_ref.place_ref, bf16[12,8,8,768]{3,2,1,0:T(8,128)(2,1)} %q_ref.3, bf16[6,2,384,128]{3,2,1,0:T(8,128)(2,1)} %bitcast.10, bf16[6,2,384,128]{3,2,1,0:T(8,128)(2,1)} %bitcast.14, ...), custom_call_target="tpu_custom_call" | custom-call | bytes 1024 | tf_op jit(solution)/shard_map/first/pallas_call | solution.py:265
  117.0 1.7 %collective-permute-done.9.refs_1_.refs_3_ = bf16[6,2,384,128]{3,2,1,0:T(8,128)(2,1)} collective-permute-done((bf16[6,2,384,128]{3,2,1,0:T(8,128)(2,1)}, bf16[6,2,384,128]{3,2,1,0:T(8,128)(2,1)}, u32[]{:S(2)}, u32[]{:S(2)}) %collective-permute-start.9) | collective-permute-done | bytes 1179680 | tf_op jit(solution)/shard_map/ppermute | solution.py:288
  118.8 2.8 %near2.1 = bf16[6,2,384,128]{3,2,1,0:T(8,128)(2,1)} custom-call(s32[4]{0:T(128)} %pad_add_fusion.x_ref.place_ref, bf16[6,2,384,128]{3,2,1,0:T(8,128)(2,1)} %copy-done.3, bf16[6,2,384,128]{3,2,1,0:T(8,128)(2,1)} %collective-permute-done.9.refs_1_.refs_3_, bf16[6,2,384,128]{3,2,1,0:T(8,128)(2,1)} %copy-done.2), custom_call_target="tpu_custom_call" | custom-call | bytes 1024 | tf_op jit(solution)/shard_map/near2/pallas_call | solution.py:95
  121.6 0.7 collective-permute-start.15
  122.2 2.7 %collective-permute-done.15.refs_7_ = bf16[6,2,384,128]{3,2,1,0:T(8,128)(2,1)S(1)} collective-permute-done((bf16[6,2,384,128]{3,2,1,0:T(8,128)(2,1)}, bf16[6,2,384,128]{3,2,1,0:T(8,128)(2,1)S(1)}, u32[]{:S(2)}, u32[]{:S(2)}) %collective-permute-start.15) | collective-permute-done | bytes 1179680 | tf_op jit(solution)/shard_map/ppermute | solution.py:303
  124.9 1.0 copy-done.5
  126.0 12.1 %last.1 = bf16[12,8,8,768]{3,2,1,0:T(8,128)(2,1)} custom-call(s32[2,1]{1,0:T(2,128)} %copy.10.s_ref, s32[4]{0:T(128)} %pad_add_fusion.x_ref.place_ref, bf16[12,8,8,768]{3,2,1,0:T(8,128)(2,1)} %q_ref.3, bf16[6,2,384,128]{3,2,1,0:T(8,128)(2,1)} %collective-permute-done.3.refs_0_, bf16[6,2,384,128]{3,2,1,0:T(8,128)(2,1)} %copy-done.3, ...), custom_call_target="tpu_custom_call" | custom-call | bytes 1024 | tf_op jit(solution)/shard_map/last/pallas_call | solution.py:265
  (35 shorter events, 0.9 us)
Async XLA Ops:
  0.0 53.4 %copy-start = (f32[256,768]{1,0:T(8,128)S(1)}, f32[256,768]{1,0:T(8,128)}, u32[]{:S(2)}) copy-start(f32[256,768]{1,0:T(8,128)} %param.11) | copy-start | bytes 2359300
  2.2 14.0 %copy-start.6 = (s32[2,1]{0,1:T(1,128)S(1)}, s32[2,1]{0,1:T(1,128)}, u32[]{:S(2)}) copy-start(s32[2,1]{0,1:T(1,128)} %param.9) | copy-start | bytes 28
  2.2 21.4 %collective-permute-start.10 = (bf16[6,2,384,128]{3,2,1,0:T(8,128)(2,1)}, bf16[6,2,384,128]{3,2,1,0:T(8,128)(2,1)}, u32[]{:S(2)}, u32[]{:S(2)}) collective-permute-start(bf16[6,2,384,128]{3,2,1,0:T(8,128)(2,1)} %bitcast.7), channel_id=1, source_target_pairs={{32,64},{64,32},{96,128},{128,96},{160,192},{192,160},{33,65},{65,... | collective-permute-start | bytes 3538952 | tf_op jit(solution)/shard_map/ppermute | solution.py:298
  5.7 34.9 %collective-permute-start.2 = (bf16[6,2,384,128]{3,2,1,0:T(8,128)(2,1)}, bf16[6,2,384,128]{3,2,1,0:T(8,128)(2,1)}, u32[]{:S(2)}, u32[]{:S(2)}) collective-permute-start(bf16[6,2,384,128]{3,2,1,0:T(8,128)(2,1)} %bitcast.8), channel_id=1, source_target_pairs={{30,0},{0,2},{2,4},{4,6},{6,8},{8,10},{10,12},{12,14},{14,16},{16,... | collective-permute-start | bytes 3538952 | tf_op jit(solution)/shard_map/ppermute | solution.py:288
  7.4 33.2 %collective-permute-start.6 = (bf16[6,2,384,128]{3,2,1,0:T(8,128)(2,1)}, bf16[6,2,384,128]{3,2,1,0:T(8,128)(2,1)S(1)}, u32[]{:S(2)}, u32[]{:S(2)}) collective-permute-start(bf16[6,2,384,128]{3,2,1,0:T(8,128)(2,1)} %bitcast.9), channel_id=1, source_target_pairs={{2,0},{4,2},{6,4},{8,6},{10,8},{12,10},{14,12},{16,14},{18,16},{20... | collective-permute-start | bytes 3538952 | tf_op jit(solution)/shard_map/ppermute | solution.py:288
  16.1 29.6 %collective-permute-start.11 = (bf16[6,2,384,128]{3,2,1,0:T(8,128)(2,1)}, bf16[6,2,384,128]{3,2,1,0:T(8,128)(2,1)}, u32[]{:S(2)}, u32[]{:S(2)}) collective-permute-start(bf16[6,2,384,128]{3,2,1,0:T(8,128)(2,1)} %bitcast.11), channel_id=1, source_target_pairs={{0,32},{32,0},{64,96},{96,64},{128,160},{160,128},{192,224},{224,1... | collective-permute-start | bytes 3538952 | tf_op jit(solution)/shard_map/ppermute | solution.py:303
  17.0 5.5 %collective-permute-start = (s32[1]{0:T(128)}, s32[1]{0:T(128)}, u32[]{:S(2)}, u32[]{:S(2)}) collective-permute-start(s32[1]{0:T(128)} %get-tuple-element.23), channel_id=1, source_target_pairs={{32,64},{64,32},{96,128},{128,96},{160,192},{192,160},{33,65},{65,... | collective-permute-start | bytes 20 | tf_op jit(solution)/shard_map/ppermute | solution.py:298
  22.4 1.2 collective-permute-start.1
  23.6 42.3 %collective-permute-start.4 = (bf16[6,2,384,128]{3,2,1,0:T(8,128)(2,1)}, bf16[6,2,384,128]{3,2,1,0:T(8,128)(2,1)}, u32[]{:S(2)}, u32[]{:S(2)}) collective-permute-start(bf16[6,2,384,128]{3,2,1,0:T(8,128)(2,1)} %bitcast.12), channel_id=1, source_target_pairs={{30,0},{0,2},{2,4},{4,6},{6,8},{8,10},{10,12},{12,14},{14,16},{16,... | collective-permute-start | bytes 3538952 | tf_op jit(solution)/shard_map/ppermute | solution.py:288
  23.6 42.3 %collective-permute-start.8 = (bf16[6,2,384,128]{3,2,1,0:T(8,128)(2,1)}, bf16[6,2,384,128]{3,2,1,0:T(8,128)(2,1)S(1)}, u32[]{:S(2)}, u32[]{:S(2)}) collective-permute-start(bf16[6,2,384,128]{3,2,1,0:T(8,128)(2,1)} %bitcast.13), channel_id=1, source_target_pairs={{2,0},{4,2},{6,4},{8,6},{10,8},{12,10},{14,12},{16,14},{18,16},{20... | collective-permute-start | bytes 3538952 | tf_op jit(solution)/shard_map/ppermute | solution.py:288
  40.6 50.5 %collective-permute-start.3 = (bf16[6,2,384,128]{3,2,1,0:T(8,128)(2,1)}, bf16[6,2,384,128]{3,2,1,0:T(8,128)(2,1)}, u32[]{:S(2)}, u32[]{:S(2)}) collective-permute-start(bf16[6,2,384,128]{3,2,1,0:T(8,128)(2,1)} %collective-permute-done.2.refs_0_.refs_4_), channel_id=1, source_target_pairs={{30,0},{0,2},{2,4},{4,6},{6,8},{8,10},{10,12},{12,14},{14,16},{16,... | collective-permute-start | bytes 3538952 | tf_op jit(solution)/shard_map/ppermute | solution.py:288
  40.6 6.3 %copy-start.1 = (bf16[6,2,384,128]{3,2,1,0:T(8,128)(2,1)}, bf16[6,2,384,128]{3,2,1,0:T(8,128)(2,1)S(1)}, u32[]{:S(2)}) copy-start(bf16[6,2,384,128]{3,2,1,0:T(8,128)(2,1)S(1)} %collective-permute-done.6.refs_1_.refs_2_.refs_6_.refs_4_) | copy-start | bytes 3538948
  40.6 52.0 %collective-permute-start.7 = (bf16[6,2,384,128]{3,2,1,0:T(8,128)(2,1)S(1)}, bf16[6,2,384,128]{3,2,1,0:T(8,128)(2,1)}, u32[]{:S(2)}, u32[]{:S(2)}) collective-permute-start(bf16[6,2,384,128]{3,2,1,0:T(8,128)(2,1)S(1)} %collective-permute-done.6.refs_1_.refs_2_.refs_6_.refs_4_), channel_id=1, source_target_pairs={{2,0},{4,2},{6,4},{8,6},{10,8},{12,10},{14,12},{16,14},{18,16},{20... | collective-permute-start | bytes 3538952 | tf_op jit(solution)/shard_map/ppermute | solution.py:288
  46.9 6.3 %copy-start.7 = (s32[2]{0:T(128)S(1)}, s32[2]{0:T(128)}, u32[]{:S(2)}) copy-start(s32[2]{0:T(128)} %param.10) | copy-start | bytes 28
  49.9 45.5 %collective-permute-start.12 = (bf16[6,2,384,128]{3,2,1,0:T(8,128)(2,1)}, bf16[6,2,384,128]{3,2,1,0:T(8,128)(2,1)}, u32[]{:S(2)}, u32[]{:S(2)}) collective-permute-start(bf16[6,2,384,128]{3,2,1,0:T(8,128)(2,1)} %far1.1), channel_id=1, source_target_pairs={{32,64},{64,32},{96,128},{128,96},{160,192},{192,160},{33,65},{65,... | collective-permute-start | bytes 3538952 | tf_op jit(solution)/shard_map/ppermute | solution.py:298
  65.9 1.0 copy-start.2
  69.8 29.9 %collective-permute-start.13 = (bf16[6,2,384,128]{3,2,1,0:T(8,128)(2,1)}, bf16[6,2,384,128]{3,2,1,0:T(8,128)(2,1)}, u32[]{:S(2)}, u32[]{:S(2)}) collective-permute-start(bf16[6,2,384,128]{3,2,1,0:T(8,128)(2,1)} %near1.1), channel_id=1, source_target_pairs={{0,32},{32,0},{64,96},{96,64},{128,160},{160,128},{192,224},{224,1... | collective-permute-start | bytes 3538952 | tf_op jit(solution)/shard_map/ppermute | solution.py:303
  70.5 46.5 %collective-permute-start.5 = (bf16[6,2,384,128]{3,2,1,0:T(8,128)(2,1)}, bf16[6,2,384,128]{3,2,1,0:T(8,128)(2,1)S(1)}, u32[]{:S(2)}, u32[]{:S(2)}) collective-permute-start(bf16[6,2,384,128]{3,2,1,0:T(8,128)(2,1)} %collective-permute-done.4.refs_0_.refs_5_), channel_id=1, source_target_pairs={{30,0},{0,2},{2,4},{4,6},{6,8},{8,10},{10,12},{12,14},{14,16},{16,... | collective-permute-start | bytes 3538952 | tf_op jit(solution)/shard_map/ppermute | solution.py:288
  91.1 27.7 %collective-permute-start.9 = (bf16[6,2,384,128]{3,2,1,0:T(8,128)(2,1)}, bf16[6,2,384,128]{3,2,1,0:T(8,128)(2,1)}, u32[]{:S(2)}, u32[]{:S(2)}) collective-permute-start(bf16[6,2,384,128]{3,2,1,0:T(8,128)(2,1)} %copy-done.2), channel_id=1, source_target_pairs={{2,0},{4,2},{6,4},{8,6},{10,8},{12,10},{14,12},{16,14},{18,16},{20... | collective-permute-start | bytes 3538952 | tf_op jit(solution)/shard_map/ppermute | solution.py:288
  95.4 26.1 %collective-permute-start.14 = (bf16[6,2,384,128]{3,2,1,0:T(8,128)(2,1)}, bf16[6,2,384,128]{3,2,1,0:T(8,128)(2,1)S(1)}, u32[]{:S(2)}, u32[]{:S(2)}) collective-permute-start(bf16[6,2,384,128]{3,2,1,0:T(8,128)(2,1)} %far2.1), channel_id=1, source_target_pairs={{32,64},{64,32},{96,128},{128,96},{160,192},{192,160},{33,65},{65,... | collective-permute-start | bytes 3538952 | tf_op jit(solution)/shard_map/ppermute | solution.py:298
  117.0 1.8 %copy-start.3 = (bf16[6,2,384,128]{3,2,1,0:T(8,128)(2,1)}, bf16[6,2,384,128]{3,2,1,0:T(8,128)(2,1)S(1)}, u32[]{:S(2)}) copy-start(bf16[6,2,384,128]{3,2,1,0:T(8,128)(2,1)S(1)} %collective-permute-done.5.refs_0_.refs_1_) | copy-start | bytes 3538948
  121.6 3.4 %copy-start.4 = (bf16[6,2,384,128]{3,2,1,0:T(8,128)(2,1)}, bf16[6,2,384,128]{3,2,1,0:T(8,128)(2,1)S(1)}, u32[]{:S(2)}) copy-start(bf16[6,2,384,128]{3,2,1,0:T(8,128)(2,1)S(1)} %collective-permute-done.14.refs_6_) | copy-start | bytes 3538948
  121.6 3.4 %collective-permute-start.15 = (bf16[6,2,384,128]{3,2,1,0:T(8,128)(2,1)}, bf16[6,2,384,128]{3,2,1,0:T(8,128)(2,1)S(1)}, u32[]{:S(2)}, u32[]{:S(2)}) collective-permute-start(bf16[6,2,384,128]{3,2,1,0:T(8,128)(2,1)} %near2.1), channel_id=1, source_target_pairs={{0,32},{32,0},{64,96},{96,64},{128,160},{160,128},{192,224},{224,1... | collective-permute-start | bytes 3538952 | tf_op jit(solution)/shard_map/ppermute | solution.py:303
  124.9 1.0 copy-start.5

commit v5 on v4

--- a/solution.py
+++ b/solution.py
@@ -331,10 +331,10 @@
 
     attn = functools.partial(attend, s=tile_offsets, place=place, q=query_field)
     far0, near0 = far_swap(xf), near_swap(xn)
-    later = hand_on(place, far0, near0)
+    later = hand_on(place, near0)
     far1 = far_swap(choose("far1", 1, 2, later, [rf, lf]))
     near1 = near_swap(choose("near1", 1, 3, later, [rn, ln]))
-    far2 = choose("far2", 2, 2, place, [r2f, l2f, lf])
+    far2 = choose("far2", 2, 2, hand_on(place, far0), [r2f, l2f, lf])
     far1, far2, gate_rows = lax.optimization_barrier((far1, far2, gate_rows))
     parts = [(0, [(xf, xn)], (far0, near0)), (1, [(rf, rn), (lf, ln)], (far1, near1))]
     state = attn("first", parts)

time: 139 us -> 136 us (0.978)
  waiting for transfers between devices: 50.3 us -> 39.6 us
  starting transfers between devices: 34.4 us -> 40.2 us
    ppermute x8, waiting for transfers between devices: 43.3 us -> 33.2 us  [from_behind(): lax.ppermute(block, 'lon', [((i - distance) % size, i) for i in range(siz...]
    ppermute x4, starting transfers between devices: 12.7 us -> 18.5 us  [far_swap(): return lax.ppermute(x, 'tm', route)]
  transfers between devices with their start and end apart: 16 -> 16, of which waited for: 7 -> 6; matrix products, arithmetic and copies ran while one was open for 3% -> 3% of each run, Pallas kernels for 23% -> 25%
where the time goes in v5:
time: 136 us; the launch traced here: 135 us
  Pallas kernels  47.6 us (35%)
  starting transfers between devices  40.2 us (30%)
  waiting for transfers between devices  39.6 us (29%)
  local copies, waits for them, and re-layouts  4.07 us (3%)
  other arithmetic  2.05 us (2%)
    ppermute x8, waiting for transfers between devices, from_behind(): lax.ppermute(block, 'lon', [((i - distance) % size, i) for i in range(siz...  33.2 us
    pallas_call x2, Pallas kernels, attend(): pl.pallas_call(functools.partial(attn_kernel, plan, 0, heads), out_shape=...  29.3 us
    ppermute x8, starting transfers between devices, from_behind(): lax.ppermute(block, 'lon', [((i - distance) % size, i) for i in range(siz...  19.7 us
    ppermute x4, starting transfers between devices, far_swap(): return lax.ppermute(x, 'tm', route)  18.5 us
    pallas_call x4, Pallas kernels, choose(): pl.pallas_call(functools.partial(choose_kernel, PICKS[phase], slot), out_...  11.4 us
    pallas_call x2, Pallas kernels, split(): pl.pallas_call(functools.partial(split_kernel, far), out_shape=jax.ShapeD...  4.42 us
    ppermute x4, waiting for transfers between devices, near_swap(): return lax.ppermute(x, 'tm', route)  4 us
    unnamed x17, local copies, waits for them, and re-layouts  2.74 us
  transfers between devices with their start and end apart: 16, of which 6 were waited for; matrix products, arithmetic and copies ran while one was open for 3% of the time, Pallas kernels for 25%

profile of v5, /device:TPU:17, one launch (start us, length us, event | category | flops | bytes accessed | tf_op | source)
XLA Modules:
  0.0 134.5 jit_solution(2190512972000491069)
XLA Ops:
  0.0 2.2 %split_far.1 = bf16[6,2,6,8,8,128]{5,4,3,2,1,0:T(8,128)(2,1)} custom-call(s32[1]{0:T(128)} %bitcast.place_ref, bf16[12,8,8,768]{3,2,1,0:T(8,128)(2,1)} %k_ref.3, bf16[12,8,8,768]{3,2,1,0:T(8,128)(2,1)} %v_ref.3), custom_call_target="tpu_custom_call" | custom-call | bytes 1024 | tf_op jit(solution)/shard_map/split_far/pallas_call | solution.py:45
  2.2 1.7 %collective-permute-start.2 = (bf16[6,2,384,128]{3,2,1,0:T(8,128)(2,1)}, bf16[6,2,384,128]{3,2,1,0:T(8,128)(2,1)}, u32[]{:S(2)}, u32[]{:S(2)}) collective-permute-start(bf16[6,2,384,128]{3,2,1,0:T(8,128)(2,1)} %bitcast.7), channel_id=1, source_target_pairs={{30,0},{0,2},{2,4},{4,6},{6,8},{8,10},{10,12},{12,14},{14,16},{16,... | collective-permute-start | bytes 3538952 | tf_op jit(solution)/shard_map/ppermute | solution.py:288
  3.9 6.5 %collective-permute-start.6 = (bf16[6,2,384,128]{3,2,1,0:T(8,128)(2,1)}, bf16[6,2,384,128]{3,2,1,0:T(8,128)(2,1)S(1)}, u32[]{:S(2)}, u32[]{:S(2)}) collective-permute-start(bf16[6,2,384,128]{3,2,1,0:T(8,128)(2,1)} %bitcast.8), channel_id=1, source_target_pairs={{2,0},{4,2},{6,4},{8,6},{10,8},{12,10},{14,12},{16,14},{18,16},{20... | collective-permute-start | bytes 3538952 | tf_op jit(solution)/shard_map/ppermute | solution.py:288
  10.4 2.2 %split_near.1 = bf16[6,2,6,8,8,128]{5,4,3,2,1,0:T(8,128)(2,1)} custom-call(s32[1]{0:T(128)} %bitcast.place_ref, bf16[12,8,8,768]{3,2,1,0:T(8,128)(2,1)} %k_ref.3, bf16[12,8,8,768]{3,2,1,0:T(8,128)(2,1)} %v_ref.3), custom_call_target="tpu_custom_call" | custom-call | bytes 1024 | tf_op jit(solution)/shard_map/split_near/pallas_call | solution.py:45
  12.7 1.0 collective-permute-start.11
  14.4 2.9 %collective-permute-start = (s32[1]{0:T(128)}, s32[1]{0:T(128)}, u32[]{:S(2)}, u32[]{:S(2)}) collective-permute-start(s32[1]{0:T(128)} %get-tuple-element.23), channel_id=1, source_target_pairs={{32,64},{64,32},{96,128},{128,96},{160,192},{192,160},{33,65},{65,... | collective-permute-start | bytes 20 | tf_op jit(solution)/shard_map/ppermute | solution.py:298
  17.3 2.4 %collective-permute-done = s32[1]{0:T(128)} collective-permute-done((s32[1]{0:T(128)}, s32[1]{0:T(128)}, u32[]{:S(2)}, u32[]{:S(2)}) %collective-permute-start) | collective-permute-done | bytes 36 | tf_op jit(solution)/shard_map/ppermute | solution.py:298
  19.7 1.3 collective-permute-done.1
  21.0 5.1 %collective-permute-start.8 = (bf16[6,2,384,128]{3,2,1,0:T(8,128)(2,1)}, bf16[6,2,384,128]{3,2,1,0:T(8,128)(2,1)S(1)}, u32[]{:S(2)}, u32[]{:S(2)}) collective-permute-start(bf16[6,2,384,128]{3,2,1,0:T(8,128)(2,1)} %bitcast.13), channel_id=1, source_target_pairs={{2,0},{4,2},{6,4},{8,6},{10,8},{12,10},{14,12},{16,14},{18,16},{20... | collective-permute-start | bytes 3538952 | tf_op jit(solution)/shard_map/ppermute | solution.py:288
  26.1 1.9 %pad_add_fusion.x_ref.place_ref = s32[4]{0:T(128)} fusion(s32[1]{0:T(128)} %collective-permute-done.1, s32[1]{0:T(128)} %collective-permute-done, s32[1]{0:T(128)} %bitcast.1, s32[1]{0:T(128)} %bitcast.place_ref), kind=kLoop, calls=%fused_computation.7 | loop fusion | flops 12 | bytes 32 | tf_op jit(solution)/shard_map/stack | solution.py:314
  28.0 8.3 %collective-permute-done.2.refs_0_.refs_4_ = bf16[6,2,384,128]{3,2,1,0:T(8,128)(2,1)} collective-permute-done((bf16[6,2,384,128]{3,2,1,0:T(8,128)(2,1)}, bf16[6,2,384,128]{3,2,1,0:T(8,128)(2,1)}, u32[]{:S(2)}, u32[]{:S(2)}) %collective-permute-start.2) | collective-permute-done | bytes 1179680 | tf_op jit(solution)/shard_map/ppermute | solution.py:288
  36.4 4.8 %collective-permute-start.10 = (bf16[6,2,384,128]{3,2,1,0:T(8,128)(2,1)}, bf16[6,2,384,128]{3,2,1,0:T(8,128)(2,1)}, u32[]{:S(2)}, u32[]{:S(2)}) collective-permute-start(bf16[6,2,384,128]{3,2,1,0:T(8,128)(2,1)} %bitcast.9), channel_id=1, source_target_pairs={{32,64},{64,32},{96,128},{128,96},{160,192},{192,160},{33,65},{65,... | collective-permute-start | bytes 3538952 | tf_op jit(solution)/shard_map/ppermute | solution.py:298
  41.3 5.1 %collective-permute-start.7 = (bf16[6,2,384,128]{3,2,1,0:T(8,128)(2,1)S(1)}, bf16[6,2,384,128]{3,2,1,0:T(8,128)(2,1)}, u32[]{:S(2)}, u32[]{:S(2)}) collective-permute-start(bf16[6,2,384,128]{3,2,1,0:T(8,128)(2,1)S(1)} %collective-permute-done.6.refs_1_.refs_2_.refs_6_.refs_4_), channel_id=1, source_target_pairs={{2,0},{4,2},{6,4},{8,6},{10,8},{12,10},{14,12},{16,14},{18,16},{20... | collective-permute-start | bytes 3538952 | tf_op jit(solution)/shard_map/ppermute | solution.py:288
  46.4 1.2 hand_on.2.place_ref
  47.6 3.0 %far1.1 = bf16[6,2,384,128]{3,2,1,0:T(8,128)(2,1)} custom-call(s32[4]{0:T(128)} %hand_on.2.place_ref, bf16[6,2,384,128]{3,2,1,0:T(8,128)(2,1)} %collective-permute-done.2.refs_0_.refs_4_, bf16[6,2,384,128]{3,2,1,0:T(8,128)(2,1)} %copy-done.1), custom_call_target="tpu_custom_call" | custom-call | bytes 1024 | tf_op jit(solution)/shard_map/far1/pallas_call | solution.py:95
  50.6 11.1 %collective-permute-done.4.refs_0_.refs_5_ = bf16[6,2,384,128]{3,2,1,0:T(8,128)(2,1)} collective-permute-done((bf16[6,2,384,128]{3,2,1,0:T(8,128)(2,1)}, bf16[6,2,384,128]{3,2,1,0:T(8,128)(2,1)}, u32[]{:S(2)}, u32[]{:S(2)}) %collective-permute-start.4) | collective-permute-done | bytes 1179680 | tf_op jit(solution)/shard_map/ppermute | solution.py:288
  61.6 4.8 %collective-permute-start.12 = (bf16[6,2,384,128]{3,2,1,0:T(8,128)(2,1)}, bf16[6,2,384,128]{3,2,1,0:T(8,128)(2,1)}, u32[]{:S(2)}, u32[]{:S(2)}) collective-permute-start(bf16[6,2,384,128]{3,2,1,0:T(8,128)(2,1)} %far1.1), channel_id=1, source_target_pairs={{32,64},{64,32},{96,128},{128,96},{160,192},{192,160},{33,65},{65,... | collective-permute-start | bytes 3538952 | tf_op jit(solution)/shard_map/ppermute | solution.py:298
  67.1 0.6 reshape.17.refs_9_
  67.7 1.0 copy-done.2
  68.8 2.8 %near1.1 = bf16[6,2,384,128]{3,2,1,0:T(8,128)(2,1)} custom-call(s32[4]{0:T(128)} %hand_on.2.place_ref, bf16[6,2,384,128]{3,2,1,0:T(8,128)(2,1)} %collective-permute-done.4.refs_0_.refs_5_, bf16[6,2,384,128]{3,2,1,0:T(8,128)(2,1)} %copy-done.2), custom_call_target="tpu_custom_call" | custom-call | bytes 1024 | tf_op jit(solution)/shard_map/near1/pallas_call | solution.py:95
  71.8 1.3 hand_on.3.place_ref
  73.1 13.8 %collective-permute-done.3.refs_0_ = bf16[6,2,384,128]{3,2,1,0:T(8,128)(2,1)} collective-permute-done((bf16[6,2,384,128]{3,2,1,0:T(8,128)(2,1)}, bf16[6,2,384,128]{3,2,1,0:T(8,128)(2,1)}, u32[]{:S(2)}, u32[]{:S(2)}) %collective-permute-start.3) | collective-permute-done | bytes 1179680 | tf_op jit(solution)/shard_map/ppermute | solution.py:288
  86.9 1.1 collective-permute-start.9
  88.1 2.8 %far2.1 = bf16[6,2,384,128]{3,2,1,0:T(8,128)(2,1)} custom-call(s32[4]{0:T(128)} %hand_on.3.place_ref, bf16[6,2,384,128]{3,2,1,0:T(8,128)(2,1)} %collective-permute-done.3.refs_0_, bf16[6,2,384,128]{3,2,1,0:T(8,128)(2,1)} %collective-permute-done.7.refs_1_.refs_2_, bf16[6,2,384,128]{3,2,1,0:T(8,128)(2,1)} %copy-done.1), custom_call_target="tpu_custom_call" | custom-call | bytes 1024 | tf_op jit(solution)/shard_map/far2/pallas_call | solution.py:95
  90.9 6.0 %collective-permute-start.14 = (bf16[6,2,384,128]{3,2,1,0:T(8,128)(2,1)}, bf16[6,2,384,128]{3,2,1,0:T(8,128)(2,1)S(1)}, u32[]{:S(2)}, u32[]{:S(2)}) collective-permute-start(bf16[6,2,384,128]{3,2,1,0:T(8,128)(2,1)} %far2.1), channel_id=1, source_target_pairs={{32,64},{64,32},{96,128},{128,96},{160,192},{192,160},{33,65},{65,... | collective-permute-start | bytes 3538952 | tf_op jit(solution)/shard_map/ppermute | solution.py:298
  96.9 0.7 copy.10.s_ref
  97.5 17.3 %first.1.refs_8_ = f32[6,2,384,256]{3,2,1,0:T(8,128)} custom-call(s32[2,1]{1,0:T(2,128)} %copy.10.s_ref, s32[4]{0:T(128)} %pad_add_fusion.x_ref.place_ref, bf16[12,8,8,768]{3,2,1,0:T(8,128)(2,1)} %q_ref.3, bf16[6,2,384,128]{3,2,1,0:T(8,128)(2,1)} %bitcast.10, bf16[6,2,384,128]{3,2,1,0:T(8,128)(2,1)} %bitcast.14, ...), custom_call_target="tpu_custom_call" | custom-call | bytes 1024 | tf_op jit(solution)/shard_map/first/pallas_call | solution.py:265
  114.8 2.8 %near2.1 = bf16[6,2,384,128]{3,2,1,0:T(8,128)(2,1)} custom-call(s32[4]{0:T(128)} %pad_add_fusion.x_ref.place_ref, bf16[6,2,384,128]{3,2,1,0:T(8,128)(2,1)} %collective-permute-done.5.refs_0_.refs_1_, bf16[6,2,384,128]{3,2,1,0:T(8,128)(2,1)} %collective-permute-done.9.refs_1_.refs_3_, bf16[6,2,384,128]{3,2,1,0:T(8,128)(2,1)} %copy-done.2), custom_call_target="tpu_custom_call" | custom-call | bytes 1024 | tf_op jit(solution)/shard_map/near2/pallas_call | solution.py:95
  117.7 0.9 collective-permute-start.15
  118.5 2.7 %collective-permute-done.15.refs_7_ = bf16[6,2,384,128]{3,2,1,0:T(8,128)(2,1)S(1)} collective-permute-done((bf16[6,2,384,128]{3,2,1,0:T(8,128)(2,1)}, bf16[6,2,384,128]{3,2,1,0:T(8,128)(2,1)S(1)}, u32[]{:S(2)}, u32[]{:S(2)}) %collective-permute-start.15) | collective-permute-done | bytes 1179680 | tf_op jit(solution)/shard_map/ppermute | solution.py:303
  121.2 1.0 copy-done.5
  122.3 12.1 %last.1 = bf16[12,8,8,768]{3,2,1,0:T(8,128)(2,1)} custom-call(s32[2,1]{1,0:T(2,128)} %copy.10.s_ref, s32[4]{0:T(128)} %pad_add_fusion.x_ref.place_ref, bf16[12,8,8,768]{3,2,1,0:T(8,128)(2,1)} %q_ref.3, bf16[6,2,384,128]{3,2,1,0:T(8,128)(2,1)} %collective-permute-done.3.refs_0_, bf16[6,2,384,128]{3,2,1,0:T(8,128)(2,1)} %collective-permute-done.5.refs_0_.refs_1_, ...), custom_call_target="tpu_custom_call" | custom-call | bytes 1024 | tf_op jit(solution)/shard_map/last/pallas_call | solution.py:265
  (36 shorter events, 1.6 us)
Async XLA Ops:
  0.0 66.6 %copy-start = (f32[256,768]{1,0:T(8,128)S(1)}, f32[256,768]{1,0:T(8,128)}, u32[]{:S(2)}) copy-start(f32[256,768]{1,0:T(8,128)} %param.11) | copy-start | bytes 2359300
  2.2 11.5 %copy-start.6 = (s32[2,1]{0,1:T(1,128)S(1)}, s32[2,1]{0,1:T(1,128)}, u32[]{:S(2)}) copy-start(s32[2,1]{0,1:T(1,128)} %param.9) | copy-start | bytes 28
  2.2 34.1 %collective-permute-start.2 = (bf16[6,2,384,128]{3,2,1,0:T(8,128)(2,1)}, bf16[6,2,384,128]{3,2,1,0:T(8,128)(2,1)}, u32[]{:S(2)}, u32[]{:S(2)}) collective-permute-start(bf16[6,2,384,128]{3,2,1,0:T(8,128)(2,1)} %bitcast.7), channel_id=1, source_target_pairs={{30,0},{0,2},{2,4},{4,6},{6,8},{8,10},{10,12},{12,14},{14,16},{16,... | collective-permute-start | bytes 3538952 | tf_op jit(solution)/shard_map/ppermute | solution.py:288
  3.9 37.3 %collective-permute-start.6 = (bf16[6,2,384,128]{3,2,1,0:T(8,128)(2,1)}, bf16[6,2,384,128]{3,2,1,0:T(8,128)(2,1)S(1)}, u32[]{:S(2)}, u32[]{:S(2)}) collective-permute-start(bf16[6,2,384,128]{3,2,1,0:T(8,128)(2,1)} %bitcast.8), channel_id=1, source_target_pairs={{2,0},{4,2},{6,4},{8,6},{10,8},{12,10},{14,12},{16,14},{18,16},{20... | collective-permute-start | bytes 3538952 | tf_op jit(solution)/shard_map/ppermute | solution.py:288
  12.7 28.7 %collective-permute-start.11 = (bf16[6,2,384,128]{3,2,1,0:T(8,128)(2,1)}, bf16[6,2,384,128]{3,2,1,0:T(8,128)(2,1)}, u32[]{:S(2)}, u32[]{:S(2)}) collective-permute-start(bf16[6,2,384,128]{3,2,1,0:T(8,128)(2,1)} %bitcast.11), channel_id=1, source_target_pairs={{0,32},{32,0},{64,96},{96,64},{128,160},{160,128},{192,224},{224,1... | collective-permute-start | bytes 3538952 | tf_op jit(solution)/shard_map/ppermute | solution.py:303
  13.7 47.9 %collective-permute-start.4 = (bf16[6,2,384,128]{3,2,1,0:T(8,128)(2,1)}, bf16[6,2,384,128]{3,2,1,0:T(8,128)(2,1)}, u32[]{:S(2)}, u32[]{:S(2)}) collective-permute-start(bf16[6,2,384,128]{3,2,1,0:T(8,128)(2,1)} %bitcast.12), channel_id=1, source_target_pairs={{30,0},{0,2},{2,4},{4,6},{6,8},{8,10},{10,12},{12,14},{14,16},{16,... | collective-permute-start | bytes 3538952 | tf_op jit(solution)/shard_map/ppermute | solution.py:288
  14.4 5.3 %collective-permute-start = (s32[1]{0:T(128)}, s32[1]{0:T(128)}, u32[]{:S(2)}, u32[]{:S(2)}) collective-permute-start(s32[1]{0:T(128)} %get-tuple-element.23), channel_id=1, source_target_pairs={{32,64},{64,32},{96,128},{128,96},{160,192},{192,160},{33,65},{65,... | collective-permute-start | bytes 20 | tf_op jit(solution)/shard_map/ppermute | solution.py:298
  19.7 1.3 collective-permute-start.1
  21.0 46.7 %collective-permute-start.8 = (bf16[6,2,384,128]{3,2,1,0:T(8,128)(2,1)}, bf16[6,2,384,128]{3,2,1,0:T(8,128)(2,1)S(1)}, u32[]{:S(2)}, u32[]{:S(2)}) collective-permute-start(bf16[6,2,384,128]{3,2,1,0:T(8,128)(2,1)} %bitcast.13), channel_id=1, source_target_pairs={{2,0},{4,2},{6,4},{8,6},{10,8},{12,10},{14,12},{16,14},{18,16},{20... | collective-permute-start | bytes 3538952 | tf_op jit(solution)/shard_map/ppermute | solution.py:288
  36.4 35.3 %collective-permute-start.10 = (bf16[6,2,384,128]{3,2,1,0:T(8,128)(2,1)}, bf16[6,2,384,128]{3,2,1,0:T(8,128)(2,1)}, u32[]{:S(2)}, u32[]{:S(2)}) collective-permute-start(bf16[6,2,384,128]{3,2,1,0:T(8,128)(2,1)} %bitcast.9), channel_id=1, source_target_pairs={{32,64},{64,32},{96,128},{128,96},{160,192},{192,160},{33,65},{65,... | collective-permute-start | bytes 3538952 | tf_op jit(solution)/shard_map/ppermute | solution.py:298
  41.2 6.4 %copy-start.1 = (bf16[6,2,384,128]{3,2,1,0:T(8,128)(2,1)}, bf16[6,2,384,128]{3,2,1,0:T(8,128)(2,1)S(1)}, u32[]{:S(2)}) copy-start(bf16[6,2,384,128]{3,2,1,0:T(8,128)(2,1)S(1)} %collective-permute-done.6.refs_1_.refs_2_.refs_6_.refs_4_) | copy-start | bytes 3538948
  41.2 45.7 %collective-permute-start.3 = (bf16[6,2,384,128]{3,2,1,0:T(8,128)(2,1)}, bf16[6,2,384,128]{3,2,1,0:T(8,128)(2,1)}, u32[]{:S(2)}, u32[]{:S(2)}) collective-permute-start(bf16[6,2,384,128]{3,2,1,0:T(8,128)(2,1)} %collective-permute-done.2.refs_0_.refs_4_), channel_id=1, source_target_pairs={{30,0},{0,2},{2,4},{4,6},{6,8},{8,10},{10,12},{12,14},{14,16},{16,... | collective-permute-start | bytes 3538952 | tf_op jit(solution)/shard_map/ppermute | solution.py:288
  41.3 46.7 %collective-permute-start.7 = (bf16[6,2,384,128]{3,2,1,0:T(8,128)(2,1)S(1)}, bf16[6,2,384,128]{3,2,1,0:T(8,128)(2,1)}, u32[]{:S(2)}, u32[]{:S(2)}) collective-permute-start(bf16[6,2,384,128]{3,2,1,0:T(8,128)(2,1)S(1)} %collective-permute-done.6.refs_1_.refs_2_.refs_6_.refs_4_), channel_id=1, source_target_pairs={{2,0},{4,2},{6,4},{8,6},{10,8},{12,10},{14,12},{16,14},{18,16},{20... | collective-permute-start | bytes 3538952 | tf_op jit(solution)/shard_map/ppermute | solution.py:288
  47.6 18.9 %copy-start.7 = (s32[2]{0:T(128)S(1)}, s32[2]{0:T(128)}, u32[]{:S(2)}) copy-start(s32[2]{0:T(128)} %param.10) | copy-start | bytes 28
  61.6 29.3 %collective-permute-start.12 = (bf16[6,2,384,128]{3,2,1,0:T(8,128)(2,1)}, bf16[6,2,384,128]{3,2,1,0:T(8,128)(2,1)}, u32[]{:S(2)}, u32[]{:S(2)}) collective-permute-start(bf16[6,2,384,128]{3,2,1,0:T(8,128)(2,1)} %far1.1), channel_id=1, source_target_pairs={{32,64},{64,32},{96,128},{128,96},{160,192},{192,160},{33,65},{65,... | collective-permute-start | bytes 3538952 | tf_op jit(solution)/shard_map/ppermute | solution.py:298
  67.7 1.0 copy-start.2
  71.6 15.3 %copy-start.3 = (bf16[6,2,384,128]{3,2,1,0:T(8,128)(2,1)S(1)}, bf16[6,2,384,128]{3,2,1,0:T(8,128)(2,1)}, u32[]{:S(2)}) copy-start(bf16[6,2,384,128]{3,2,1,0:T(8,128)(2,1)} %copy-done.2) | copy-start | bytes 3538948
  71.6 25.9 %collective-permute-start.13 = (bf16[6,2,384,128]{3,2,1,0:T(8,128)(2,1)}, bf16[6,2,384,128]{3,2,1,0:T(8,128)(2,1)}, u32[]{:S(2)}, u32[]{:S(2)}) collective-permute-start(bf16[6,2,384,128]{3,2,1,0:T(8,128)(2,1)} %near1.1), channel_id=1, source_target_pairs={{0,32},{32,0},{64,96},{96,64},{128,160},{160,128},{192,224},{224,1... | collective-permute-start | bytes 3538952 | tf_op jit(solution)/shard_map/ppermute | solution.py:303
  71.7 43.1 %collective-permute-start.5 = (bf16[6,2,384,128]{3,2,1,0:T(8,128)(2,1)}, bf16[6,2,384,128]{3,2,1,0:T(8,128)(2,1)}, u32[]{:S(2)}, u32[]{:S(2)}) collective-permute-start(bf16[6,2,384,128]{3,2,1,0:T(8,128)(2,1)} %collective-permute-done.4.refs_0_.refs_5_), channel_id=1, source_target_pairs={{30,0},{0,2},{2,4},{4,6},{6,8},{8,10},{10,12},{12,14},{14,16},{16,... | collective-permute-start | bytes 3538952 | tf_op jit(solution)/shard_map/ppermute | solution.py:288
  86.9 27.9 %collective-permute-start.9 = (bf16[6,2,384,128]{3,2,1,0:T(8,128)(2,1)S(1)}, bf16[6,2,384,128]{3,2,1,0:T(8,128)(2,1)}, u32[]{:S(2)}, u32[]{:S(2)}) collective-permute-start(bf16[6,2,384,128]{3,2,1,0:T(8,128)(2,1)S(1)} %copy-done.3), channel_id=1, source_target_pairs={{2,0},{4,2},{6,4},{8,6},{10,8},{12,10},{14,12},{16,14},{18,16},{20... | collective-permute-start | bytes 3538952 | tf_op jit(solution)/shard_map/ppermute | solution.py:288
  90.9 26.7 %collective-permute-start.14 = (bf16[6,2,384,128]{3,2,1,0:T(8,128)(2,1)}, bf16[6,2,384,128]{3,2,1,0:T(8,128)(2,1)S(1)}, u32[]{:S(2)}, u32[]{:S(2)}) collective-permute-start(bf16[6,2,384,128]{3,2,1,0:T(8,128)(2,1)} %far2.1), channel_id=1, source_target_pairs={{32,64},{64,32},{96,128},{128,96},{160,192},{192,160},{33,65},{65,... | collective-permute-start | bytes 3538952 | tf_op jit(solution)/shard_map/ppermute | solution.py:298
  117.7 3.6 %copy-start.4 = (bf16[6,2,384,128]{3,2,1,0:T(8,128)(2,1)}, bf16[6,2,384,128]{3,2,1,0:T(8,128)(2,1)S(1)}, u32[]{:S(2)}) copy-start(bf16[6,2,384,128]{3,2,1,0:T(8,128)(2,1)S(1)} %collective-permute-done.14.refs_6_) | copy-start | bytes 3538948
  117.7 3.6 %collective-permute-start.15 = (bf16[6,2,384,128]{3,2,1,0:T(8,128)(2,1)}, bf16[6,2,384,128]{3,2,1,0:T(8,128)(2,1)S(1)}, u32[]{:S(2)}, u32[]{:S(2)}) collective-permute-start(bf16[6,2,384,128]{3,2,1,0:T(8,128)(2,1)} %near2.1), channel_id=1, source_target_pairs={{0,32},{32,0},{64,96},{96,64},{128,160},{160,128},{192,224},{224,1... | collective-permute-start | bytes 3538952 | tf_op jit(solution)/shard_map/ppermute | solution.py:303
  121.2 1.0 copy-start.5

commit v6 on v5

--- a/solution.py
+++ b/solution.py
@@ -105,7 +105,7 @@
 
 
 def attn_kernel(plan, first, count, s_ref, place_ref, q_ref, *refs):
-    names, starts, finishes, phases = plan
+    names, starts, finishes, phases, units = plan
     blocks = [[(phase, b) for phase in phases for b in letters] for letters in ("EFN", "FNM")]
     ops = dict(zip(names, refs))
     out_ref, kv, qv, sc, top, si, so, ov, ksem, qsem, isem, osem = refs[len(refs) - 12:]
@@ -116,7 +116,7 @@
 
     def fill(i, slot):
         h = first + i
-        for u in range(2):
+        for u in units:
             for j, ((phase, sides), block) in enumerate(blocks[u]):
                 side = PICKS[phase](s_ref[tiles[u], 0])
                 to = kv.at[slot, :, base[u] + j]
@@ -139,7 +139,7 @@
             state_in(i, slot).start()
 
     def filled(i, slot):
-        for u in range(2):
+        for u in units:
             whole = kv.at[slot, :, pl.ds(base[u], len(blocks[u]))]
             pltpu.make_async_copy(whole, whole, ksem.at[slot, u]).wait()
         q_copy(i, slot).wait()
@@ -153,10 +153,15 @@
         return pltpu.make_async_copy(q_ref.at[:, :, :, lanes(i)], qv.at[slot], qsem.at[slot])
 
     def state_in(i, slot):
+        if len(units) == 1:
+            return pltpu.make_async_copy(ops["state"].at[first + i, units[0]], si.at[slot, units[0]], isem.at[slot])
         return pltpu.make_async_copy(ops["state"].at[first + i], si.at[slot], isem.at[slot])
 
     def result(i):
         slot = lax.rem(i, 2)
+        if len(units) == 1:
+            frames = pl.ds(tiles[units[0]] * TT, TT)
+            return pltpu.make_async_copy(ov.at[slot, frames], out_ref.at[frames, :, :, lanes(i)], osem.at[slot])
         if finishes:
             return pltpu.make_async_copy(ov.at[slot], out_ref.at[:, :, :, lanes(i)], osem.at[slot])
         return pltpu.make_async_copy(so.at[slot], out_ref.at[first + i], osem.at[slot])
@@ -221,10 +226,10 @@
         @pl.when(i >= 2)
         def _():
             result(i - 2).wait()
-        steps = [weigh(i, slot, u, sc.at[par, u], top.at[par, u]) for u in range(2)]
+        steps = [weigh(i, slot, u, sc.at[par, u], top.at[par, u]) for u in units]
         if not last:
             filled(i + 1, ahead)
-            steps += [scores(ahead, u, sc.at[1 - par, u], top.at[1 - par, u]) for u in range(2)]
+            steps += [scores(ahead, u, sc.at[1 - par, u], top.at[1 - par, u]) for u in units]
         both(*steps)
         result(i).start()
 
@@ -232,7 +237,7 @@
     if count > 1:
         fill(1, 1)
     filled(0, 0)
-    both(*[scores(0, u, sc.at[0, u], top.at[0, u]) for u in range(2)])
+    both(*[scores(0, u, sc.at[0, u], top.at[0, u]) for u in units])
 
     def pair(p, _):
         head(2 * p, 0, False)
@@ -246,18 +251,18 @@
         result(i).wait()
 
 
-def attend(name, parts, *, s, place, q, state=None, gate=None):
+def attend(name, parts, *, s, place, q, units=(0, 1), state=None, gate=None, prev=None):
     arrays, phases = {}, []
     for phase, columns, halos in parts:
         phases.append((phase, len(columns)))
         for c, (far, near) in enumerate(columns):
             arrays[f"F{phase}{c}"], arrays[f"N{phase}{c}"] = far, near
         arrays[f"E{phase}"], arrays[f"M{phase}"] = halos
-    arrays.update(state=state, gate=gate)
+    arrays.update(state=state, gate=gate, prev=prev)
     arrays = {n: x for n, x in arrays.items() if x is not None}
     names = tuple(arrays)
     heads = q.shape[3] // HD
-    plan = (names, state is None, gate is not None, phases)
+    plan = (names, state is None, gate is not None, phases, units)
     shape = jax.ShapeDtypeStruct((heads, 2, ROWS, 2 * HD), jnp.float32)
     if gate is not None:
         shape = jax.ShapeDtypeStruct(q.shape, q.dtype)
@@ -267,6 +272,7 @@
         out_shape=shape,
         in_specs=[SMEM, SMEM, ANY] + [VMEM if n == "gate" else ANY for n in names],
         out_specs=ANY,
+        input_output_aliases={} if prev is None else {3 + names.index("prev"): 0},
         scratch_shapes=[
             pltpu.VMEM((3, 2, 2 * blocks, ROWS, HD), jnp.bfloat16),
             pltpu.VMEM((3, 12, 8, 8, HD), jnp.bfloat16),
@@ -341,8 +347,10 @@
 
     r2n_, l2n_, state = lax.optimization_barrier((r2n, l2n, state))
     near2, far2 = lax.optimization_barrier((choose("near2", 2, 3, place, [r2n_, l2n_, ln]), far_swap(far2)))
-    parts = [(2, [(r2f, r2n), (l2f, l2n), (lf, ln)], (far2, near_swap(near2)))]
-    return attn("last", parts, state=state, gate=gate_rows)
+    columns = [(r2f, r2n), (l2f, l2n), (lf, ln)]
+    near2 = near_swap(near2)
+    out = attn("last_far", [(2, columns, (far2, None))], units=(0,), state=state, gate=gate_rows)
+    return attn("last_near", [(2, columns, (None, near2))], units=(1,), state=state, gate=gate_rows, prev=out)
 
 
 def solution(mesh):

time: 136 us -> 141 us (1.037)
  Pallas kernels: 47.6 us -> 54.3 us
  waiting for transfers between devices: 39.6 us -> 36.9 us
    pallas_call x2 -> x3, Pallas kernels: 29.3 us -> 35.9 us  [attend(): pl.pallas_call(functools.partial(attn_kernel, plan, 0, heads), out_shape=...]
    ppermute x4, waiting for transfers between devices: 4 us -> 1.32 us  [near_swap(): return lax.ppermute(x, 'tm', route)]
  transfers between devices with their start and end apart: 16 -> 16, of which waited for: 6 -> 5; matrix products, arithmetic and copies ran while one was open for 3% -> 3% of each run, Pallas kernels for 25% -> 31%
where the time goes in v6:
time: 141 us; the launch traced here: 139 us
  Pallas kernels  54.3 us (39%)
  starting transfers between devices  40.2 us (29%)
  waiting for transfers between devices  36.9 us (26%)
  local copies, waits for them, and re-layouts  4.27 us (3%)
  other arithmetic  2.05 us (1%)
    pallas_call x3, Pallas kernels, attend(): pl.pallas_call(functools.partial(attn_kernel, plan, 0, heads), out_shape=...  35.9 us
    ppermute x8, waiting for transfers between devices, from_behind(): lax.ppermute(block, 'lon', [((i - distance) % size, i) for i in range(siz...  33.2 us
    ppermute x8, starting transfers between devices, from_behind(): lax.ppermute(block, 'lon', [((i - distance) % size, i) for i in range(siz...  19.7 us
    ppermute x4, starting transfers between devices, far_swap(): return lax.ppermute(x, 'tm', route)  18.5 us
    pallas_call x4, Pallas kernels, choose(): pl.pallas_call(functools.partial(choose_kernel, PICKS[phase], slot), out_...  11.4 us
    pallas_call x2, Pallas kernels, split(): pl.pallas_call(functools.partial(split_kernel, far), out_shape=jax.ShapeD...  4.42 us
    unnamed x17, local copies, waits for them, and re-layouts  2.93 us
  transfers between devices with their start and end apart: 16, of which 5 were waited for; matrix products, arithmetic and copies ran while one was open for 3% of the time, Pallas kernels for 31%

profile of v6, /device:TPU:17, one launch (start us, length us, event | category | flops | bytes accessed | tf_op | source)
XLA Modules:
  0.0 138.6 jit_solution(10263370962997896564)
XLA Ops:
  0.0 2.2 %split_far.1 = bf16[6,2,6,8,8,128]{5,4,3,2,1,0:T(8,128)(2,1)} custom-call(s32[1]{0:T(128)} %bitcast.place_ref, bf16[12,8,8,768]{3,2,1,0:T(8,128)(2,1)} %k_ref.3, bf16[12,8,8,768]{3,2,1,0:T(8,128)(2,1)} %v_ref.3), custom_call_target="tpu_custom_call" | custom-call | bytes 1024 | tf_op jit(solution)/shard_map/split_far/pallas_call | solution.py:45
  2.2 1.7 %collective-permute-start.2 = (bf16[6,2,384,128]{3,2,1,0:T(8,128)(2,1)}, bf16[6,2,384,128]{3,2,1,0:T(8,128)(2,1)}, u32[]{:S(2)}, u32[]{:S(2)}) collective-permute-start(bf16[6,2,384,128]{3,2,1,0:T(8,128)(2,1)} %bitcast.7), channel_id=1, source_target_pairs={{30,0},{0,2},{2,4},{4,6},{6,8},{8,10},{10,12},{12,14},{14,16},{16,... | collective-permute-start | bytes 3538952 | tf_op jit(solution)/shard_map/ppermute | solution.py:294
  3.9 6.5 %collective-permute-start.6 = (bf16[6,2,384,128]{3,2,1,0:T(8,128)(2,1)}, bf16[6,2,384,128]{3,2,1,0:T(8,128)(2,1)S(1)}, u32[]{:S(2)}, u32[]{:S(2)}) collective-permute-start(bf16[6,2,384,128]{3,2,1,0:T(8,128)(2,1)} %bitcast.8), channel_id=1, source_target_pairs={{2,0},{4,2},{6,4},{8,6},{10,8},{12,10},{14,12},{16,14},{18,16},{20... | collective-permute-start | bytes 3538952 | tf_op jit(solution)/shard_map/ppermute | solution.py:294
  10.4 2.2 %split_near.1 = bf16[6,2,6,8,8,128]{5,4,3,2,1,0:T(8,128)(2,1)} custom-call(s32[1]{0:T(128)} %bitcast.place_ref, bf16[12,8,8,768]{3,2,1,0:T(8,128)(2,1)} %k_ref.3, bf16[12,8,8,768]{3,2,1,0:T(8,128)(2,1)} %v_ref.3), custom_call_target="tpu_custom_call" | custom-call | bytes 1024 | tf_op jit(solution)/shard_map/split_near/pallas_call | solution.py:45
  12.7 1.0 collective-permute-start.11
  14.4 2.9 %collective-permute-start = (s32[1]{0:T(128)}, s32[1]{0:T(128)}, u32[]{:S(2)}, u32[]{:S(2)}) collective-permute-start(s32[1]{0:T(128)} %get-tuple-element.23), channel_id=1, source_target_pairs={{32,64},{64,32},{96,128},{128,96},{160,192},{192,160},{33,65},{65,... | collective-permute-start | bytes 20 | tf_op jit(solution)/shard_map/ppermute | solution.py:304
  17.3 2.4 %collective-permute-done = s32[1]{0:T(128)} collective-permute-done((s32[1]{0:T(128)}, s32[1]{0:T(128)}, u32[]{:S(2)}, u32[]{:S(2)}) %collective-permute-start) | collective-permute-done | bytes 36 | tf_op jit(solution)/shard_map/ppermute | solution.py:304
  19.7 1.3 collective-permute-done.1
  21.0 5.1 %collective-permute-start.8 = (bf16[6,2,384,128]{3,2,1,0:T(8,128)(2,1)}, bf16[6,2,384,128]{3,2,1,0:T(8,128)(2,1)S(1)}, u32[]{:S(2)}, u32[]{:S(2)}) collective-permute-start(bf16[6,2,384,128]{3,2,1,0:T(8,128)(2,1)} %bitcast.13), channel_id=1, source_target_pairs={{2,0},{4,2},{6,4},{8,6},{10,8},{12,10},{14,12},{16,14},{18,16},{20... | collective-permute-start | bytes 3538952 | tf_op jit(solution)/shard_map/ppermute | solution.py:294
  26.1 1.9 %pad_add_fusion.x_ref.place_ref = s32[4]{0:T(128)} fusion(s32[1]{0:T(128)} %collective-permute-done.1, s32[1]{0:T(128)} %collective-permute-done, s32[1]{0:T(128)} %bitcast.1, s32[1]{0:T(128)} %bitcast.place_ref), kind=kLoop, calls=%fused_computation.7 | loop fusion | flops 12 | bytes 32 | tf_op jit(solution)/shard_map/stack | solution.py:320
  28.0 8.3 %collective-permute-done.2.refs_0_.refs_4_ = bf16[6,2,384,128]{3,2,1,0:T(8,128)(2,1)} collective-permute-done((bf16[6,2,384,128]{3,2,1,0:T(8,128)(2,1)}, bf16[6,2,384,128]{3,2,1,0:T(8,128)(2,1)}, u32[]{:S(2)}, u32[]{:S(2)}) %collective-permute-start.2) | collective-permute-done | bytes 1179680 | tf_op jit(solution)/shard_map/ppermute | solution.py:294
  36.4 4.8 %collective-permute-start.10 = (bf16[6,2,384,128]{3,2,1,0:T(8,128)(2,1)}, bf16[6,2,384,128]{3,2,1,0:T(8,128)(2,1)}, u32[]{:S(2)}, u32[]{:S(2)}) collective-permute-start(bf16[6,2,384,128]{3,2,1,0:T(8,128)(2,1)} %bitcast.9), channel_id=1, source_target_pairs={{32,64},{64,32},{96,128},{128,96},{160,192},{192,160},{33,65},{65,... | collective-permute-start | bytes 3538952 | tf_op jit(solution)/shard_map/ppermute | solution.py:304
  41.3 5.1 %collective-permute-start.7 = (bf16[6,2,384,128]{3,2,1,0:T(8,128)(2,1)S(1)}, bf16[6,2,384,128]{3,2,1,0:T(8,128)(2,1)}, u32[]{:S(2)}, u32[]{:S(2)}) collective-permute-start(bf16[6,2,384,128]{3,2,1,0:T(8,128)(2,1)S(1)} %collective-permute-done.6.refs_1_.refs_2_.refs_6_.refs_4_), channel_id=1, source_target_pairs={{2,0},{4,2},{6,4},{8,6},{10,8},{12,10},{14,12},{16,14},{18,16},{20... | collective-permute-start | bytes 3538952 | tf_op jit(solution)/shard_map/ppermute | solution.py:294
  46.4 1.2 hand_on.2.place_ref
  47.6 3.0 %far1.1 = bf16[6,2,384,128]{3,2,1,0:T(8,128)(2,1)} custom-call(s32[4]{0:T(128)} %hand_on.2.place_ref, bf16[6,2,384,128]{3,2,1,0:T(8,128)(2,1)} %collective-permute-done.2.refs_0_.refs_4_, bf16[6,2,384,128]{3,2,1,0:T(8,128)(2,1)} %copy-done.1), custom_call_target="tpu_custom_call" | custom-call | bytes 1024 | tf_op jit(solution)/shard_map/far1/pallas_call | solution.py:95
  50.6 11.1 %collective-permute-done.4.refs_0_.refs_5_ = bf16[6,2,384,128]{3,2,1,0:T(8,128)(2,1)} collective-permute-done((bf16[6,2,384,128]{3,2,1,0:T(8,128)(2,1)}, bf16[6,2,384,128]{3,2,1,0:T(8,128)(2,1)}, u32[]{:S(2)}, u32[]{:S(2)}) %collective-permute-start.4) | collective-permute-done | bytes 1179680 | tf_op jit(solution)/shard_map/ppermute | solution.py:294
  61.6 4.8 %collective-permute-start.12 = (bf16[6,2,384,128]{3,2,1,0:T(8,128)(2,1)}, bf16[6,2,384,128]{3,2,1,0:T(8,128)(2,1)}, u32[]{:S(2)}, u32[]{:S(2)}) collective-permute-start(bf16[6,2,384,128]{3,2,1,0:T(8,128)(2,1)} %far1.1), channel_id=1, source_target_pairs={{32,64},{64,32},{96,128},{128,96},{160,192},{192,160},{33,65},{65,... | collective-permute-start | bytes 3538952 | tf_op jit(solution)/shard_map/ppermute | solution.py:304
  67.1 0.6 reshape.17.refs_8_
  67.7 1.0 copy-done.2
  68.8 2.8 %near1.1 = bf16[6,2,384,128]{3,2,1,0:T(8,128)(2,1)} custom-call(s32[4]{0:T(128)} %hand_on.2.place_ref, bf16[6,2,384,128]{3,2,1,0:T(8,128)(2,1)} %collective-permute-done.4.refs_0_.refs_5_, bf16[6,2,384,128]{3,2,1,0:T(8,128)(2,1)} %copy-done.2), custom_call_target="tpu_custom_call" | custom-call | bytes 1024 | tf_op jit(solution)/shard_map/near1/pallas_call | solution.py:95
  71.8 1.3 hand_on.3.place_ref
  73.1 13.8 %collective-permute-done.3.refs_0_ = bf16[6,2,384,128]{3,2,1,0:T(8,128)(2,1)} collective-permute-done((bf16[6,2,384,128]{3,2,1,0:T(8,128)(2,1)}, bf16[6,2,384,128]{3,2,1,0:T(8,128)(2,1)}, u32[]{:S(2)}, u32[]{:S(2)}) %collective-permute-start.3) | collective-permute-done | bytes 1179680 | tf_op jit(solution)/shard_map/ppermute | solution.py:294
  86.9 1.1 collective-permute-start.9
  88.1 2.8 %far2.1 = bf16[6,2,384,128]{3,2,1,0:T(8,128)(2,1)} custom-call(s32[4]{0:T(128)} %hand_on.3.place_ref, bf16[6,2,384,128]{3,2,1,0:T(8,128)(2,1)} %collective-permute-done.3.refs_0_, bf16[6,2,384,128]{3,2,1,0:T(8,128)(2,1)} %collective-permute-done.7.refs_1_.refs_2_, bf16[6,2,384,128]{3,2,1,0:T(8,128)(2,1)} %copy-done.1), custom_call_target="tpu_custom_call" | custom-call | bytes 1024 | tf_op jit(solution)/shard_map/far2/pallas_call | solution.py:95
  90.9 6.0 %collective-permute-start.14 = (bf16[6,2,384,128]{3,2,1,0:T(8,128)(2,1)}, bf16[6,2,384,128]{3,2,1,0:T(8,128)(2,1)S(1)}, u32[]{:S(2)}, u32[]{:S(2)}) collective-permute-start(bf16[6,2,384,128]{3,2,1,0:T(8,128)(2,1)} %far2.1), channel_id=1, source_target_pairs={{32,64},{64,32},{96,128},{128,96},{160,192},{192,160},{33,65},{65,... | collective-permute-start | bytes 3538952 | tf_op jit(solution)/shard_map/ppermute | solution.py:304
  96.9 0.7 copy.13.s_ref
  97.5 17.3 %first.1.refs_7_ = f32[6,2,384,256]{3,2,1,0:T(8,128)} custom-call(s32[2,1]{1,0:T(2,128)} %copy.13.s_ref, s32[4]{0:T(128)} %pad_add_fusion.x_ref.place_ref, bf16[12,8,8,768]{3,2,1,0:T(8,128)(2,1)} %q_ref.5, bf16[6,2,384,128]{3,2,1,0:T(8,128)(2,1)} %bitcast.10, bf16[6,2,384,128]{3,2,1,0:T(8,128)(2,1)} %bitcast.14, ...), custom_call_target="tpu_custom_call" | custom-call | bytes 1024 | tf_op jit(solution)/shard_map/first/pallas_call | solution.py:270
  114.9 2.8 %near2.1 = bf16[6,2,384,128]{3,2,1,0:T(8,128)(2,1)} custom-call(s32[4]{0:T(128)} %pad_add_fusion.x_ref.place_ref, bf16[6,2,384,128]{3,2,1,0:T(8,128)(2,1)} %collective-permute-done.5.refs_0_.refs_1_, bf16[6,2,384,128]{3,2,1,0:T(8,128)(2,1)} %collective-permute-done.9.refs_1_.refs_3_, bf16[6,2,384,128]{3,2,1,0:T(8,128)(2,1)} %copy-done.2), custom_call_target="tpu_custom_call" | custom-call | bytes 1024 | tf_op jit(solution)/shard_map/near2/pallas_call | solution.py:95
  117.7 0.9 collective-permute-start.15
  118.7 9.3 %last_far.1.refs_9_ = bf16[12,8,8,768]{3,2,1,0:T(8,128)(2,1)} custom-call(s32[2,1]{1,0:T(2,128)} %copy.13.s_ref, s32[4]{0:T(128)} %pad_add_fusion.x_ref.place_ref, bf16[12,8,8,768]{3,2,1,0:T(8,128)(2,1)} %q_ref.5, bf16[6,2,384,128]{3,2,1,0:T(8,128)(2,1)} %collective-permute-done.3.refs_0_, bf16[6,2,384,128]{3,2,1,0:T(8,128)(2,1)} %collective-permute-done.5.refs_0_.refs_1_, ...), custom_call_target="tpu_custom_call" | custom-call | bytes 1024 | tf_op jit(solution)/shard_map/last_far/pallas_call | solution.py:270
  128.1 1.0 copy-done.5
  129.1 9.3 %last_near.1 = bf16[12,8,8,768]{3,2,1,0:T(8,128)(2,1)} custom-call(s32[2,1]{1,0:T(2,128)} %copy.13.s_ref, s32[4]{0:T(128)} %pad_add_fusion.x_ref.place_ref, bf16[12,8,8,768]{3,2,1,0:T(8,128)(2,1)} %q_ref.5, bf16[6,2,384,128]{3,2,1,0:T(8,128)(2,1)} %collective-permute-done.3.refs_0_, ...), custom_call_target="tpu_custom_call", output_to_operand_aliasing={{}: (12, {})} | custom-call | bytes 1024 | tf_op jit(solution)/shard_map/last_near/pallas_call | solution.py:270
  (37 shorter events, 1.8 us)
Async XLA Ops:
  0.0 66.6 %copy-start = (f32[256,768]{1,0:T(8,128)S(1)}, f32[256,768]{1,0:T(8,128)}, u32[]{:S(2)}) copy-start(f32[256,768]{1,0:T(8,128)} %param.11) | copy-start | bytes 2359300
  2.2 11.5 %copy-start.6 = (s32[2,1]{0,1:T(1,128)S(1)}, s32[2,1]{0,1:T(1,128)}, u32[]{:S(2)}) copy-start(s32[2,1]{0,1:T(1,128)} %param.9) | copy-start | bytes 28
  2.2 34.1 %collective-permute-start.2 = (bf16[6,2,384,128]{3,2,1,0:T(8,128)(2,1)}, bf16[6,2,384,128]{3,2,1,0:T(8,128)(2,1)}, u32[]{:S(2)}, u32[]{:S(2)}) collective-permute-start(bf16[6,2,384,128]{3,2,1,0:T(8,128)(2,1)} %bitcast.7), channel_id=1, source_target_pairs={{30,0},{0,2},{2,4},{4,6},{6,8},{8,10},{10,12},{12,14},{14,16},{16,... | collective-permute-start | bytes 3538952 | tf_op jit(solution)/shard_map/ppermute | solution.py:294
  3.9 37.3 %collective-permute-start.6 = (bf16[6,2,384,128]{3,2,1,0:T(8,128)(2,1)}, bf16[6,2,384,128]{3,2,1,0:T(8,128)(2,1)S(1)}, u32[]{:S(2)}, u32[]{:S(2)}) collective-permute-start(bf16[6,2,384,128]{3,2,1,0:T(8,128)(2,1)} %bitcast.8), channel_id=1, source_target_pairs={{2,0},{4,2},{6,4},{8,6},{10,8},{12,10},{14,12},{16,14},{18,16},{20... | collective-permute-start | bytes 3538952 | tf_op jit(solution)/shard_map/ppermute | solution.py:294
  12.7 28.7 %collective-permute-start.11 = (bf16[6,2,384,128]{3,2,1,0:T(8,128)(2,1)}, bf16[6,2,384,128]{3,2,1,0:T(8,128)(2,1)}, u32[]{:S(2)}, u32[]{:S(2)}) collective-permute-start(bf16[6,2,384,128]{3,2,1,0:T(8,128)(2,1)} %bitcast.11), channel_id=1, source_target_pairs={{0,32},{32,0},{64,96},{96,64},{128,160},{160,128},{192,224},{224,1... | collective-permute-start | bytes 3538952 | tf_op jit(solution)/shard_map/ppermute | solution.py:309
  13.7 47.9 %collective-permute-start.4 = (bf16[6,2,384,128]{3,2,1,0:T(8,128)(2,1)}, bf16[6,2,384,128]{3,2,1,0:T(8,128)(2,1)}, u32[]{:S(2)}, u32[]{:S(2)}) collective-permute-start(bf16[6,2,384,128]{3,2,1,0:T(8,128)(2,1)} %bitcast.12), channel_id=1, source_target_pairs={{30,0},{0,2},{2,4},{4,6},{6,8},{8,10},{10,12},{12,14},{14,16},{16,... | collective-permute-start | bytes 3538952 | tf_op jit(solution)/shard_map/ppermute | solution.py:294
  14.4 5.3 %collective-permute-start = (s32[1]{0:T(128)}, s32[1]{0:T(128)}, u32[]{:S(2)}, u32[]{:S(2)}) collective-permute-start(s32[1]{0:T(128)} %get-tuple-element.23), channel_id=1, source_target_pairs={{32,64},{64,32},{96,128},{128,96},{160,192},{192,160},{33,65},{65,... | collective-permute-start | bytes 20 | tf_op jit(solution)/shard_map/ppermute | solution.py:304
  19.7 1.3 collective-permute-start.1
  21.0 46.7 %collective-permute-start.8 = (bf16[6,2,384,128]{3,2,1,0:T(8,128)(2,1)}, bf16[6,2,384,128]{3,2,1,0:T(8,128)(2,1)S(1)}, u32[]{:S(2)}, u32[]{:S(2)}) collective-permute-start(bf16[6,2,384,128]{3,2,1,0:T(8,128)(2,1)} %bitcast.13), channel_id=1, source_target_pairs={{2,0},{4,2},{6,4},{8,6},{10,8},{12,10},{14,12},{16,14},{18,16},{20... | collective-permute-start | bytes 3538952 | tf_op jit(solution)/shard_map/ppermute | solution.py:294
  36.4 35.3 %collective-permute-start.10 = (bf16[6,2,384,128]{3,2,1,0:T(8,128)(2,1)}, bf16[6,2,384,128]{3,2,1,0:T(8,128)(2,1)}, u32[]{:S(2)}, u32[]{:S(2)}) collective-permute-start(bf16[6,2,384,128]{3,2,1,0:T(8,128)(2,1)} %bitcast.9), channel_id=1, source_target_pairs={{32,64},{64,32},{96,128},{128,96},{160,192},{192,160},{33,65},{65,... | collective-permute-start | bytes 3538952 | tf_op jit(solution)/shard_map/ppermute | solution.py:304
  41.2 6.4 %copy-start.1 = (bf16[6,2,384,128]{3,2,1,0:T(8,128)(2,1)}, bf16[6,2,384,128]{3,2,1,0:T(8,128)(2,1)S(1)}, u32[]{:S(2)}) copy-start(bf16[6,2,384,128]{3,2,1,0:T(8,128)(2,1)S(1)} %collective-permute-done.6.refs_1_.refs_2_.refs_6_.refs_4_) | copy-start | bytes 3538948
  41.2 45.7 %collective-permute-start.3 = (bf16[6,2,384,128]{3,2,1,0:T(8,128)(2,1)}, bf16[6,2,384,128]{3,2,1,0:T(8,128)(2,1)}, u32[]{:S(2)}, u32[]{:S(2)}) collective-permute-start(bf16[6,2,384,128]{3,2,1,0:T(8,128)(2,1)} %collective-permute-done.2.refs_0_.refs_4_), channel_id=1, source_target_pairs={{30,0},{0,2},{2,4},{4,6},{6,8},{8,10},{10,12},{12,14},{14,16},{16,... | collective-permute-start | bytes 3538952 | tf_op jit(solution)/shard_map/ppermute | solution.py:294
  41.3 46.7 %collective-permute-start.7 = (bf16[6,2,384,128]{3,2,1,0:T(8,128)(2,1)S(1)}, bf16[6,2,384,128]{3,2,1,0:T(8,128)(2,1)}, u32[]{:S(2)}, u32[]{:S(2)}) collective-permute-start(bf16[6,2,384,128]{3,2,1,0:T(8,128)(2,1)S(1)} %collective-permute-done.6.refs_1_.refs_2_.refs_6_.refs_4_), channel_id=1, source_target_pairs={{2,0},{4,2},{6,4},{8,6},{10,8},{12,10},{14,12},{16,14},{18,16},{20... | collective-permute-start | bytes 3538952 | tf_op jit(solution)/shard_map/ppermute | solution.py:294
  47.6 18.9 %copy-start.7 = (s32[2]{0:T(128)S(1)}, s32[2]{0:T(128)}, u32[]{:S(2)}) copy-start(s32[2]{0:T(128)} %param.10) | copy-start | bytes 28
  61.6 29.3 %collective-permute-start.12 = (bf16[6,2,384,128]{3,2,1,0:T(8,128)(2,1)}, bf16[6,2,384,128]{3,2,1,0:T(8,128)(2,1)}, u32[]{:S(2)}, u32[]{:S(2)}) collective-permute-start(bf16[6,2,384,128]{3,2,1,0:T(8,128)(2,1)} %far1.1), channel_id=1, source_target_pairs={{32,64},{64,32},{96,128},{128,96},{160,192},{192,160},{33,65},{65,... | collective-permute-start | bytes 3538952 | tf_op jit(solution)/shard_map/ppermute | solution.py:304
  67.7 1.0 copy-start.2
  71.6 15.3 %copy-start.3 = (bf16[6,2,384,128]{3,2,1,0:T(8,128)(2,1)S(1)}, bf16[6,2,384,128]{3,2,1,0:T(8,128)(2,1)}, u32[]{:S(2)}) copy-start(bf16[6,2,384,128]{3,2,1,0:T(8,128)(2,1)} %copy-done.2) | copy-start | bytes 3538948
  71.6 25.9 %collective-permute-start.13 = (bf16[6,2,384,128]{3,2,1,0:T(8,128)(2,1)}, bf16[6,2,384,128]{3,2,1,0:T(8,128)(2,1)}, u32[]{:S(2)}, u32[]{:S(2)}) collective-permute-start(bf16[6,2,384,128]{3,2,1,0:T(8,128)(2,1)} %near1.1), channel_id=1, source_target_pairs={{0,32},{32,0},{64,96},{96,64},{128,160},{160,128},{192,224},{224,1... | collective-permute-start | bytes 3538952 | tf_op jit(solution)/shard_map/ppermute | solution.py:309
  71.7 43.1 %collective-permute-start.5 = (bf16[6,2,384,128]{3,2,1,0:T(8,128)(2,1)}, bf16[6,2,384,128]{3,2,1,0:T(8,128)(2,1)}, u32[]{:S(2)}, u32[]{:S(2)}) collective-permute-start(bf16[6,2,384,128]{3,2,1,0:T(8,128)(2,1)} %collective-permute-done.4.refs_0_.refs_5_), channel_id=1, source_target_pairs={{30,0},{0,2},{2,4},{4,6},{6,8},{8,10},{10,12},{12,14},{14,16},{16,... | collective-permute-start | bytes 3538952 | tf_op jit(solution)/shard_map/ppermute | solution.py:294
  86.9 27.9 %collective-permute-start.9 = (bf16[6,2,384,128]{3,2,1,0:T(8,128)(2,1)S(1)}, bf16[6,2,384,128]{3,2,1,0:T(8,128)(2,1)}, u32[]{:S(2)}, u32[]{:S(2)}) collective-permute-start(bf16[6,2,384,128]{3,2,1,0:T(8,128)(2,1)S(1)} %copy-done.3), channel_id=1, source_target_pairs={{2,0},{4,2},{6,4},{8,6},{10,8},{12,10},{14,12},{16,14},{18,16},{20... | collective-permute-start | bytes 3538952 | tf_op jit(solution)/shard_map/ppermute | solution.py:294
  90.9 26.8 %collective-permute-start.14 = (bf16[6,2,384,128]{3,2,1,0:T(8,128)(2,1)}, bf16[6,2,384,128]{3,2,1,0:T(8,128)(2,1)S(1)}, u32[]{:S(2)}, u32[]{:S(2)}) collective-permute-start(bf16[6,2,384,128]{3,2,1,0:T(8,128)(2,1)} %far2.1), channel_id=1, source_target_pairs={{32,64},{64,32},{96,128},{128,96},{160,192},{192,160},{33,65},{65,... | collective-permute-start | bytes 3538952 | tf_op jit(solution)/shard_map/ppermute | solution.py:304
  117.7 1.0 copy-start.4
  117.7 10.4 %collective-permute-start.15 = (bf16[6,2,384,128]{3,2,1,0:T(8,128)(2,1)}, bf16[6,2,384,128]{3,2,1,0:T(8,128)(2,1)S(1)}, u32[]{:S(2)}, u32[]{:S(2)}) collective-permute-start(bf16[6,2,384,128]{3,2,1,0:T(8,128)(2,1)} %near2.1), channel_id=1, source_target_pairs={{0,32},{32,0},{64,96},{96,64},{128,160},{160,128},{192,224},{224,1... | collective-permute-start | bytes 3538952 | tf_op jit(solution)/shard_map/ppermute | solution.py:309
  128.1 1.0 copy-start.5

commit v7 on v5

--- a/solution.py
+++ b/solution.py
@@ -211,20 +211,22 @@
         for _ in itertools.zip_longest(*steps):
             pass
 
-    def head(i, par, last):
+    def head(i, par):
         slot, ahead = lax.rem(i, 3), lax.rem(i + 1, 3)
-        if not last:
-            @pl.when(i + 2 < count)
-            def _():
-                fill(i + 2, lax.rem(i + 2, 3))
+
+        @pl.when(i + 2 < count)
+        def _():
+            fill(i + 2, lax.rem(i + 2, 3))
 
         @pl.when(i >= 2)
         def _():
             result(i - 2).wait()
         steps = [weigh(i, slot, u, sc.at[par, u], top.at[par, u]) for u in range(2)]
-        if not last:
+
+        @pl.when(i + 1 < count)
+        def _():
             filled(i + 1, ahead)
-            steps += [scores(ahead, u, sc.at[1 - par, u], top.at[1 - par, u]) for u in range(2)]
+        steps += [scores(ahead, u, sc.at[1 - par, u], top.at[1 - par, u]) for u in range(2)]
         both(*steps)
         result(i).start()
 
@@ -235,13 +237,10 @@
     both(*[scores(0, u, sc.at[0, u], top.at[0, u]) for u in range(2)])
 
     def pair(p, _):
-        head(2 * p, 0, False)
-        head(2 * p + 1, 1, False)
+        head(2 * p, 0)
+        head(2 * p + 1, 1)
         return 0
-    lax.fori_loop(0, (count - 1) // 2, pair, 0)
-    if count % 2 == 0:
-        head(jnp.int32(count - 2), 0, False)
-    head(jnp.int32(count - 1), (count - 1) % 2, True)
+    lax.fori_loop(0, count // 2, pair, 0)
     for i in range(max(0, count - 2), count):
         result(i).wait()
 

time: 136 us -> 136 us (level)
  no operation moved by 1% of the time
where the time goes in v7:
time: 136 us; the launch traced here: 135 us
  Pallas kernels  48.1 us (35%)
  starting transfers between devices  39.7 us (29%)
  waiting for transfers between devices  39.7 us (29%)
  local copies, waits for them, and re-layouts  4.07 us (3%)
  other arithmetic  2.05 us (2%)
    ppermute x8, waiting for transfers between devices, from_behind(): lax.ppermute(block, 'lon', [((i - distance) % size, i) for i in range(siz...  33.2 us
    pallas_call x2, Pallas kernels, attend(): pl.pallas_call(functools.partial(attn_kernel, plan, 0, heads), out_shape=...  29.8 us
    ppermute x8, starting transfers between devices, from_behind(): lax.ppermute(block, 'lon', [((i - distance) % size, i) for i in range(siz...  19.7 us
    ppermute x4, starting transfers between devices, far_swap(): return lax.ppermute(x, 'tm', route)  18.5 us
    pallas_call x4, Pallas kernels, choose(): pl.pallas_call(functools.partial(choose_kernel, PICKS[phase], slot), out_...  11.4 us
    pallas_call x2, Pallas kernels, split(): pl.pallas_call(functools.partial(split_kernel, far), out_shape=jax.ShapeD...  4.42 us
    ppermute x4, waiting for transfers between devices, near_swap(): return lax.ppermute(x, 'tm', route)  4.07 us
    unnamed x17, local copies, waits for them, and re-layouts  2.74 us
  transfers between devices with their start and end apart: 16, of which 6 were waited for; matrix products, arithmetic and copies ran while one was open for 3% of the time, Pallas kernels for 25%

profile of v7, /device:TPU:17, one launch (start us, length us, event | category | flops | bytes accessed | tf_op | source)
XLA Modules:
  0.0 134.5 jit_solution(17798324825181503379)
XLA Ops:
  0.0 2.2 %split_far.1 = bf16[6,2,6,8,8,128]{5,4,3,2,1,0:T(8,128)(2,1)} custom-call(s32[1]{0:T(128)} %bitcast.place_ref, bf16[12,8,8,768]{3,2,1,0:T(8,128)(2,1)} %k_ref.3, bf16[12,8,8,768]{3,2,1,0:T(8,128)(2,1)} %v_ref.3), custom_call_target="tpu_custom_call" | custom-call | bytes 1024 | tf_op jit(solution)/shard_map/split_far/pallas_call | solution.py:45
  2.2 1.7 %collective-permute-start.2 = (bf16[6,2,384,128]{3,2,1,0:T(8,128)(2,1)}, bf16[6,2,384,128]{3,2,1,0:T(8,128)(2,1)}, u32[]{:S(2)}, u32[]{:S(2)}) collective-permute-start(bf16[6,2,384,128]{3,2,1,0:T(8,128)(2,1)} %bitcast.7), channel_id=1, source_target_pairs={{30,0},{0,2},{2,4},{4,6},{6,8},{8,10},{10,12},{12,14},{14,16},{16,... | collective-permute-start | bytes 3538952 | tf_op jit(solution)/shard_map/ppermute | solution.py:287
  3.9 6.5 %collective-permute-start.6 = (bf16[6,2,384,128]{3,2,1,0:T(8,128)(2,1)}, bf16[6,2,384,128]{3,2,1,0:T(8,128)(2,1)S(1)}, u32[]{:S(2)}, u32[]{:S(2)}) collective-permute-start(bf16[6,2,384,128]{3,2,1,0:T(8,128)(2,1)} %bitcast.8), channel_id=1, source_target_pairs={{2,0},{4,2},{6,4},{8,6},{10,8},{12,10},{14,12},{16,14},{18,16},{20... | collective-permute-start | bytes 3538952 | tf_op jit(solution)/shard_map/ppermute | solution.py:287
  10.4 2.2 %split_near.1 = bf16[6,2,6,8,8,128]{5,4,3,2,1,0:T(8,128)(2,1)} custom-call(s32[1]{0:T(128)} %bitcast.place_ref, bf16[12,8,8,768]{3,2,1,0:T(8,128)(2,1)} %k_ref.3, bf16[12,8,8,768]{3,2,1,0:T(8,128)(2,1)} %v_ref.3), custom_call_target="tpu_custom_call" | custom-call | bytes 1024 | tf_op jit(solution)/shard_map/split_near/pallas_call | solution.py:45
  12.7 1.0 collective-permute-start.11
  13.8 0.6 fusion.5
  14.4 2.9 %collective-permute-start = (s32[1]{0:T(128)}, s32[1]{0:T(128)}, u32[]{:S(2)}, u32[]{:S(2)}) collective-permute-start(s32[1]{0:T(128)} %get-tuple-element.23), channel_id=1, source_target_pairs={{32,64},{64,32},{96,128},{128,96},{160,192},{192,160},{33,65},{65,... | collective-permute-start | bytes 20 | tf_op jit(solution)/shard_map/ppermute | solution.py:297
  17.3 2.4 %collective-permute-done = s32[1]{0:T(128)} collective-permute-done((s32[1]{0:T(128)}, s32[1]{0:T(128)}, u32[]{:S(2)}, u32[]{:S(2)}) %collective-permute-start) | collective-permute-done | bytes 36 | tf_op jit(solution)/shard_map/ppermute | solution.py:297
  19.7 1.3 collective-permute-done.1
  21.0 5.1 %collective-permute-start.8 = (bf16[6,2,384,128]{3,2,1,0:T(8,128)(2,1)}, bf16[6,2,384,128]{3,2,1,0:T(8,128)(2,1)S(1)}, u32[]{:S(2)}, u32[]{:S(2)}) collective-permute-start(bf16[6,2,384,128]{3,2,1,0:T(8,128)(2,1)} %bitcast.13), channel_id=1, source_target_pairs={{2,0},{4,2},{6,4},{8,6},{10,8},{12,10},{14,12},{16,14},{18,16},{20... | collective-permute-start | bytes 3538952 | tf_op jit(solution)/shard_map/ppermute | solution.py:287
  26.1 1.9 %pad_add_fusion.x_ref.place_ref = s32[4]{0:T(128)} fusion(s32[1]{0:T(128)} %collective-permute-done.1, s32[1]{0:T(128)} %collective-permute-done, s32[1]{0:T(128)} %bitcast.1, s32[1]{0:T(128)} %bitcast.place_ref), kind=kLoop, calls=%fused_computation.7 | loop fusion | flops 12 | bytes 32 | tf_op jit(solution)/shard_map/stack | solution.py:313
  28.0 8.3 %collective-permute-done.2.refs_0_.refs_4_ = bf16[6,2,384,128]{3,2,1,0:T(8,128)(2,1)} collective-permute-done((bf16[6,2,384,128]{3,2,1,0:T(8,128)(2,1)}, bf16[6,2,384,128]{3,2,1,0:T(8,128)(2,1)}, u32[]{:S(2)}, u32[]{:S(2)}) %collective-permute-start.2) | collective-permute-done | bytes 1179680 | tf_op jit(solution)/shard_map/ppermute | solution.py:287
  36.4 4.8 %collective-permute-start.10 = (bf16[6,2,384,128]{3,2,1,0:T(8,128)(2,1)}, bf16[6,2,384,128]{3,2,1,0:T(8,128)(2,1)}, u32[]{:S(2)}, u32[]{:S(2)}) collective-permute-start(bf16[6,2,384,128]{3,2,1,0:T(8,128)(2,1)} %bitcast.9), channel_id=1, source_target_pairs={{32,64},{64,32},{96,128},{128,96},{160,192},{192,160},{33,65},{65,... | collective-permute-start | bytes 3538952 | tf_op jit(solution)/shard_map/ppermute | solution.py:297
  41.3 5.1 %collective-permute-start.7 = (bf16[6,2,384,128]{3,2,1,0:T(8,128)(2,1)S(1)}, bf16[6,2,384,128]{3,2,1,0:T(8,128)(2,1)}, u32[]{:S(2)}, u32[]{:S(2)}) collective-permute-start(bf16[6,2,384,128]{3,2,1,0:T(8,128)(2,1)S(1)} %collective-permute-done.6.refs_1_.refs_2_.refs_6_.refs_4_), channel_id=1, source_target_pairs={{2,0},{4,2},{6,4},{8,6},{10,8},{12,10},{14,12},{16,14},{18,16},{20... | collective-permute-start | bytes 3538952 | tf_op jit(solution)/shard_map/ppermute | solution.py:287
  46.4 1.2 hand_on.2.place_ref
  47.6 3.0 %far1.1 = bf16[6,2,384,128]{3,2,1,0:T(8,128)(2,1)} custom-call(s32[4]{0:T(128)} %hand_on.2.place_ref, bf16[6,2,384,128]{3,2,1,0:T(8,128)(2,1)} %collective-permute-done.2.refs_0_.refs_4_, bf16[6,2,384,128]{3,2,1,0:T(8,128)(2,1)} %copy-done.1), custom_call_target="tpu_custom_call" | custom-call | bytes 1024 | tf_op jit(solution)/shard_map/far1/pallas_call | solution.py:95
  50.6 11.1 %collective-permute-done.4.refs_0_.refs_5_ = bf16[6,2,384,128]{3,2,1,0:T(8,128)(2,1)} collective-permute-done((bf16[6,2,384,128]{3,2,1,0:T(8,128)(2,1)}, bf16[6,2,384,128]{3,2,1,0:T(8,128)(2,1)}, u32[]{:S(2)}, u32[]{:S(2)}) %collective-permute-start.4) | collective-permute-done | bytes 1179680 | tf_op jit(solution)/shard_map/ppermute | solution.py:287
  61.6 4.8 %collective-permute-start.12 = (bf16[6,2,384,128]{3,2,1,0:T(8,128)(2,1)}, bf16[6,2,384,128]{3,2,1,0:T(8,128)(2,1)}, u32[]{:S(2)}, u32[]{:S(2)}) collective-permute-start(bf16[6,2,384,128]{3,2,1,0:T(8,128)(2,1)} %far1.1), channel_id=1, source_target_pairs={{32,64},{64,32},{96,128},{128,96},{160,192},{192,160},{33,65},{65,... | collective-permute-start | bytes 3538952 | tf_op jit(solution)/shard_map/ppermute | solution.py:297
  67.1 0.6 reshape.17.refs_9_
  67.7 1.0 copy-done.2
  68.8 2.8 %near1.1 = bf16[6,2,384,128]{3,2,1,0:T(8,128)(2,1)} custom-call(s32[4]{0:T(128)} %hand_on.2.place_ref, bf16[6,2,384,128]{3,2,1,0:T(8,128)(2,1)} %collective-permute-done.4.refs_0_.refs_5_, bf16[6,2,384,128]{3,2,1,0:T(8,128)(2,1)} %copy-done.2), custom_call_target="tpu_custom_call" | custom-call | bytes 1024 | tf_op jit(solution)/shard_map/near1/pallas_call | solution.py:95
  71.8 1.3 hand_on.3.place_ref
  73.1 13.8 %collective-permute-done.3.refs_0_ = bf16[6,2,384,128]{3,2,1,0:T(8,128)(2,1)} collective-permute-done((bf16[6,2,384,128]{3,2,1,0:T(8,128)(2,1)}, bf16[6,2,384,128]{3,2,1,0:T(8,128)(2,1)}, u32[]{:S(2)}, u32[]{:S(2)}) %collective-permute-start.3) | collective-permute-done | bytes 1179680 | tf_op jit(solution)/shard_map/ppermute | solution.py:287
  86.9 1.1 collective-permute-start.9
  88.1 2.8 %far2.1 = bf16[6,2,384,128]{3,2,1,0:T(8,128)(2,1)} custom-call(s32[4]{0:T(128)} %hand_on.3.place_ref, bf16[6,2,384,128]{3,2,1,0:T(8,128)(2,1)} %collective-permute-done.3.refs_0_, bf16[6,2,384,128]{3,2,1,0:T(8,128)(2,1)} %collective-permute-done.7.refs_1_.refs_2_, bf16[6,2,384,128]{3,2,1,0:T(8,128)(2,1)} %copy-done.1), custom_call_target="tpu_custom_call" | custom-call | bytes 1024 | tf_op jit(solution)/shard_map/far2/pallas_call | solution.py:95
  90.9 6.0 %collective-permute-start.14 = (bf16[6,2,384,128]{3,2,1,0:T(8,128)(2,1)}, bf16[6,2,384,128]{3,2,1,0:T(8,128)(2,1)S(1)}, u32[]{:S(2)}, u32[]{:S(2)}) collective-permute-start(bf16[6,2,384,128]{3,2,1,0:T(8,128)(2,1)} %far2.1), channel_id=1, source_target_pairs={{32,64},{64,32},{96,128},{128,96},{160,192},{192,160},{33,65},{65,... | collective-permute-start | bytes 3538952 | tf_op jit(solution)/shard_map/ppermute | solution.py:297
  96.9 0.7 copy.10.s_ref
  97.5 17.5 %first.1.refs_8_ = f32[6,2,384,256]{3,2,1,0:T(8,128)} custom-call(s32[2,1]{1,0:T(2,128)} %copy.10.s_ref, s32[4]{0:T(128)} %pad_add_fusion.x_ref.place_ref, bf16[12,8,8,768]{3,2,1,0:T(8,128)(2,1)} %q_ref.3, bf16[6,2,384,128]{3,2,1,0:T(8,128)(2,1)} %bitcast.10, bf16[6,2,384,128]{3,2,1,0:T(8,128)(2,1)} %bitcast.14, ...), custom_call_target="tpu_custom_call" | custom-call | bytes 1024 | tf_op jit(solution)/shard_map/first/pallas_call | solution.py:264
  115.1 2.8 %near2.1 = bf16[6,2,384,128]{3,2,1,0:T(8,128)(2,1)} custom-call(s32[4]{0:T(128)} %pad_add_fusion.x_ref.place_ref, bf16[6,2,384,128]{3,2,1,0:T(8,128)(2,1)} %collective-permute-done.5.refs_0_.refs_1_, bf16[6,2,384,128]{3,2,1,0:T(8,128)(2,1)} %collective-permute-done.9.refs_1_.refs_3_, bf16[6,2,384,128]{3,2,1,0:T(8,128)(2,1)} %copy-done.2), custom_call_target="tpu_custom_call" | custom-call | bytes 1024 | tf_op jit(solution)/shard_map/near2/pallas_call | solution.py:95
  118.3 2.8 %collective-permute-done.15.refs_7_ = bf16[6,2,384,128]{3,2,1,0:T(8,128)(2,1)S(1)} collective-permute-done((bf16[6,2,384,128]{3,2,1,0:T(8,128)(2,1)}, bf16[6,2,384,128]{3,2,1,0:T(8,128)(2,1)S(1)}, u32[]{:S(2)}, u32[]{:S(2)}) %collective-permute-start.15) | collective-permute-done | bytes 1179680 | tf_op jit(solution)/shard_map/ppermute | solution.py:302
  121.1 1.0 copy-done.5
  122.1 12.3 %last.1 = bf16[12,8,8,768]{3,2,1,0:T(8,128)(2,1)} custom-call(s32[2,1]{1,0:T(2,128)} %copy.10.s_ref, s32[4]{0:T(128)} %pad_add_fusion.x_ref.place_ref, bf16[12,8,8,768]{3,2,1,0:T(8,128)(2,1)} %q_ref.3, bf16[6,2,384,128]{3,2,1,0:T(8,128)(2,1)} %collective-permute-done.3.refs_0_, bf16[6,2,384,128]{3,2,1,0:T(8,128)(2,1)} %collective-permute-done.5.refs_0_.refs_1_, ...), custom_call_target="tpu_custom_call" | custom-call | bytes 1024 | tf_op jit(solution)/shard_map/last/pallas_call | solution.py:264
  (36 shorter events, 1.4 us)
Async XLA Ops:
  0.0 66.6 %copy-start = (f32[256,768]{1,0:T(8,128)S(1)}, f32[256,768]{1,0:T(8,128)}, u32[]{:S(2)}) copy-start(f32[256,768]{1,0:T(8,128)} %param.11) | copy-start | bytes 2359300
  2.2 11.5 %copy-start.6 = (s32[2,1]{0,1:T(1,128)S(1)}, s32[2,1]{0,1:T(1,128)}, u32[]{:S(2)}) copy-start(s32[2,1]{0,1:T(1,128)} %param.9) | copy-start | bytes 28
  2.2 34.1 %collective-permute-start.2 = (bf16[6,2,384,128]{3,2,1,0:T(8,128)(2,1)}, bf16[6,2,384,128]{3,2,1,0:T(8,128)(2,1)}, u32[]{:S(2)}, u32[]{:S(2)}) collective-permute-start(bf16[6,2,384,128]{3,2,1,0:T(8,128)(2,1)} %bitcast.7), channel_id=1, source_target_pairs={{30,0},{0,2},{2,4},{4,6},{6,8},{8,10},{10,12},{12,14},{14,16},{16,... | collective-permute-start | bytes 3538952 | tf_op jit(solution)/shard_map/ppermute | solution.py:287
  3.9 37.3 %collective-permute-start.6 = (bf16[6,2,384,128]{3,2,1,0:T(8,128)(2,1)}, bf16[6,2,384,128]{3,2,1,0:T(8,128)(2,1)S(1)}, u32[]{:S(2)}, u32[]{:S(2)}) collective-permute-start(bf16[6,2,384,128]{3,2,1,0:T(8,128)(2,1)} %bitcast.8), channel_id=1, source_target_pairs={{2,0},{4,2},{6,4},{8,6},{10,8},{12,10},{14,12},{16,14},{18,16},{20... | collective-permute-start | bytes 3538952 | tf_op jit(solution)/shard_map/ppermute | solution.py:287
  12.7 28.7 %collective-permute-start.11 = (bf16[6,2,384,128]{3,2,1,0:T(8,128)(2,1)}, bf16[6,2,384,128]{3,2,1,0:T(8,128)(2,1)}, u32[]{:S(2)}, u32[]{:S(2)}) collective-permute-start(bf16[6,2,384,128]{3,2,1,0:T(8,128)(2,1)} %bitcast.11), channel_id=1, source_target_pairs={{0,32},{32,0},{64,96},{96,64},{128,160},{160,128},{192,224},{224,1... | collective-permute-start | bytes 3538952 | tf_op jit(solution)/shard_map/ppermute | solution.py:302
  13.7 47.9 %collective-permute-start.4 = (bf16[6,2,384,128]{3,2,1,0:T(8,128)(2,1)}, bf16[6,2,384,128]{3,2,1,0:T(8,128)(2,1)}, u32[]{:S(2)}, u32[]{:S(2)}) collective-permute-start(bf16[6,2,384,128]{3,2,1,0:T(8,128)(2,1)} %bitcast.12), channel_id=1, source_target_pairs={{30,0},{0,2},{2,4},{4,6},{6,8},{8,10},{10,12},{12,14},{14,16},{16,... | collective-permute-start | bytes 3538952 | tf_op jit(solution)/shard_map/ppermute | solution.py:287
  14.4 5.3 %collective-permute-start = (s32[1]{0:T(128)}, s32[1]{0:T(128)}, u32[]{:S(2)}, u32[]{:S(2)}) collective-permute-start(s32[1]{0:T(128)} %get-tuple-element.23), channel_id=1, source_target_pairs={{32,64},{64,32},{96,128},{128,96},{160,192},{192,160},{33,65},{65,... | collective-permute-start | bytes 20 | tf_op jit(solution)/shard_map/ppermute | solution.py:297
  19.7 1.3 collective-permute-start.1
  21.0 46.7 %collective-permute-start.8 = (bf16[6,2,384,128]{3,2,1,0:T(8,128)(2,1)}, bf16[6,2,384,128]{3,2,1,0:T(8,128)(2,1)S(1)}, u32[]{:S(2)}, u32[]{:S(2)}) collective-permute-start(bf16[6,2,384,128]{3,2,1,0:T(8,128)(2,1)} %bitcast.13), channel_id=1, source_target_pairs={{2,0},{4,2},{6,4},{8,6},{10,8},{12,10},{14,12},{16,14},{18,16},{20... | collective-permute-start | bytes 3538952 | tf_op jit(solution)/shard_map/ppermute | solution.py:287
  36.4 35.3 %collective-permute-start.10 = (bf16[6,2,384,128]{3,2,1,0:T(8,128)(2,1)}, bf16[6,2,384,128]{3,2,1,0:T(8,128)(2,1)}, u32[]{:S(2)}, u32[]{:S(2)}) collective-permute-start(bf16[6,2,384,128]{3,2,1,0:T(8,128)(2,1)} %bitcast.9), channel_id=1, source_target_pairs={{32,64},{64,32},{96,128},{128,96},{160,192},{192,160},{33,65},{65,... | collective-permute-start | bytes 3538952 | tf_op jit(solution)/shard_map/ppermute | solution.py:297
  41.2 6.4 %copy-start.1 = (bf16[6,2,384,128]{3,2,1,0:T(8,128)(2,1)}, bf16[6,2,384,128]{3,2,1,0:T(8,128)(2,1)S(1)}, u32[]{:S(2)}) copy-start(bf16[6,2,384,128]{3,2,1,0:T(8,128)(2,1)S(1)} %collective-permute-done.6.refs_1_.refs_2_.refs_6_.refs_4_) | copy-start | bytes 3538948
  41.2 45.7 %collective-permute-start.3 = (bf16[6,2,384,128]{3,2,1,0:T(8,128)(2,1)}, bf16[6,2,384,128]{3,2,1,0:T(8,128)(2,1)}, u32[]{:S(2)}, u32[]{:S(2)}) collective-permute-start(bf16[6,2,384,128]{3,2,1,0:T(8,128)(2,1)} %collective-permute-done.2.refs_0_.refs_4_), channel_id=1, source_target_pairs={{30,0},{0,2},{2,4},{4,6},{6,8},{8,10},{10,12},{12,14},{14,16},{16,... | collective-permute-start | bytes 3538952 | tf_op jit(solution)/shard_map/ppermute | solution.py:287
  41.3 46.7 %collective-permute-start.7 = (bf16[6,2,384,128]{3,2,1,0:T(8,128)(2,1)S(1)}, bf16[6,2,384,128]{3,2,1,0:T(8,128)(2,1)}, u32[]{:S(2)}, u32[]{:S(2)}) collective-permute-start(bf16[6,2,384,128]{3,2,1,0:T(8,128)(2,1)S(1)} %collective-permute-done.6.refs_1_.refs_2_.refs_6_.refs_4_), channel_id=1, source_target_pairs={{2,0},{4,2},{6,4},{8,6},{10,8},{12,10},{14,12},{16,14},{18,16},{20... | collective-permute-start | bytes 3538952 | tf_op jit(solution)/shard_map/ppermute | solution.py:287
  47.6 18.9 %copy-start.7 = (s32[2]{0:T(128)S(1)}, s32[2]{0:T(128)}, u32[]{:S(2)}) copy-start(s32[2]{0:T(128)} %param.10) | copy-start | bytes 28
  61.6 29.3 %collective-permute-start.12 = (bf16[6,2,384,128]{3,2,1,0:T(8,128)(2,1)}, bf16[6,2,384,128]{3,2,1,0:T(8,128)(2,1)}, u32[]{:S(2)}, u32[]{:S(2)}) collective-permute-start(bf16[6,2,384,128]{3,2,1,0:T(8,128)(2,1)} %far1.1), channel_id=1, source_target_pairs={{32,64},{64,32},{96,128},{128,96},{160,192},{192,160},{33,65},{65,... | collective-permute-start | bytes 3538952 | tf_op jit(solution)/shard_map/ppermute | solution.py:297
  67.7 1.0 copy-start.2
  71.6 15.3 %copy-start.3 = (bf16[6,2,384,128]{3,2,1,0:T(8,128)(2,1)S(1)}, bf16[6,2,384,128]{3,2,1,0:T(8,128)(2,1)}, u32[]{:S(2)}) copy-start(bf16[6,2,384,128]{3,2,1,0:T(8,128)(2,1)} %copy-done.2) | copy-start | bytes 3538948
  71.6 25.9 %collective-permute-start.13 = (bf16[6,2,384,128]{3,2,1,0:T(8,128)(2,1)}, bf16[6,2,384,128]{3,2,1,0:T(8,128)(2,1)}, u32[]{:S(2)}, u32[]{:S(2)}) collective-permute-start(bf16[6,2,384,128]{3,2,1,0:T(8,128)(2,1)} %near1.1), channel_id=1, source_target_pairs={{0,32},{32,0},{64,96},{96,64},{128,160},{160,128},{192,224},{224,1... | collective-permute-start | bytes 3538952 | tf_op jit(solution)/shard_map/ppermute | solution.py:302
  71.7 43.4 %collective-permute-start.5 = (bf16[6,2,384,128]{3,2,1,0:T(8,128)(2,1)}, bf16[6,2,384,128]{3,2,1,0:T(8,128)(2,1)}, u32[]{:S(2)}, u32[]{:S(2)}) collective-permute-start(bf16[6,2,384,128]{3,2,1,0:T(8,128)(2,1)} %collective-permute-done.4.refs_0_.refs_5_), channel_id=1, source_target_pairs={{30,0},{0,2},{2,4},{4,6},{6,8},{8,10},{10,12},{12,14},{14,16},{16,... | collective-permute-start | bytes 3538952 | tf_op jit(solution)/shard_map/ppermute | solution.py:287
  86.9 28.2 %collective-permute-start.9 = (bf16[6,2,384,128]{3,2,1,0:T(8,128)(2,1)S(1)}, bf16[6,2,384,128]{3,2,1,0:T(8,128)(2,1)}, u32[]{:S(2)}, u32[]{:S(2)}) collective-permute-start(bf16[6,2,384,128]{3,2,1,0:T(8,128)(2,1)S(1)} %copy-done.3), channel_id=1, source_target_pairs={{2,0},{4,2},{6,4},{8,6},{10,8},{12,10},{14,12},{16,14},{18,16},{20... | collective-permute-start | bytes 3538952 | tf_op jit(solution)/shard_map/ppermute | solution.py:287
  90.9 27.0 %collective-permute-start.14 = (bf16[6,2,384,128]{3,2,1,0:T(8,128)(2,1)}, bf16[6,2,384,128]{3,2,1,0:T(8,128)(2,1)S(1)}, u32[]{:S(2)}, u32[]{:S(2)}) collective-permute-start(bf16[6,2,384,128]{3,2,1,0:T(8,128)(2,1)} %far2.1), channel_id=1, source_target_pairs={{32,64},{64,32},{96,128},{128,96},{160,192},{192,160},{33,65},{65,... | collective-permute-start | bytes 3538952 | tf_op jit(solution)/shard_map/ppermute | solution.py:297
  117.9 3.2 %copy-start.4 = (bf16[6,2,384,128]{3,2,1,0:T(8,128)(2,1)}, bf16[6,2,384,128]{3,2,1,0:T(8,128)(2,1)S(1)}, u32[]{:S(2)}) copy-start(bf16[6,2,384,128]{3,2,1,0:T(8,128)(2,1)S(1)} %collective-permute-done.14.refs_6_) | copy-start | bytes 3538948
  117.9 3.1 %collective-permute-start.15 = (bf16[6,2,384,128]{3,2,1,0:T(8,128)(2,1)}, bf16[6,2,384,128]{3,2,1,0:T(8,128)(2,1)S(1)}, u32[]{:S(2)}, u32[]{:S(2)}) collective-permute-start(bf16[6,2,384,128]{3,2,1,0:T(8,128)(2,1)} %near2.1), channel_id=1, source_target_pairs={{0,32},{32,0},{64,96},{96,64},{128,160},{160,128},{192,224},{224,1... | collective-permute-start | bytes 3538952 | tf_op jit(solution)/shard_map/ppermute | solution.py:302
  121.1 1.0 copy-start.5
